TPU v7x, 32 devices: a whole 2x2x4 slice. The times are simulated.
32 devices in a mesh: seq: 8 (over y, x, core), rows: 4 (over z).
Axes of the slice: x: 2, y: 2, z: 4, core: 2. Of those that a mesh axis runs over, the one named last changes fastest.
Arguments:
- tokens: bfloat16 [8, 2048, 2048], P('rows', 'seq'), may hold values from -6 to 6
- lengths: int32 [8], P('rows'), may hold values from 64 to 2048, as said below
- norm_gains: bfloat16 [2, 2048], P(None, ('seq', 'rows')), may hold values from 0.099609375 to 1.8984375
- qk_gains: bfloat16 [2, 64], replicated, may hold values from 0.099609375 to 1.8984375
- qkv_weight: bfloat16 [2048, 3072], P(('seq', 'rows')), may hold values from -0.125 to 0.125
- out_weight: bfloat16 [2048, 2048], P(('seq', 'rows')), may hold values from -0.5 to 0.5
- gate_up_weight: bfloat16 [2048, 16384], P(('seq', 'rows')), may hold values from -0.125 to 0.125
- down_weight: bfloat16 [2048, 8192], P(('seq', 'rows')), may hold values from -0.09375 to 0.09375
- cotangent: bfloat16 [8, 2048, 2048], P('rows', 'seq'), may hold values from -6 to 6
Outputs:
- output: bfloat16 [8, 2048, 2048], P('rows', 'seq')
- input_grad: bfloat16 [8, 2048, 2048], P('rows', 'seq')
- norm_gains_grad: float32 [2, 2048], P(None, ('seq', 'rows'))
- qk_gains_grad: float32 [2, 64], replicated
- qkv_grad: float32 [2048, 3072], P(('seq', 'rows'))
- out_grad: float32 [2048, 2048], P(('seq', 'rows'))
- gate_up_grad: float32 [2048, 16384], P(('seq', 'rows'))
- down_grad: float32 [2048, 8192], P(('seq', 'rows'))
Inputs may be any that keep to these rules, and one draw needn't show every extreme that they name: `lengths`: in each aligned block of 2 rows (the rows of one device) one row has length 2048; some row has length 64.
All inputs are finite; a program needn't handle non-finite values.
Results may differ from a plain program's by a relative error of at most 0.025.
Values may be sent and summed in bfloat16 or wider, within the bound.
A program may use at most 768 MiB of HBM per device.

v0:
```python
from functools import partial
import math

import jax
import jax.numpy as jnp
from jax import lax
from jax.sharding import PartitionSpec as P

QUERY_HEADS = 32
KEY_VALUE_HEADS = 8
HEAD_SIZE = 64


EPSILON = 1e-06
NEG_LARGE = -1e30


def passed_along(block, axis, distance):
    devices = range(lax.axis_size(axis))
    route = [(i - distance, i) for i in devices if i - distance in devices]
    return lax.ppermute(block, axis, route)


def from_behind(array, axis, by):
    count = lax.axis_size(axis)
    return lax.ppermute(array, axis, [(i, (i + by) % count) for i in range(count)])


def rms_norm(values, gain_vector):
    factor = lax.rsqrt(jnp.mean(values * values, axis=-1, keepdims=True) + EPSILON)
    return values * factor * gain_vector


def rotary(values, positions):
    half_width = values.shape[-1] // 2
    exponent = jnp.arange(half_width).astype(jnp.float32) * (2.0 / values.shape[-1])
    frequency = jnp.exp(-math.log(10000.0) * exponent)
    angles = positions.astype(jnp.float32)[:, None] * frequency[None, :]
    cosine = jnp.cos(angles)[:, None, :]
    sine_part = jnp.sin(angles)[:, None, :]
    first_half = values[..., :half_width]
    second_half = values[..., half_width:]
    return jnp.concatenate(
        [
            first_half * cosine - second_half * sine_part,
            second_half * cosine + first_half * sine_part,
        ],
        axis=-1,
    )


def swiglu(gate_up):
    half_width = gate_up.shape[-1] // 2
    return jax.nn.silu(gate_up[..., :half_width]) * gate_up[..., half_width:]


def prepare(positions, query_key_value_unnormed, qk_gain):
    count_of_rows, slots_per_shard = (
        query_key_value_unnormed.shape[0],
        query_key_value_unnormed.shape[1],
    )
    query_rows_all = query_key_value_unnormed[..., : QUERY_HEADS * HEAD_SIZE].reshape(
        count_of_rows, slots_per_shard, QUERY_HEADS, HEAD_SIZE
    )
    key_row_block = query_key_value_unnormed[
        ..., QUERY_HEADS * HEAD_SIZE : (QUERY_HEADS + KEY_VALUE_HEADS) * HEAD_SIZE
    ].reshape(count_of_rows, slots_per_shard, KEY_VALUE_HEADS, HEAD_SIZE)
    value_row_block = query_key_value_unnormed[
        ..., (QUERY_HEADS + KEY_VALUE_HEADS) * HEAD_SIZE :
    ].reshape(count_of_rows, slots_per_shard, KEY_VALUE_HEADS, HEAD_SIZE)
    query_rows_all = rotary(rms_norm(query_rows_all, qk_gain[0]), positions)
    key_row_block = rotary(rms_norm(key_row_block, qk_gain[1]), positions)
    return (query_rows_all, key_row_block, value_row_block)


def matmul(left_side, right_side):
    return jnp.dot(left_side, right_side, preferred_element_type=jnp.float32)


def matmul_nt(left_side, right_side):
    return lax.dot_general(
        left_side, right_side, (((1,), (1,)), ((), ())), preferred_element_type=jnp.float32
    )


def matmul_tn(left_side, right_side):
    return lax.dot_general(
        left_side, right_side, (((0,), (0,)), ((), ())), preferred_element_type=jnp.float32
    )


def shards(
    tokens,
    lengths,
    norm_gains,
    qk_gains,
    qkv_weight,
    out_weight,
    gate_up_weight,
    down_weight,
    cotangent,
):
    count_of_rows, slots_per_shard, model_width = tokens.shape
    tok_count = count_of_rows * slots_per_shard
    seq_size = lax.axis_size("seq")
    seq_index = lax.axis_index("seq")
    positions = seq_index * slots_per_shard + jnp.arange(slots_per_shard, dtype=jnp.int32)
    query_group_width = QUERY_HEADS // KEY_VALUE_HEADS
    score_scale = HEAD_SIZE ** (-0.5)
    inputs = tokens.reshape(tok_count, model_width).astype(jnp.float32)
    qkv_full, out_full, gains_full = (
        lax.all_gather(qkv_weight, ("seq", "rows"), axis=0, tiled=True),
        lax.all_gather(out_weight, ("seq", "rows"), axis=0, tiled=True),
        lax.all_gather(norm_gains, ("seq", "rows"), axis=1, tiled=True),
    )
    gain_values = gains_full.astype(jnp.float32)
    normed, norm_back = jax.vjp(rms_norm, inputs, gain_values[0])
    normed_low = normed.astype(jnp.bfloat16)
    query_key_value_unnormed = matmul(normed_low, qkv_full).reshape(
        count_of_rows, slots_per_shard, -1
    )
    (query_rows_all, key_row_block, value_row_block), prep_back = jax.vjp(
        partial(prepare, positions), query_key_value_unnormed, qk_gains.astype(jnp.float32)
    )
    query_narrow = query_rows_all.astype(jnp.bfloat16).reshape(
        count_of_rows, slots_per_shard, KEY_VALUE_HEADS, query_group_width, HEAD_SIZE
    )
    kv_local = jnp.stack(
        [
            key_row_block.astype(jnp.bfloat16).reshape(
                count_of_rows, slots_per_shard, KEY_VALUE_HEADS * HEAD_SIZE
            ),
            value_row_block.astype(jnp.bfloat16).reshape(
                count_of_rows, slots_per_shard, KEY_VALUE_HEADS * HEAD_SIZE
            ),
        ],
        axis=2,
    )
    last_place = seq_index * slots_per_shard + slots_per_shard - 1
    longest = jnp.max(lengths)

    def allowed_mask(key_start, count_of_keys):
        key_places = key_start + jnp.arange(count_of_keys, dtype=jnp.int32)
        allowed = (key_places[None, None, :] <= positions[None, :, None]) & (
            key_places[None, None, :] < lengths[:, None, None]
        )
        return allowed[:, None, None, :, :]

    def needed(key_start):
        return (key_start <= last_place) & (key_start < longest)

    def split_block(key_value_block):
        count_of_keys = key_value_block.shape[1]
        return (
            key_value_block[:, :, 0].reshape(
                count_of_rows, count_of_keys, KEY_VALUE_HEADS, HEAD_SIZE
            ),
            key_value_block[:, :, 1].reshape(
                count_of_rows, count_of_keys, KEY_VALUE_HEADS, HEAD_SIZE
            ),
        )

    def forward_block(carry_state, key_value_block, key_start):

        def forward_compute(inner_state):
            running_max, denominator, numerator = inner_state
            key_part, value_part = split_block(key_value_block)
            scores = (
                jnp.einsum(
                    "rqhgd,rkhd->rhgqk", query_narrow, key_part, preferred_element_type=jnp.float32
                )
                * score_scale
            )
            scores = jnp.where(allowed_mask(key_start, key_value_block.shape[1]), scores, NEG_LARGE)
            new_max = jnp.maximum(running_max, jnp.max(scores, axis=-1))
            weights = jnp.exp(scores - new_max[..., None])
            factor = jnp.exp(running_max - new_max)
            denominator = denominator * factor + jnp.sum(weights, axis=-1)
            numerator = numerator * factor[..., None] + jnp.einsum(
                "rhgqk,rkhd->rhgqd",
                weights.astype(jnp.bfloat16),
                value_part,
                preferred_element_type=jnp.float32,
            )
            return (new_max, denominator, numerator)

        return lax.cond(
            needed(key_start), forward_compute, lambda kept_state: kept_state, carry_state
        )

    statistic_shape = (count_of_rows, KEY_VALUE_HEADS, query_group_width, slots_per_shard)
    carry_state = (
        jnp.full(statistic_shape, NEG_LARGE, jnp.float32),
        jnp.zeros(statistic_shape, jnp.float32),
        jnp.zeros(statistic_shape + (HEAD_SIZE,), jnp.float32),
    )
    carry_state = forward_block(carry_state, kv_local, seq_index * slots_per_shard)

    def cycle_step(cycle_turn, carry):
        key_value_block, inner_state = carry
        key_value_block = passed_along(key_value_block, "seq", 1)
        source = (seq_index - cycle_turn) % seq_size
        return (
            key_value_block,
            forward_block(inner_state, key_value_block, source * slots_per_shard),
        )

    carry_state = lax.fori_loop(1, seq_size, cycle_step, (kv_local, carry_state))[1]
    running_max, denominator, numerator = carry_state
    log_total = running_max + jnp.log(denominator)
    attended_rows = jnp.transpose(numerator / denominator[..., None], (0, 3, 1, 2, 4))
    attended_low = attended_rows.reshape(tok_count, QUERY_HEADS * HEAD_SIZE).astype(jnp.bfloat16)
    middle = inputs + matmul_nt(attended_low, out_full)
    gate_up_full, down_full = (
        lax.all_gather(gate_up_weight, ("seq", "rows"), axis=0, tiled=True),
        lax.all_gather(down_weight, ("seq", "rows"), axis=0, tiled=True),
    )
    hidden, hidden_back = jax.vjp(rms_norm, middle, gain_values[1])
    hidden_low = hidden.astype(jnp.bfloat16)
    gate_up = matmul(hidden_low, gate_up_full)
    activated, act_back = jax.vjp(swiglu, gate_up)
    act_low = activated.astype(jnp.bfloat16)
    result = middle + matmul_nt(act_low, down_full)
    output = result.astype(jnp.bfloat16).reshape(count_of_rows, slots_per_shard, model_width)
    grad_low = cotangent.reshape(tok_count, model_width)
    grad_out = grad_low.astype(jnp.float32)
    fresh_gate_up, fresh_down, grad_low = lax.optimization_barrier(
        (gate_up_weight, down_weight, grad_low)
    )
    gate_up_full, down_full = (
        lax.all_gather(fresh_gate_up, ("seq", "rows"), axis=0, tiled=True),
        lax.all_gather(fresh_down, ("seq", "rows"), axis=0, tiled=True),
    )
    d_activated = matmul(grad_low, down_full)
    (d_gate_up,) = act_back(d_activated)
    d_gu_low = d_gate_up.astype(jnp.bfloat16)
    d_hidden = matmul_nt(d_gu_low, gate_up_full)
    d_middle_norm, d_gain_ffn = hidden_back(d_hidden)
    d_middle = grad_out + d_middle_norm
    d_branch_low = d_middle.astype(jnp.bfloat16)
    fresh_qkv, fresh_out, d_branch_low = lax.optimization_barrier(
        (qkv_weight, out_weight, d_branch_low)
    )
    qkv_full, out_full = (
        lax.all_gather(fresh_qkv, ("seq", "rows"), axis=0, tiled=True),
        lax.all_gather(fresh_out, ("seq", "rows"), axis=0, tiled=True),
    )
    attended_gradient = matmul(d_branch_low, out_full)
    attended_grad_narrow = attended_gradient.astype(jnp.bfloat16).reshape(
        count_of_rows, slots_per_shard, KEY_VALUE_HEADS, query_group_width, HEAD_SIZE
    )
    row_delta = jnp.transpose(
        jnp.sum(attended_grad_narrow.astype(jnp.float32) * attended_rows, axis=-1), (0, 2, 3, 1)
    )

    def backward_block(query_gradient, key_value_block, key_start):
        count_of_keys = key_value_block.shape[1]

        def backward_compute(query_inner_rows):
            key_part, value_part = split_block(key_value_block)
            scores = (
                jnp.einsum(
                    "rqhgd,rkhd->rhgqk", query_narrow, key_part, preferred_element_type=jnp.float32
                )
                * score_scale
            )
            weights = jnp.where(
                allowed_mask(key_start, count_of_keys), jnp.exp(scores - log_total[..., None]), 0.0
            )
            value_gradient = jnp.einsum(
                "rhgqk,rqhgd->rkhd",
                weights.astype(jnp.bfloat16),
                attended_grad_narrow,
                preferred_element_type=jnp.float32,
            )
            d_weights = jnp.einsum(
                "rqhgd,rkhd->rhgqk",
                attended_grad_narrow,
                value_part,
                preferred_element_type=jnp.float32,
            )
            d_scores = (weights * (d_weights - row_delta[..., None])).astype(jnp.bfloat16)
            query_inner_rows = (
                query_inner_rows
                + jnp.einsum(
                    "rhgqk,rkhd->rqhgd", d_scores, key_part, preferred_element_type=jnp.float32
                )
                * score_scale
            )
            key_gradient = (
                jnp.einsum(
                    "rhgqk,rqhgd->rkhd", d_scores, query_narrow, preferred_element_type=jnp.float32
                )
                * score_scale
            )
            pieces = jnp.stack(
                [
                    key_gradient.reshape(count_of_rows, count_of_keys, KEY_VALUE_HEADS * HEAD_SIZE),
                    value_gradient.reshape(
                        count_of_rows, count_of_keys, KEY_VALUE_HEADS * HEAD_SIZE
                    ),
                ],
                axis=2,
            )
            return (query_inner_rows, pieces)

        def skipped(query_inner_rows):
            return (
                query_inner_rows,
                jnp.zeros(
                    (count_of_rows, count_of_keys, 2, KEY_VALUE_HEADS * HEAD_SIZE), jnp.float32
                ),
            )

        return lax.cond(needed(key_start), backward_compute, skipped, query_gradient)

    query_gradient = jnp.zeros(
        (count_of_rows, slots_per_shard, KEY_VALUE_HEADS, query_group_width, HEAD_SIZE), jnp.float32
    )

    def pass_grads(travelling):
        return from_behind(travelling.astype(jnp.bfloat16), "seq", 1).astype(travelling.dtype)

    query_gradient, key_value_gradients = backward_block(
        query_gradient, kv_local, seq_index * slots_per_shard
    )

    def back_step(cycle_turn, carry):
        key_value_block, query_inner_rows, running_grads = carry
        key_value_block = passed_along(key_value_block, "seq", 1)
        running_grads = pass_grads(running_grads)
        source = (seq_index - cycle_turn) % seq_size
        query_inner_rows, fresh_grads = backward_block(
            query_inner_rows, key_value_block, source * slots_per_shard
        )
        return (key_value_block, query_inner_rows, running_grads + fresh_grads)

    looped = lax.fori_loop(1, seq_size, back_step, (kv_local, query_gradient, key_value_gradients))
    query_gradient = looped[1]
    key_value_gradients = pass_grads(looped[2])
    key_gradient = key_value_gradients[:, :, 0].reshape(
        count_of_rows, slots_per_shard, KEY_VALUE_HEADS, HEAD_SIZE
    )
    value_gradient = key_value_gradients[:, :, 1].reshape(
        count_of_rows, slots_per_shard, KEY_VALUE_HEADS, HEAD_SIZE
    )
    d_queries = query_gradient.reshape(count_of_rows, slots_per_shard, QUERY_HEADS, HEAD_SIZE)
    d_qkv_raw, d_qk_gain = prep_back((d_queries, key_gradient, value_gradient))
    d_qkv_low = d_qkv_raw.reshape(tok_count, -1).astype(jnp.bfloat16)
    d_normed = matmul_nt(d_qkv_low, qkv_full)
    d_input_norm, d_gain_attn = norm_back(d_normed)
    input_grad = (
        (d_middle + d_input_norm)
        .astype(jnp.bfloat16)
        .reshape(count_of_rows, slots_per_shard, model_width)
    )
    qkv_cols = qkv_weight.shape[1]
    attn_sums = lax.psum_scatter(
        jnp.concatenate(
            [matmul_tn(normed_low, d_qkv_low), matmul_tn(d_branch_low, attended_low)], axis=1
        ),
        ("seq", "rows"),
        scatter_dimension=0,
        tiled=True,
    )
    ffn_sums = lax.psum_scatter(
        jnp.concatenate([matmul_tn(hidden_low, d_gu_low), matmul_tn(grad_low, act_low)], axis=1),
        ("seq", "rows"),
        scatter_dimension=0,
        tiled=True,
    )
    gain_grads, qk_grad = lax.psum(
        (jnp.stack([d_gain_attn, d_gain_ffn]), d_qk_gain), ("seq", "rows")
    )
    shard_width = norm_gains.shape[1]
    flat_index = lax.axis_index(("seq", "rows"))
    norm_gain_grad = lax.dynamic_slice_in_dim(gain_grads, flat_index * shard_width, shard_width, 1)
    up_cols = gate_up_weight.shape[1]
    return (
        output,
        input_grad,
        norm_gain_grad,
        qk_grad,
        attn_sums[:, :qkv_cols],
        attn_sums[:, qkv_cols:],
        ffn_sums[:, :up_cols],
        ffn_sums[:, up_cols:],
    )


def solution(mesh):
    in_specs = (
        P("rows", "seq", None),
        P("rows"),
        P(None, ("seq", "rows")),
        P(),
        P(("seq", "rows"), None),
        P(("seq", "rows"), None),
        P(("seq", "rows"), None),
        P(("seq", "rows"), None),
        P("rows", "seq", None),
    )
    out_specs = (
        P("rows", "seq", None),
        P("rows", "seq", None),
        P(None, ("seq", "rows")),
        P(),
        P(("seq", "rows"), None),
        P(("seq", "rows"), None),
        P(("seq", "rows"), None),
        P(("seq", "rows"), None),
    )
    return jax.shard_map(shards, mesh=mesh, in_specs=in_specs, out_specs=out_specs, check_vma=False)
```

profile of v0, /device:TPU:0, one launch (start us, length us, event | category | flops | bytes accessed | tf_op | source)
XLA Modules:
  0.0 4369.9 jit_solution(13248249377796847390)
XLA Ops:
  11.9 69.9 %all-gather = bf16[32,64,2]{1,2,0:T(2,128)(2,1)S(1)} all-gather(bf16[1,64,2]{1,2,0:T(2,128)(2,1)S(1)} %bitcast.309), channel_id=1, replica_groups=mesh['seq'=8,'rows'=4] {'seq','rows'}, dimensions={0}, use_global_device_ids=true | all-gather | bytes 8448 | tf_op jit(solution)/shard_map/all_gather | solution.py:114
  174.1 267.0 %while.45 = (s32[]{:T(128)}, bf16[2,256,2,512]{1,3,0,2:T(8,128)(2,1)}, f32[2,8,4,256]{3,2,1,0:T(4,128)}, f32[2,8,4,256]{3,2,1,0:T(4,128)S(1)}, f32[2,8,4,256,64]...) while((s32[]{:T(128)}, ...), condition=%wide.region_13.14_spmd.clone, body=%wide.region_8.13_spmd.clone.sunk | while | flops 1122206720 | bytes 71967208 | solution.py:208
  180.1 48.1 %collective-permute-start = (bf16[2,256,2,512]{1,3,0,2:T(8,128)(2,1)}, bf16[2,256,2,512]{1,3,0,2:T(8,128)(2,1)S(1)}, u32[]{:S(2)}, u32[]{:S(2)}) collective-permute-start(bf16[2,256,2,512]{1,3,0,2:T(8,128)(2,1)} %get-tuple-element.1235), channel_id=1, source_target_pairs={{0,4},{4,8},{8,12},{12,16},{16,20},{20,24},{24,28},{1,5},{5,9},{9,... | collective-permute-start | bytes 3145736 | tf_op jit(solution)/shard_map/while/body/eval_jaxpr/ppermute | solution.py:21
  248.7 72.4 %collective-permute-start = (bf16[2,256,2,512]{1,3,0,2:T(8,128)(2,1)}, bf16[2,256,2,512]{1,3,0,2:T(8,128)(2,1)S(1)}, u32[]{:S(2)}, u32[]{:S(2)}) collective-permute-start(bf16[2,256,2,512]{1,3,0,2:T(8,128)(2,1)} %get-tuple-element.1235), channel_id=1, source_target_pairs={{0,4},{4,8},{8,12},{12,16},{16,20},{20,24},{24,28},{1,5},{5,9},{9,... | collective-permute-start | bytes 3145736 | tf_op jit(solution)/shard_map/while/body/eval_jaxpr/ppermute | solution.py:21
  343.6 54.4 %collective-permute-start = (bf16[2,256,2,512]{1,3,0,2:T(8,128)(2,1)}, bf16[2,256,2,512]{1,3,0,2:T(8,128)(2,1)S(1)}, u32[]{:S(2)}, u32[]{:S(2)}) collective-permute-start(bf16[2,256,2,512]{1,3,0,2:T(8,128)(2,1)} %get-tuple-element.1235), channel_id=1, source_target_pairs={{0,4},{4,8},{8,12},{12,16},{16,20},{20,24},{24,28},{1,5},{5,9},{9,... | collective-permute-start | bytes 3145736 | tf_op jit(solution)/shard_map/while/body/eval_jaxpr/ppermute | solution.py:21
  401.3 36.3 collective-permute-start
  463.8 127.2 %all-gather.14.cloned.1.call-done = bf16[2048,16384]{1,0:T(8,128)(2,1)} async-done(((bf16[64,16384]{1,0:T(8,128)(2,1)}), bf16[2048,16384]{1,0:T(8,128)(2,1)}) %all-gather.14.cloned.1.call-update) | async-done | bytes 67108880 | tf_op jit(solution)/shard_map/all_gather | solution.py:215
  590.9 46.3 %fusion.84 = f32[512,16384]{1,0:T(8,128)} fusion(bf16[2048,16384]{1,0:T(8,128)(2,1)} %all-gather.14.cloned.1.call-done, f32[512,2048]{1,0:T(8,128)} %get-tuple-element.1039, f32[2048]{0:T(1024)S(1)} %bitcast.282, f32[512]{0:T(512)S(1)} %fusion.78), kind=kOutput, calls=%fused_computation.180 | convolution fusion | flops 34362884096 | bytes 104867840 | tf_op jit(solution)/shard_map/dot_general | solution.py:77
  637.2 149.1 %all-gather.18.cloned.1.call-done = bf16[2048,8192]{1,0:T(8,128)(2,1)} async-done(((bf16[64,8192]{1,0:T(8,128)(2,1)}), bf16[2048,8192]{1,0:T(8,128)(2,1)}) %all-gather.18.cloned.1.call-update) | async-done | bytes 33554448 | tf_op jit(solution)/shard_map/all_gather | solution.py:232
  786.4 40.4 fusion.73
  826.7 316.9 %all-gather.20.cloned.1.call-done = bf16[2048,16384]{1,0:T(8,128)(2,1)} async-done(((bf16[64,16384]{1,0:T(8,128)(2,1)}), bf16[2048,16384]{1,0:T(8,128)(2,1)}) %all-gather.20.cloned.1.call-update) | async-done | bytes 67108880 | tf_op jit(solution)/shard_map/all_gather | solution.py:231
  1143.7 47.0 %multiply_reduce_fusion.1 = (f32[2048]{0:T(1024)}, f32[512]{0:T(512)S(1)}, f32[512,2048]{1,0:T(8,128)}) fusion(f32[512,2048]{1,0:T(8,128)} %get-tuple-element.1039, f32[512]{0:T(512)S(1)} %fusion.78, f32[2048]{0:T(1024)S(1)} %bitcast.283, bf16[2048,16384]{1,0:T(8,128)(2,1)} %all-gather.20.cloned.1.call-done, f32[512,8192]{1,0:T(8,128)} %get-tuple-element.1020, ...), kind=kOutput, calls=%fused_computation.121 | convolution fusion | flops 34382807040 | bytes 109072384 | tf_op jit(solution)/shard_map/dot_general | solution.py:81
  1212.7 60.4 %all-gather.22.cloned.1.call-done = bf16[2048,2048]{1,0:T(8,128)(2,1)} async-done(((bf16[64,2048]{1,0:T(8,128)(2,1)}), bf16[2048,2048]{1,0:T(8,128)(2,1)}) %all-gather.22.cloned.1.call-update) | async-done | bytes 8388624 | tf_op jit(solution)/shard_map/all_gather | solution.py:246
  1297.0 36.0 conditional.5
  1334.0 421.4 %while.46 = (s32[]{:T(128)}, bf16[2,256,2,512]{1,3,0,2:T(8,128)(2,1)}, f32[2,256,8,4,64]{1,4,3,2,0:T(8,128)}, bf16[2,256,2,512]{1,3,0,2:T(8,128)(2,1)}, s32[]{:T...) while((s32[]{:T(128)}, ...), condition=%wide.region_22.23_spmd.clone, body=%wide.region_19.22_spmd.clone.sunk | while | flops 2730951680 | bytes 121840152 | solution.py:338
  1362.6 43.4 collective-permute-start.1
  1645.1 46.0 %collective-permute-done.2 = bf16[2,256,2,512]{1,3,0,2:T(8,128)(2,1)} collective-permute-done((bf16[2,256,2,512]{1,3,0,2:T(8,128)(2,1)}, bf16[2,256,2,512]{1,3,0,2:T(8,128)(2,1)}, u32[]{:S(2)}, u32[]{:S(2)}) %collective-permute-start.2) | collective-permute-done | bytes 1048608 | tf_op jit(solution)/shard_map/while/body/eval_jaxpr/ppermute | solution.py:26
  1701.8 50.5 %collective-permute-done.2 = bf16[2,256,2,512]{1,3,0,2:T(8,128)(2,1)} collective-permute-done((bf16[2,256,2,512]{1,3,0,2:T(8,128)(2,1)}, bf16[2,256,2,512]{1,3,0,2:T(8,128)(2,1)}, u32[]{:S(2)}, u32[]{:S(2)}) %collective-permute-start.2) | collective-permute-done | bytes 1048608 | tf_op jit(solution)/shard_map/while/body/eval_jaxpr/ppermute | solution.py:26
  1771.9 41.7 collective-permute-done.3
  1893.4 61.6 %fusion.71 = f32[2048,16384]{1,0:T(8,128)} fusion(f32[512,8192]{1,0:T(8,128)} %get-tuple-element.1020, f32[512,8192]{1,0:T(8,128)} %get-tuple-element.1019, f32[512,2048]{1,0:T(8,128)} %get-tuple-element.1039, f32[2048]{0:T(1024)S(1)} %bitcast.285, f32[512]{0:T(512)S(1)} %copy-done.28), kind=kOutput, calls=%fused_computation.131 | convolution fusion | flops 34379661312 | bytes 171976704 | tf_op jit(solution)/shard_map/dot_general | solution.py:87
  1955.1 131.5 %pad_maximum_fusion.2 = f32[2048,24576]{1,0:T(8,128)} fusion(f32[2048,8192]{1,0:T(8,128)} %fusion.91, f32[2048,16384]{1,0:T(8,128)} %fusion.71), kind=kLoop, calls=%fused_computation.85 | loop fusion | flops 50331648 | bytes 402653184 | tf_op jit(solution)/shard_map/concatenate | solution.py:367
  2125.9 47.0 %all-reduce.11 = (f32[2,2048]{1,0:T(2,128)S(1)}, f32[2,64]{1,0:T(2,128)}) all-reduce(f32[2,2048]{1,0:T(2,128)S(1)} %pad_maximum_fusion.6, f32[2,64]{1,0:T(2,128)S(1)} %pad_add_fusion.2), channel_id=1, replica_groups=mesh['seq'=8,'rows'=4] {'seq','rows'}, use_global_device_ids=true, to_apply=%region_28.29 | all-reduce | flops 4224 | bytes 33792 | tf_op jit(solution)/shard_map/psum | solution.py:372
  2181.5 568.9 %reduce-scatter.3.cloned.1.call-done = f32[64,5120]{1,0:T(8,128)} async-done(((f32[2048,5120]{1,0:T(8,128)}), f32[64,5120]{1,0:T(8,128)}) %reduce-scatter.3.cloned.1.call-update) | async-done | bytes 1310736 | tf_op jit(solution)/shard_map/reduce_scatter | solution.py:358
  2754.3 1600.8 %reduce-scatter.5.cloned.1.call-done = f32[64,24576]{1,0:T(8,128)} async-done(((f32[2048,24576]{1,0:T(8,128)}), f32[64,24576]{1,0:T(8,128)}) %reduce-scatter.5.cloned.1.call-update) | async-done | bytes 6291472 | tf_op jit(solution)/shard_map/reduce_scatter | solution.py:366
  (353 shorter events, 726.8 us)
Async XLA Ops:
  7.2 102.6 %all-gather.10.cloned.1.call-start = ((), (), s32[]{:S(2)}) async-start(), calls=%async_computation.2 | async-start | bytes 12976128 | tf_op jit(solution)/shard_map/all_gather | solution.py:112
  7.9 445.1 %all-gather.12.cloned.1.call-start = ((), (), s32[]{:S(2)}) async-start(), calls=%async_computation.3 | async-start | bytes 8650752 | tf_op jit(solution)/shard_map/all_gather | solution.py:113
  8.7 582.2 %all-gather.14.cloned.1.call-start = ((), (), s32[]{:S(2)}) async-start(), calls=%async_computation.4 | async-start | bytes 69206016 | tf_op jit(solution)/shard_map/all_gather | solution.py:215
  9.4 776.9 %all-gather.18.cloned.1.call-start = ((), (), s32[]{:S(2)}) async-start(), calls=%async_computation.6 | async-start | bytes 34603008 | tf_op jit(solution)/shard_map/all_gather | solution.py:232
  10.0 1133.7 %all-gather.20.cloned.1.call-start = ((), (), s32[]{:S(2)}) async-start(), calls=%async_computation.7 | async-start | bytes 69206016 | tf_op jit(solution)/shard_map/all_gather | solution.py:231
  10.6 1262.5 %all-gather.22.cloned.1.call-start = ((), (), s32[]{:S(2)}) async-start(), calls=%async_computation.8 | async-start | bytes 8650752 | tf_op jit(solution)/shard_map/all_gather | solution.py:246
  180.1 50.6 %collective-permute-start = (bf16[2,256,2,512]{1,3,0,2:T(8,128)(2,1)}, bf16[2,256,2,512]{1,3,0,2:T(8,128)(2,1)S(1)}, u32[]{:S(2)}, u32[]{:S(2)}) collective-permute-start(bf16[2,256,2,512]{1,3,0,2:T(8,128)(2,1)} %get-tuple-element.1235), channel_id=1, source_target_pairs={{0,4},{4,8},{8,12},{12,16},{16,20},{20,24},{24,28},{1,5},{5,9},{9,... | collective-permute-start | bytes 3145736 | tf_op jit(solution)/shard_map/while/body/eval_jaxpr/ppermute | solution.py:21
  248.7 74.8 %collective-permute-start = (bf16[2,256,2,512]{1,3,0,2:T(8,128)(2,1)}, bf16[2,256,2,512]{1,3,0,2:T(8,128)(2,1)S(1)}, u32[]{:S(2)}, u32[]{:S(2)}) collective-permute-start(bf16[2,256,2,512]{1,3,0,2:T(8,128)(2,1)} %get-tuple-element.1235), channel_id=1, source_target_pairs={{0,4},{4,8},{8,12},{12,16},{16,20},{20,24},{24,28},{1,5},{5,9},{9,... | collective-permute-start | bytes 3145736 | tf_op jit(solution)/shard_map/while/body/eval_jaxpr/ppermute | solution.py:21
  343.6 56.8 %collective-permute-start = (bf16[2,256,2,512]{1,3,0,2:T(8,128)(2,1)}, bf16[2,256,2,512]{1,3,0,2:T(8,128)(2,1)S(1)}, u32[]{:S(2)}, u32[]{:S(2)}) collective-permute-start(bf16[2,256,2,512]{1,3,0,2:T(8,128)(2,1)} %get-tuple-element.1235), channel_id=1, source_target_pairs={{0,4},{4,8},{8,12},{12,16},{16,20},{20,24},{24,28},{1,5},{5,9},{9,... | collective-permute-start | bytes 3145736 | tf_op jit(solution)/shard_map/while/body/eval_jaxpr/ppermute | solution.py:21
  401.3 38.8 collective-permute-start
  1197.3 889.9 %all-gather.16.cloned.1.call-start = ((), (), s32[]{:S(2)}) async-start(), calls=%async_computation.5 | async-start | bytes 34603008 | tf_op jit(solution)/shard_map/all_gather | solution.py:216
  1198.1 914.6 %all-gather.24.cloned.1.call-start = ((), (), s32[]{:S(2)}) async-start(), calls=%async_computation.9 | async-start | bytes 12976128 | tf_op jit(solution)/shard_map/all_gather | solution.py:245
  1198.8 1551.5 %reduce-scatter.3.cloned.1.call-start = ((), (), s32[]{:S(2)}) async-start(), calls=%async_computation.10 | async-start | bytes 43253760 | tf_op jit(solution)/shard_map/reduce_scatter | solution.py:358
  1362.6 45.1 %collective-permute-start.1 = (bf16[2,256,2,512]{1,3,0,2:T(8,128)(2,1)}, bf16[2,256,2,512]{1,3,0,2:T(8,128)(2,1)}, u32[]{:S(2)}, u32[]{:S(2)}) collective-permute-start(bf16[2,256,2,512]{1,3,0,2:T(8,128)(2,1)} %get-tuple-element.1289), channel_id=1, source_target_pairs={{0,4},{4,8},{8,12},{12,16},{16,20},{20,24},{24,28},{1,5},{5,9},{9,... | collective-permute-start | bytes 3145736 | tf_op jit(solution)/shard_map/while/body/eval_jaxpr/ppermute | solution.py:21
  1406.0 37.9 collective-permute-start.2
  1447.0 44.6 %collective-permute-start.1 = (bf16[2,256,2,512]{1,3,0,2:T(8,128)(2,1)}, bf16[2,256,2,512]{1,3,0,2:T(8,128)(2,1)}, u32[]{:S(2)}, u32[]{:S(2)}) collective-permute-start(bf16[2,256,2,512]{1,3,0,2:T(8,128)(2,1)} %get-tuple-element.1289), channel_id=1, source_target_pairs={{0,4},{4,8},{8,12},{12,16},{16,20},{20,24},{24,28},{1,5},{5,9},{9,... | collective-permute-start | bytes 3145736 | tf_op jit(solution)/shard_map/while/body/eval_jaxpr/ppermute | solution.py:21
  1462.4 33.0 collective-permute-start.2
  1498.6 27.4 collective-permute-start.1
  1523.9 40.8 collective-permute-start.2
  1584.9 33.5 collective-permute-start.2
  1623.8 67.3 %collective-permute-start.2 = (bf16[2,256,2,512]{1,3,0,2:T(8,128)(2,1)}, bf16[2,256,2,512]{1,3,0,2:T(8,128)(2,1)}, u32[]{:S(2)}, u32[]{:S(2)}) collective-permute-start(bf16[2,256,2,512]{1,3,0,2:T(8,128)(2,1)} %get-tuple-element.1291), channel_id=1, source_target_pairs={{0,4},{4,8},{8,12},{12,16},{16,20},{20,24},{24,28},{28,0},{1,5},{5... | collective-permute-start | bytes 3145736 | tf_op jit(solution)/shard_map/while/body/eval_jaxpr/ppermute | solution.py:26
  1696.4 55.9 %collective-permute-start.2 = (bf16[2,256,2,512]{1,3,0,2:T(8,128)(2,1)}, bf16[2,256,2,512]{1,3,0,2:T(8,128)(2,1)}, u32[]{:S(2)}, u32[]{:S(2)}) collective-permute-start(bf16[2,256,2,512]{1,3,0,2:T(8,128)(2,1)} %get-tuple-element.1291), channel_id=1, source_target_pairs={{0,4},{4,8},{8,12},{12,16},{16,20},{20,24},{24,28},{28,0},{1,5},{5... | collective-permute-start | bytes 3145736 | tf_op jit(solution)/shard_map/while/body/eval_jaxpr/ppermute | solution.py:26
  1756.9 56.7 %collective-permute-start.3 = (bf16[2,256,2,512]{3,1,0,2:T(8,128)(2,1)S(1)}, bf16[2,256,2,512]{3,1,0,2:T(8,128)(2,1)S(1)}, u32[]{:S(2)}, u32[]{:S(2)}) collective-permute-start(bf16[2,256,2,512]{3,1,0,2:T(8,128)(2,1)S(1)} %copy.122), channel_id=1, source_target_pairs={{0,4},{4,8},{8,12},{12,16},{16,20},{20,24},{24,28},{28,0},{1,5},{5... | collective-permute-start | bytes 3145736 | tf_op jit(solution)/shard_map/ppermute | solution.py:26
  1862.6 2492.5 %reduce-scatter.5.cloned.1.call-start = ((), (), s32[]{:S(2)}) async-start(), calls=%async_computation.11 | async-start | bytes 207618048 | tf_op jit(solution)/shard_map/reduce_scatter | solution.py:366
  (76 other events, 3425.4 us)
Sparse Core Ops, SparseCore 0:
  10.9 98.8 all-gather.9
  112.7 75.6 all-gather.11
  191.4 399.5 all-gather.13
  593.7 192.5 all-gather.17
  789.2 354.4 all-gather.19
  1197.5 75.5 all-gather.21
  1276.0 210.4 all-gather.15
  1489.3 104.8 all-gather.23
  1862.7 887.6 reduce-scatter.2
  2756.6 1598.3 reduce-scatter.4
where the time goes:
time: 4380 us; the launch traced here: 4370 us
  waiting for transfers between devices  3120 us (71%)
  starting transfers between devices  403 us (9%)
  matrix products  371 us (8%)
  other arithmetic  243 us (6%)
  blocking collectives  117 us (3%)
  local copies, waits for them, and re-layouts  92 us (2%)
    reduce_scatter x1, waiting for transfers between devices, shards(): lax.psum_scatter(jnp.concatenate([matmul_tn(hidden_low, d_gu_low), matmul...  1600 us
    reduce_scatter x1, waiting for transfers between devices, shards(): lax.psum_scatter(jnp.concatenate([matmul_tn(normed_low, d_qkv_low), matmu...  569 us
    ppermute x14, starting transfers between devices, passed_along(): return lax.ppermute(block, axis, route)  352 us
    all_gather x1, waiting for transfers between devices, shards(): lax.all_gather(fresh_gate_up, ('seq', 'rows'), axis=0, tiled=True)  317 us
    ppermute x8, waiting for transfers between devices, from_behind(): lax.ppermute(array, axis, [(i, (i + by) % count) for i in range(count)])  250 us
    all_gather x1, waiting for transfers between devices, shards(): lax.all_gather(fresh_down, ('seq', 'rows'), axis=0, tiled=True)  149 us
    concatenate x1, other arithmetic, shards(): jnp.concatenate([matmul_tn(hidden_low, d_gu_low), matmul_tn(grad_low, act...  131 us
    all_gather x1, waiting for transfers between devices, shards(): lax.all_gather(gate_up_weight, ('seq', 'rows'), axis=0, tiled=True)  127 us
  transfers between devices with their start and end apart: 32, of which 24 were waited for; matrix products, arithmetic and copies ran while one was open for 14% of the time, Pallas kernels for 0%

commit v1 on v0

v1 whole, which is shorter than its diff:
```python
from functools import partial
import math

import jax
import jax.numpy as jnp
from jax import lax
from jax.experimental import pallas as pl
from jax.experimental.pallas import tpu as pltpu
from jax.sharding import PartitionSpec as P

QUERY_HEADS = 32
KEY_VALUE_HEADS = 8
HEAD = 64
EPSILON = 1e-06
F32 = jnp.float32
BF16 = jnp.bfloat16
HIGHEST = lax.Precision.HIGHEST
SCALE = HEAD ** (-0.5)
SCALE2 = SCALE * math.log2(math.e)
VMEM = 56 * 1024 * 1024


def swap(block, mask):
    return lax.ppermute(block, "seq", [(i, i ^ mask) for i in range(lax.axis_size("seq"))])


def masks_between_chips():
    return [1 << bit for bit in range(1, lax.axis_size("seq").bit_length() - 1)]


def natural(place, me, seq):
    return me[0] ^ (2 * lax.rem(place, seq // 2) + lax.div(place, seq // 2))


def dot_nn(a, b):
    return jnp.dot(a, b, preferred_element_type=F32)


def dot_nt(a, b, precision=None):
    return lax.dot_general(
        a, b, (((1,), (1,)), ((), ())), preferred_element_type=F32, precision=precision
    )


def dot_tn(a, b):
    return lax.dot_general(a, b, (((0,), (0,)), ((), ())), preferred_element_type=F32)


def gather_plane(chunk):
    half = chunk.shape[0] // 2
    masks = masks_between_chips()
    own = [chunk]
    if len(masks) == 2:
        along_x = swap(chunk, 2)
        along_y = swap(chunk, 4)
        diagonal = jnp.concatenate([swap(along_y[:half], 2), swap(along_x[half:], 4)], axis=0)
        own = [chunk, along_x, along_y, diagonal]
    else:
        for mask in masks:
            own = own + [swap(part, mask) for part in own]
    return jnp.concatenate(own + [swap(part, 1) for part in own], axis=0)


def scatter_plane(odd, even):
    masks = masks_between_chips()
    size = even.shape[0] >> len(masks)
    half = size // 2
    both = even + swap(odd, 1).astype(F32)
    parts = [both[i * size : (i + 1) * size] for i in range(1 << len(masks))]
    if len(masks) == 2:
        mine, to_x, to_y, diagonal = parts
        diagonal = diagonal.astype(BF16)
        from_x = swap(diagonal[:half], 2).astype(F32)
        from_y = swap(diagonal[half:], 4).astype(F32)
        to_x = jnp.concatenate([to_x[:half], to_x[half:] + from_y], axis=0).astype(BF16)
        to_y = jnp.concatenate([to_y[:half] + from_x, to_y[half:]], axis=0).astype(BF16)
        return mine + swap(to_x, 2).astype(F32) + swap(to_y, 4).astype(F32)
    for mask in reversed(masks):
        kept = len(parts) // 2
        parts = [
            parts[i] + swap(parts[kept + i].astype(BF16), mask).astype(F32) for i in range(kept)
        ]
    return parts[0]


def lane_of(shape):
    return lax.broadcasted_iota(jnp.int32, shape, len(shape) - 1)


def swap_halves(v):
    first = lane_of(v.shape) % HEAD < HEAD // 2
    return jnp.where(first, pltpu.roll(v, 96, 1), pltpu.roll(v, 32, 1))


def head_mean(v):
    rows = lax.broadcasted_iota(jnp.int32, (128, 128), 0) // HEAD
    cols = lax.broadcasted_iota(jnp.int32, (128, 128), 1) // HEAD
    block = jnp.where(rows == cols, 1.0 / HEAD, 0.0).astype(F32)
    return jnp.dot(v, block, preferred_element_type=F32, precision=HIGHEST)


def qkv_kernel(me, x_ref, w_ref, cos_ref, sin_ref, gain_ref, raw_ref, q_ref, kv_ref):
    rows, slots = q_ref.shape[0], q_ref.shape[1]
    raw = dot_nn(x_ref[...], w_ref[...])
    cos, sin = cos_ref[...], sin_ref[...]
    keys = lane_of((slots, 128)) < HEAD
    for r in range(rows):
        part = raw[r * slots : (r + 1) * slots]
        raw_ref[r] = part
        last = part.shape[1] // 128 - 1
        for s in range(last + 1):
            v = part[:, s * 128 : (s + 1) * 128]
            factor = lax.rsqrt(head_mean(v * v) + EPSILON)
            n = v * factor * gain_ref[:, s * 128 : (s + 1) * 128]
            out = n * cos + swap_halves(n) * sin
            if s < last:
                q_ref[r, :, s * 128 : (s + 1) * 128] = out.astype(BF16)
            else:
                kv_ref[r] = jnp.where(keys, out, v).astype(BF16)


def qkv_call(me, x, w, cos, sin, gains, rows, slots):
    chunk = rows * slots
    width = w.shape[1]
    query_width = width - 128
    seq = x.shape[0] // chunk
    total = seq * slots
    return pl.pallas_call(
        qkv_kernel,
        grid_spec=pltpu.PrefetchScalarGridSpec(
            num_scalar_prefetch=1,
            grid=(seq,),
            in_specs=[
                pl.BlockSpec((chunk, x.shape[1]), lambda i, me: (i, 0)),
                pl.BlockSpec(w.shape, lambda i, me: (0, 0)),
                pl.BlockSpec((slots, 128), lambda i, me: (natural(i, me, seq), 0)),
                pl.BlockSpec((slots, 128), lambda i, me: (natural(i, me, seq), 0)),
                pl.BlockSpec((1, width), lambda i, me: (0, 0)),
            ],
            out_specs=[
                pl.BlockSpec((rows, slots, width), lambda i, me: (0, natural(i, me, seq), 0)),
                pl.BlockSpec((rows, slots, query_width), lambda i, me: (0, natural(i, me, seq), 0)),
                pl.BlockSpec((rows, slots, 128), lambda i, me: (0, natural(i, me, seq), 0)),
            ],
        ),
        out_shape=[
            jax.ShapeDtypeStruct((rows, total, width), F32),
            jax.ShapeDtypeStruct((rows, total, query_width), BF16),
            jax.ShapeDtypeStruct((rows, total, 128), BF16),
        ],
        compiler_params=pltpu.CompilerParams(vmem_limit_bytes=VMEM),
        name="qkv_prepare",
    )(me, x, w, cos, sin, gains)


def attend_kernel(lengths, q_ref, kv_ref, out_ref, low_ref, log_ref, k2, vo, acc):
    row, step = pl.program_id(0), pl.program_id(1)
    block = q_ref.shape[1]
    group = q_ref.shape[2] // HEAD
    length = lengths[row]

    @pl.when(step == 0)
    def _():
        kv = kv_ref[0].astype(F32)
        keys = lane_of(kv.shape) < HEAD
        k2[...] = jnp.where(keys, kv, pltpu.roll(kv, HEAD, 1)).astype(BF16)
        vo[...] = jnp.where(keys, 1.0, kv).astype(BF16)

    low_half = lane_of((block, 128)) < HEAD
    queries = []
    for h in range(group):
        part = q_ref[0, :, (h // 2) * 128 : (h // 2 + 1) * 128].astype(F32)
        kept = low_half if h % 2 == 0 else jnp.logical_not(low_half)
        queries.append(jnp.where(kept, part, 0.0).astype(BF16))
    acc[...] = jnp.zeros_like(acc)

    def one_block(at, masked):
        begin = pl.multiple_of(at * block, block)
        keys = k2[pl.ds(begin, block), :]
        values = vo[pl.ds(begin, block), :]
        if masked:
            key_place = begin + lax.broadcasted_iota(jnp.int32, (block, block), 1)
            query_place = step * block + lax.broadcasted_iota(jnp.int32, (block, block), 0)
            allowed = (key_place <= query_place) & (key_place < length)
        for h in range(group):
            weights = jnp.exp2(dot_nt(queries[h], keys) * SCALE2)
            if masked:
                weights = jnp.where(allowed, weights, 0.0)
            acc[h] += dot_nn(weights.astype(BF16), values)

    full = jnp.minimum(step, lax.div(length, block))

    def body(at, carry):
        one_block(at, False)
        return carry

    lax.fori_loop(0, full, body, 0)

    @pl.when(full * block < length)
    def _():
        one_block(full, True)

    for g in range(group // 2):
        even, odd = acc[2 * g], acc[2 * g + 1]
        even_turned, odd_turned = pltpu.roll(even, HEAD, 1), pltpu.roll(odd, HEAD, 1)
        mixed = jnp.where(low_half, even_turned / even, odd / odd_turned)
        out_ref[0, :, g * 128 : (g + 1) * 128] = mixed
        low_ref[0, 0, :, g * 128 : (g + 1) * 128] = mixed.astype(BF16)
        log_ref[0, 2 * g : 2 * g + 1, :] = jnp.log2(even.T[0:1, :])
        log_ref[0, 2 * g + 1 : 2 * g + 2, :] = jnp.log2(odd.T[0:1, :])
    log_ref[0, group:, :] = jnp.zeros((8 - group, block), F32)


def attend_call(lengths, q, kv, block):
    rows, total, width = q.shape
    seq = total // block
    return pl.pallas_call(
        attend_kernel,
        grid_spec=pltpu.PrefetchScalarGridSpec(
            num_scalar_prefetch=1,
            grid=(rows, seq),
            in_specs=[
                pl.BlockSpec((1, block, width), lambda r, i, n: (r, i, 0)),
                pl.BlockSpec((1, total, 128), lambda r, i, n: (r, 0, 0)),
            ],
            out_specs=[
                pl.BlockSpec((1, block, width), lambda r, i, n: (r, i, 0)),
                pl.BlockSpec((1, 1, block, width), lambda r, i, n: (i, r, 0, 0)),
                pl.BlockSpec((1, 8, block), lambda r, i, n: (r, 0, i)),
            ],
            scratch_shapes=[
                pltpu.VMEM((total, 128), BF16),
                pltpu.VMEM((total, 128), BF16),
                pltpu.VMEM((width // HEAD, block, 128), F32),
            ],
        ),
        out_shape=[
            jax.ShapeDtypeStruct((rows, total, width), F32),
            jax.ShapeDtypeStruct((seq, rows, block, width), BF16),
            jax.ShapeDtypeStruct((rows, 8, total), F32),
        ],
        compiler_params=pltpu.CompilerParams(vmem_limit_bytes=VMEM),
        name="attend",
    )(lengths, q, kv)


def attend_back_kernel(
    lengths, q_ref, kv_ref, out_ref, grad_ref, log_ref, dq_ref, dkv_ref, delta, dqt, kacc, vacc
):
    row, step = pl.program_id(0), pl.program_id(1)
    block = kv_ref.shape[1]
    count = q_ref.shape[1] // block
    width = q_ref.shape[2]
    group = width // HEAD
    length = lengths[row]

    @pl.when(step == 0)
    def _():
        dqt[...] = jnp.zeros_like(dqt)
        heads = lax.broadcasted_iota(jnp.int32, (8, width), 0)
        pick = jnp.where(lane_of((8, width)) // HEAD == heads, 1.0, 0.0).astype(F32)
        for i in range(count):
            product = grad_ref[i, 0].astype(F32) * out_ref[0, i * block : (i + 1) * block, :]
            delta[:, i * block : (i + 1) * block] = dot_nt(pick, product, HIGHEST)

    kacc[...] = jnp.zeros_like(kacc)
    vacc[...] = jnp.zeros_like(vacc)
    begin = step * block
    kv = kv_ref[0].astype(F32)
    turned = pltpu.roll(kv, HEAD, 1)
    low_half = lane_of((block, 128)) < HEAD
    keys = [
        jnp.where(low_half, kv, 0.0).astype(BF16),
        jnp.where(low_half, 0.0, turned).astype(BF16),
    ]
    values = [
        jnp.where(low_half, turned, 0.0).astype(BF16),
        jnp.where(low_half, 0.0, kv).astype(BF16),
    ]
    keys_turned = [
        jnp.where(low_half, kv, 0.0).T.astype(BF16),
        jnp.where(low_half, 0.0, turned).T.astype(BF16),
    ]

    def one_block(at, masked):
        first = pl.multiple_of(at * block, block)
        if masked:
            key_place = begin + lax.broadcasted_iota(jnp.int32, (block, block), 0)
            query_place = first + lax.broadcasted_iota(jnp.int32, (block, block), 1)
            allowed = (key_place <= query_place) & (key_place < length)
        for g in range(group // 2):
            queries = q_ref[0, pl.ds(first, block), g * 128 : (g + 1) * 128]
            grads = grad_ref[at, 0, :, g * 128 : (g + 1) * 128]
            turned_sum = None
            for side in range(2):
                h = 2 * g + side
                logs = log_ref[0, h : h + 1, pl.ds(first, block)]
                deltas = delta[h : h + 1, pl.ds(first, block)]
                weights = jnp.exp2(dot_nt(keys[side], queries) * SCALE2 - logs)
                if masked:
                    weights = jnp.where(allowed, weights, 0.0)
                d_weights = dot_nt(values[side], grads)
                d_scores = (weights * (d_weights - deltas)).astype(BF16)
                vacc[side] += dot_nn(weights.astype(BF16), grads)
                kacc[side] += dot_nn(d_scores, queries)
                term = dot_nn(keys_turned[side], d_scores)
                turned_sum = term if turned_sum is None else turned_sum + term
            dqt[g, :, pl.ds(first, block)] += turned_sum

    @pl.when(begin < length)
    def _():
        inside = begin + block <= length

        @pl.when(inside)
        def _():
            one_block(step, True)

            def body(at, carry):
                one_block(at, False)
                return carry

            lax.fori_loop(step + 1, count, body, 0)

        @pl.when(jnp.logical_not(inside))
        def _():
            def body(at, carry):
                one_block(at, True)
                return carry

            lax.fori_loop(step, count, body, 0)

    ksum = jnp.where(low_half, kacc[0], 0.0) + pltpu.roll(jnp.where(low_half, 0.0, kacc[1]), HEAD, 1)
    vsum = pltpu.roll(jnp.where(low_half, vacc[0], 0.0), HEAD, 1) + jnp.where(
        low_half, 0.0, vacc[1]
    )
    dkv_ref[0] = jnp.where(low_half, ksum * SCALE, vsum)

    @pl.when(step == count - 1)
    def _():
        for g in range(group // 2):
            for i in range(count):
                dq_ref[0, i * block : (i + 1) * block, g * 128 : (g + 1) * 128] = (
                    dqt[g, :, i * block : (i + 1) * block].T * SCALE
                )


def attend_back_call(lengths, q, kv, attended, grads, logs):
    rows, total, width = q.shape
    seq, block = grads.shape[0], grads.shape[2]
    return pl.pallas_call(
        attend_back_kernel,
        grid_spec=pltpu.PrefetchScalarGridSpec(
            num_scalar_prefetch=1,
            grid=(rows, seq),
            in_specs=[
                pl.BlockSpec((1, total, width), lambda r, i, n: (r, 0, 0)),
                pl.BlockSpec((1, block, 128), lambda r, i, n: (r, i, 0)),
                pl.BlockSpec((1, total, width), lambda r, i, n: (r, 0, 0)),
                pl.BlockSpec((seq, 1, block, width), lambda r, i, n: (0, r, 0, 0)),
                pl.BlockSpec((1, 8, total), lambda r, i, n: (r, 0, 0)),
            ],
            out_specs=[
                pl.BlockSpec((1, total, width), lambda r, i, n: (r, 0, 0)),
                pl.BlockSpec((1, block, 128), lambda r, i, n: (r, i, 0)),
            ],
            scratch_shapes=[
                pltpu.VMEM((8, total), F32),
                pltpu.VMEM((width // 128, 128, total), F32),
                pltpu.VMEM((2, block, 128), F32),
                pltpu.VMEM((2, block, 128), F32),
            ],
        ),
        out_shape=[
            jax.ShapeDtypeStruct((rows, total, width), F32),
            jax.ShapeDtypeStruct((rows, total, 128), F32),
        ],
        compiler_params=pltpu.CompilerParams(vmem_limit_bytes=VMEM),
        name="attend_back",
    )(lengths, q, kv, attended, grads, logs)


def prepare_back_kernel(
    me, raw_ref, dq_ref, dkv_ref, cos_ref, sin_ref, gain_ref, out_ref, gain_grad_ref
):
    rows, slots = dq_ref.shape[0], dq_ref.shape[1]
    cos, sin = cos_ref[...], sin_ref[...]
    keys = lane_of((slots, 128)) < HEAD
    last = raw_ref.shape[2] // 128 - 1

    @pl.when(pl.program_id(0) == 0)
    def _():
        gain_grad_ref[...] = jnp.zeros_like(gain_grad_ref)

    for r in range(rows):
        for s in range(last + 1):
            lanes = slice(s * 128, (s + 1) * 128)
            raw = raw_ref[r, :, lanes]
            grad = dq_ref[r, :, lanes] if s < last else dkv_ref[r]
            gain = gain_ref[:, lanes]
            turned = grad * cos + swap_halves(grad * sin)
            factor = lax.rsqrt(head_mean(raw * raw) + EPSILON)
            gain_grad_ref[:, lanes] += jnp.sum(turned * raw * factor, axis=0, keepdims=True)
            u = turned * gain
            mean = head_mean(u * raw)
            result = factor * u - raw * (factor * factor * factor) * mean
            if s == last:
                result = jnp.where(keys, result, grad)
            out_ref[r * slots : (r + 1) * slots, lanes] = result.astype(BF16)


def prepare_back_call(me, raw, dq, dkv, cos, sin, gains, slots):
    rows, total, width = raw.shape
    seq = total // slots
    return pl.pallas_call(
        prepare_back_kernel,
        grid_spec=pltpu.PrefetchScalarGridSpec(
            num_scalar_prefetch=1,
            grid=(seq,),
            in_specs=[
                pl.BlockSpec((rows, slots, width), lambda i, me: (0, natural(i, me, seq), 0)),
                pl.BlockSpec((rows, slots, width - 128), lambda i, me: (0, natural(i, me, seq), 0)),
                pl.BlockSpec((rows, slots, 128), lambda i, me: (0, natural(i, me, seq), 0)),
                pl.BlockSpec((slots, 128), lambda i, me: (natural(i, me, seq), 0)),
                pl.BlockSpec((slots, 128), lambda i, me: (natural(i, me, seq), 0)),
                pl.BlockSpec((1, width), lambda i, me: (0, 0)),
            ],
            out_specs=[
                pl.BlockSpec((rows * slots, width), lambda i, me: (i, 0)),
                pl.BlockSpec((1, width), lambda i, me: (0, 0)),
            ],
        ),
        out_shape=[
            jax.ShapeDtypeStruct((rows * total, width), BF16),
            jax.ShapeDtypeStruct((1, width), F32),
        ],
        compiler_params=pltpu.CompilerParams(vmem_limit_bytes=VMEM),
        name="prepare_back",
    )(me, raw, dq, dkv, cos, sin, gains)


def ffn_kernel(hidden_ref, grad_ref, gu_ref, down_ref, act_ref, dgu_ref):
    part = down_ref.shape[1]
    hidden = hidden_ref[...]
    gate = dot_nn(hidden, gu_ref[:, :part])
    up = dot_nn(hidden, gu_ref[:, part:])
    d_act = dot_nn(grad_ref[...], down_ref[...])
    sigmoid = 1.0 / (1.0 + jnp.exp(-gate))
    silu = gate * sigmoid
    act_ref[...] = (silu * up).astype(BF16)
    dgu_ref[:, :part] = (d_act * up * (sigmoid + silu * (1.0 - sigmoid))).astype(BF16)
    dgu_ref[:, part:] = (d_act * silu).astype(BF16)


def ffn_call(hidden, grad, gu, down):
    count, width = hidden.shape
    part = down.shape[1]
    block = 256
    return pl.pallas_call(
        ffn_kernel,
        grid=(count // block,),
        in_specs=[
            pl.BlockSpec((block, width), lambda i: (i, 0)),
            pl.BlockSpec((block, width), lambda i: (i, 0)),
            pl.BlockSpec(gu.shape, lambda i: (0, 0), pipeline_mode=pl.Buffered(1)),
            pl.BlockSpec(down.shape, lambda i: (0, 0), pipeline_mode=pl.Buffered(1)),
        ],
        out_specs=[
            pl.BlockSpec((block, part), lambda i: (i, 0)),
            pl.BlockSpec((block, 2 * part), lambda i: (i, 0)),
        ],
        out_shape=[
            jax.ShapeDtypeStruct((count, part), BF16),
            jax.ShapeDtypeStruct((count, 2 * part), BF16),
        ],
        compiler_params=pltpu.CompilerParams(vmem_limit_bytes=VMEM),
        name="ffn",
    )(hidden, grad, gu, down)


def all_to_all(block):
    return lax.all_to_all(block, "seq", 0, 0, tiled=True)


def gather_z(block):
    full = lax.all_gather(block, "rows", axis=1, tiled=True)
    return full.reshape(-1, full.shape[-1])


def scatter_z(grad):
    grad = grad.reshape(lax.axis_size("seq"), -1, grad.shape[-1])
    return lax.psum_scatter(grad, "rows", scatter_dimension=1, tiled=True)


def shards(
    tokens,
    lengths,
    norm_gains,
    qk_gains,
    qkv_weight,
    out_weight,
    gate_up_weight,
    down_weight,
    cotangent,
):
    rows, slots, width = tokens.shape
    count = rows * slots
    seq = lax.axis_size("seq")
    group = QUERY_HEADS // seq
    query_width = group * HEAD
    sharing = seq // KEY_VALUE_HEADS
    total = seq * slots
    depth = qkv_weight.shape[0]
    kv_at = QUERY_HEADS * HEAD
    part = down_weight.shape[1] // seq
    me = lax.axis_index("seq").astype(jnp.int32)[None]
    gains = norm_gains.astype(F32)

    qkv_scaled = (qkv_weight.astype(F32) * gains[0][:, None]).astype(BF16)
    kv_scaled = qkv_scaled[:, kv_at:].reshape(depth, 2, KEY_VALUE_HEADS, HEAD)
    qkv_blocks = jnp.concatenate(
        [
            qkv_scaled[:, :kv_at].reshape(depth, seq, query_width),
            jnp.repeat(kv_scaled[:, 0], sharing, axis=1),
            jnp.repeat(kv_scaled[:, 1], sharing, axis=1),
        ],
        axis=2,
    ).transpose(1, 0, 2)
    qkv_mine = gather_z(all_to_all(qkv_blocks))
    out_full = lax.all_gather(out_weight, ("seq", "rows"), axis=0, tiled=True)
    gu_scaled = (gate_up_weight.astype(F32) * gains[1][:, None]).astype(BF16)
    gu_blocks = gu_scaled.reshape(depth, 2, seq, part).transpose(2, 0, 1, 3)
    gu_mine = gather_z(all_to_all(gu_blocks.reshape(seq, depth, 2 * part)))
    down_blocks = down_weight.reshape(depth, seq, part).transpose(1, 0, 2)
    down_mine = gather_z(all_to_all(down_blocks))

    lane = jnp.arange(128) % HEAD
    frequency = jnp.exp(
        -math.log(10000.0) * ((lane % (HEAD // 2)).astype(F32) * (2.0 / HEAD))
    )
    angles = jnp.arange(total).astype(F32)[:, None] * frequency[None, :]
    cos = jnp.cos(angles)
    sin = jnp.where(lane < HEAD // 2, -1.0, 1.0)[None, :] * jnp.sin(angles)
    qk = qk_gains.astype(F32)
    head_gains = jnp.concatenate([jnp.tile(qk[0], group), qk[1], jnp.ones((HEAD,), F32)])[None, :]

    inputs = tokens.reshape(count, width).astype(F32)
    r0 = lax.rsqrt(jnp.mean(inputs * inputs, axis=-1, keepdims=True) + EPSILON)
    unit0 = gather_plane((inputs * r0).astype(BF16))
    raw, q, kv = qkv_call(me, unit0, qkv_mine, cos, sin, head_gains, rows, slots)
    attended_mine, attended_low, logs = attend_call(lengths, q, kv, slots)
    attended = all_to_all(attended_low).transpose(1, 2, 0, 3).reshape(count, kv_at)
    middle = inputs + dot_nt(attended, out_full)
    r1 = lax.rsqrt(jnp.mean(middle * middle, axis=-1, keepdims=True) + EPSILON)

    grad_low = cotangent.reshape(count, width)
    grad_all = gather_plane(grad_low)
    unit1 = gather_plane((middle * r1).astype(BF16))
    act, d_gu = ffn_call(unit1, grad_all, gu_mine, down_mine)
    half = seq * count // 2
    u_odd = dot_nt(d_gu[half:], gu_mine).astype(BF16)
    u = scatter_plane(u_odd, dot_nt(d_gu[:half], gu_mine))
    down_sum = scatter_z(dot_tn(grad_all, act).astype(BF16))
    gu_sum = scatter_z(dot_tn(unit1, d_gu).astype(BF16))
    branch_odd = dot_nt(act[half:], down_mine).astype(BF16)
    branch = scatter_plane(branch_odd, dot_nt(act[:half], down_mine))
    output = (middle + branch).astype(BF16).reshape(rows, slots, width)

    d_middle = (
        grad_low.astype(F32)
        + r1 * u
        - middle * (r1 * r1 * r1) * jnp.mean(u * middle, axis=-1, keepdims=True)
    )
    d_branch = d_middle.astype(BF16)
    d_attended = dot_nn(d_branch, out_full).astype(BF16)
    d_attended = d_attended.reshape(rows, slots, seq, query_width).transpose(2, 0, 1, 3)
    d_attended = all_to_all(d_attended)
    out_sum = lax.psum_scatter(
        dot_tn(d_branch, attended).astype(BF16), "seq", scatter_dimension=0, tiled=True
    )
    out_sum = lax.psum_scatter(out_sum, "rows", scatter_dimension=0, tiled=True)
    dq, dkv = attend_back_call(lengths, q, kv, attended_mine, d_attended, logs)
    d_qkv, head_gain_grad = prepare_back_call(me, raw, dq, dkv, cos, sin, head_gains, slots)
    u0_odd = dot_nt(d_qkv[half:], qkv_mine).astype(BF16)
    u0 = scatter_plane(u0_odd, dot_nt(d_qkv[:half], qkv_mine))
    qkv_sum = scatter_z(dot_tn(unit0, d_qkv).astype(BF16))
    input_grad = (
        d_middle + r0 * u0 - inputs * (r0 * r0 * r0) * jnp.mean(u0 * inputs, axis=-1, keepdims=True)
    )
    input_grad = input_grad.astype(BF16).reshape(rows, slots, width)
    qk_grad = jnp.stack(
        [head_gain_grad[0, :query_width].reshape(group, HEAD).sum(0), head_gain_grad[0, query_width : query_width + HEAD]]
    )
    qk_grad = lax.psum(qk_grad, ("seq", "rows"))

    gu_sum = all_to_all(gu_sum).reshape(seq, depth, 2, part).transpose(1, 2, 0, 3)
    gu_sum = gu_sum.reshape(depth, 2 * seq * part).astype(F32)
    down_sum = all_to_all(down_sum).transpose(1, 0, 2).reshape(depth, seq * part).astype(F32)
    qkv_sum = all_to_all(qkv_sum).transpose(1, 0, 2).astype(F32)
    kv_sum = qkv_sum[:, :, query_width:].reshape(depth, KEY_VALUE_HEADS, sharing, 2 * HEAD).sum(2)
    qkv_sum = jnp.concatenate(
        [
            qkv_sum[:, :, :query_width].reshape(depth, -1),
            kv_sum[:, :, :HEAD].reshape(depth, -1),
            kv_sum[:, :, HEAD:].reshape(depth, -1),
        ],
        axis=1,
    )
    norm_gain_grad = jnp.stack(
        [
            jnp.sum(qkv_weight.astype(F32) * qkv_sum, axis=1),
            jnp.sum(gate_up_weight.astype(F32) * gu_sum, axis=1),
        ]
    )
    return (
        output,
        input_grad,
        norm_gain_grad,
        qk_grad,
        qkv_sum * gains[0][:, None],
        out_sum.astype(F32),
        gu_sum * gains[1][:, None],
        down_sum,
    )


def solution(mesh):
    in_specs = (
        P("rows", "seq", None),
        P("rows"),
        P(None, ("seq", "rows")),
        P(),
        P(("seq", "rows"), None),
        P(("seq", "rows"), None),
        P(("seq", "rows"), None),
        P(("seq", "rows"), None),
        P("rows", "seq", None),
    )
    out_specs = (
        P("rows", "seq", None),
        P("rows", "seq", None),
        P(None, ("seq", "rows")),
        P(),
        P(("seq", "rows"), None),
        P(("seq", "rows"), None),
        P(("seq", "rows"), None),
        P(("seq", "rows"), None),
    )
    return jax.shard_map(shards, mesh=mesh, in_specs=in_specs, out_specs=out_specs, check_vma=False)
```

time: 4380 us -> 1300 us (0.30)
  waiting for transfers between devices: 3120 us -> 477 us
  starting transfers between devices: 403 us -> 49.8 us
  Pallas kernels: 0 us -> 204 us
  other arithmetic: 243 us -> 63.8 us
  matrix products: 371 us -> 207 us
  blocking collectives: 117 us -> 176 us
    reduce_scatter x2 -> x5, waiting for transfers between devices: 2170 us -> 115 us  [the longest x3 104 us: scatter_z(): return lax.psum_scatter(grad, 'rows', scatter_dimension=1, tiled=True)]
    all_gather x8 -> x4, waiting for transfers between devices: 680 us -> 0.01 us  [the longest x3 0.01 us: gather_z(): full = lax.all_gather(block, 'rows', axis=1, tiled=True)]
    ppermute x22 -> x39, starting transfers between devices: 402 us -> 25.4 us  [swap(): lax.ppermute(block, 'seq', [(i, i ^ mask) for i in range(lax.axis_size('s...]
    pallas_call x0 -> x5, Pallas kernels: none -> 204 us  [the longest x1 66.2 us: attend_back_call(): pl.pallas_call(attend_back_kernel, grid_spec=pltpu.PrefetchScalarGridSpec...]
    dot_general x19 -> x12, matrix products: 371 us -> 207 us  [the longest x7 109 us: dot_nt(): lax.dot_general(a, b, (((1,), (1,)), ((), ())), preferred_element_type=F3...]
    concatenate x3 -> x10, other arithmetic: 160 us -> 9.94 us  [the longest x3 4.53 us: scatter_plane(): jnp.concatenate([to_x[:half], to_x[half:] + from_y], axis=0).astype(BF16)]
    psum x1, blocking collectives: 47 us -> 133 us  [shards(): qk_grad = lax.psum(qk_grad, ('seq', 'rows'))]
    all_gather x1 -> x0, blocking collectives: 69.9 us -> none  [shards(): lax.all_gather(norm_gains, ('seq', 'rows'), axis=1, tiled=True)]
  transfers between devices with their start and end apart: 32 -> 54, of which waited for: 24 -> 21; matrix products, arithmetic and copies ran while one was open for 14% -> 26% of each run, Pallas kernels for 0% -> 11%
where the time goes in v1:
time: 1300 us; the launch traced here: 1290 us
  waiting for transfers between devices  477 us (37%)
  matrix products  207 us (16%)
  Pallas kernels  204 us (16%)
  blocking collectives  176 us (14%)
  local copies, waits for them, and re-layouts  98.3 us (8%)
  other arithmetic  63.8 us (5%)
  starting transfers between devices  49.8 us (4%)
  between operations  14.9 us (1%)
    ppermute x39, waiting for transfers between devices, swap(): lax.ppermute(block, 'seq', [(i, i ^ mask) for i in range(lax.axis_size('s...  323 us
    psum x1, blocking collectives, shards(): qk_grad = lax.psum(qk_grad, ('seq', 'rows'))  133 us
    dot_general x7, matrix products, dot_nt(): lax.dot_general(a, b, (((1,), (1,)), ((), ())), preferred_element_type=F3...  109 us
    reduce_scatter x3, waiting for transfers between devices, scatter_z(): return lax.psum_scatter(grad, 'rows', scatter_dimension=1, tiled=True)  104 us
    dot_general x4, matrix products, dot_tn(): lax.dot_general(a, b, (((0,), (0,)), ((), ())), preferred_element_type=F32)  88.4 us
    pallas_call x1, Pallas kernels, attend_back_call(): pl.pallas_call(attend_back_kernel, grid_spec=pltpu.PrefetchScalarGridSpec...  66.2 us
    pallas_call x1, Pallas kernels, ffn_call(): pl.pallas_call(ffn_kernel, grid=(count // block,), in_specs=[pl.BlockSpec...  62.7 us
    unnamed x120, local copies, waits for them, and re-layouts  49.2 us
  transfers between devices with their start and end apart: 54, of which 21 were waited for; matrix products, arithmetic and copies ran while one was open for 26% of the time, Pallas kernels for 11%

profile of v1, /device:TPU:0, one launch (start us, length us, event | category | flops | bytes accessed | tf_op | source)
XLA Modules:
  0.0 1291.1 jit_solution(16331418432331982948)
XLA Ops:
  64.9 39.0 %collective-permute-done.1 = bf16[512,2048]{1,0:T(8,128)(2,1)} collective-permute-done((bf16[512,2048]{1,0:T(8,128)(2,1)}, bf16[512,2048]{1,0:T(8,128)(2,1)}, u32[]{:S(2)}, u32[]{:S(2)}) %collective-permute-start.1) | collective-permute-done | bytes 2097184 | tf_op jit(solution)/shard_map/ppermute | solution.py:24
  116.6 48.8 %collective-permute-done.2 = bf16[256,2048]{1,0:T(8,128)(2,1)S(1)} collective-permute-done((bf16[256,2048]{1,0:T(8,128)(2,1)S(1)}, bf16[256,2048]{1,0:T(8,128)(2,1)S(1)}, u32[]{:S(2)}, u32[]{:S(2)}) %collective-permute-start.2) | collective-permute-done | bytes 1048608 | tf_op jit(solution)/shard_map/ppermute | solution.py:24
  190.5 20.6 %qkv_prepare.1 = (f32[2,2048,384]{2,1,0:T(8,128)}, bf16[2,2048,256]{2,1,0:T(8,128)(2,1)}, bf16[2,2048,128]{2,1,0:T(8,128)(2,1)}) custom-call(s32[1]{0:T(128)} %bitcast.1.me, bf16[4096,2048]{1,0:T(8,128)(2,1)} %constant_dynamic-update-slice_fusion.x_ref, bf16[2048,384]{1,0:T(8,128)(2,1)} %bitcast.120, f32[2048,128]{1,0:T(8,128)} %get-tuple-element.63.cos_ref, ...), custom_call_target="tpu_custom_call" | custom-call | tf_op jit(solution)/shard_map/qkv_prepare/pallas_call | solution.py:128
  211.0 38.8 %attend.1 = (f32[2,2048,256]{2,1,0:T(8,128)}, bf16[8,2,256,256]{3,2,1,0:T(8,128)(2,1)}, f32[2,8,2048]{2,1,0:T(8,128)}) custom-call(s32[2]{0:T(128)} %lengths.3, bf16[2,2048,256]{2,1,0:T(8,128)(2,1)} %get-tuple-element.20.q_ref, bf16[2,2048,128]{2,1,0:T(8,128)(2,1)} %get-tuple-element.21.kv_ref), custom_call_target="tpu_custom_call" | custom-call | tf_op jit(solution)/shard_map/attend/pallas_call | solution.py:217
  258.2 23.2 %all-to-all-done.1 = bf16[8,2,256,256]{3,2,1,0:T(8,128)(2,1)} async-done(((bf16[8,2,256,256]{3,2,1,0:T(8,128)(2,1)}), bf16[8,2,256,256]{3,2,1,0:T(8,128)(2,1)}, u32[]{:S(2)}, u32[]{:S(2)}) %all-to-all-start.1) | async-done | bytes 2097184 | tf_op jit(solution)/shard_map/all_to_all | solution.py:481
  297.2 28.2 %collective-permute-done.17 = bf16[512,2048]{1,0:T(8,128)(2,1)} collective-permute-done((bf16[512,2048]{1,0:T(8,128)(2,1)}, bf16[512,2048]{1,0:T(8,128)(2,1)}, u32[]{:S(2)}, u32[]{:S(2)}) %collective-permute-start.17) | collective-permute-done | bytes 2097184 | tf_op jit(solution)/shard_map/ppermute | solution.py:24
  330.3 22.5 %collective-permute-done.18 = bf16[256,2048]{1,0:T(8,128)(2,1)S(1)} collective-permute-done((bf16[256,2048]{1,0:T(8,128)(2,1)S(1)}, bf16[256,2048]{1,0:T(8,128)(2,1)S(1)}, u32[]{:S(2)}, u32[]{:S(2)}) %collective-permute-start.18) | collective-permute-done | bytes 1048608 | tf_op jit(solution)/shard_map/ppermute | solution.py:24
  352.8 39.3 %collective-permute-done.19 = bf16[256,2048]{1,0:T(8,128)(2,1)S(1)} collective-permute-done((bf16[256,2048]{1,0:T(8,128)(2,1)S(1)}, bf16[256,2048]{1,0:T(8,128)(2,1)S(1)}, u32[]{:S(2)}, u32[]{:S(2)}) %collective-permute-start.19) | collective-permute-done | bytes 1048608 | tf_op jit(solution)/shard_map/ppermute | solution.py:24
  400.7 21.6 %collective-permute-done.10 = bf16[256,2048]{1,0:T(8,128)(2,1)S(1)} collective-permute-done((bf16[256,2048]{1,0:T(8,128)(2,1)S(1)}, bf16[256,2048]{1,0:T(8,128)(2,1)S(1)}, u32[]{:S(2)}, u32[]{:S(2)}) %collective-permute-start.10) | collective-permute-done | bytes 1048608 | tf_op jit(solution)/shard_map/ppermute | solution.py:24
  438.3 62.7 %ffn.1 = (bf16[4096,1024]{1,0:T(8,128)(2,1)}, bf16[4096,2048]{1,0:T(8,128)(2,1)}) custom-call(bf16[4096,2048]{1,0:T(8,128)(2,1)} %constant_dynamic-update-slice_fusion.9.hidden_ref, bf16[4096,2048]{1,0:T(8,128)(2,1)} %copy-done.4, bf16[2048,2048]{1,0:T(8,128)(2,1)} %bitcast.113, bf16[2048,1024]{1,0:T(8,128)(2,1)} %bitcast.125), custom_call_target="tpu_custom_call" | custom-call | tf_op jit(solution)/shard_map/ffn/pallas_call | solution.py:458
  501.1 24.0 %fusion.3 = bf16[2048,2048]{1,0:T(8,128)(2,1)} fusion(bf16[2048,2048]{1,0:T(8,128)(2,1)} %bitcast.114, bf16[4096,2048]{1,0:T(8,128)(2,1)} %get-tuple-element.24), kind=kOutput, calls=%fused_computation.6 | convolution fusion | flops 17184063488 | bytes 25165824 | tf_op jit(solution)/shard_map/dot_general | solution.py:40
  539.3 23.9 %convolution_convert_fusion.4 = bf16[2048,1024]{1,0:T(8,128)(2,1)} fusion(bf16[4096,2048]{1,0:T(8,128)(2,1)S(1)} %bitcast.102, bf16[4096,1024]{1,0:T(8,128)(2,1)} %get-tuple-element.23), kind=kOutput, calls=%fused_computation.40 | convolution fusion | flops 17181966336 | bytes 29360128 | tf_op jit(solution)/shard_map/dot_general | solution.py:46
  563.2 26.7 %fusion.46 = (bf16[2048,2048]{1,0:T(8,128)(2,1)}, f32[2048,2048]{1,0:T(8,128)}) fusion(bf16[2048,2048]{1,0:T(8,128)(2,1)} %collective-permute-done.29, bf16[2048,2048]{1,0:T(8,128)(2,1)} %bitcast.115, bf16[4096,2048]{1,0:T(8,128)(2,1)} %get-tuple-element.24), kind=kOutput, calls=%fused_computation.146 | convolution fusion | flops 17192452096 | bytes 50331648 | tf_op jit(solution)/shard_map/dot_general | solution.py:40
  595.1 17.6 %fusion.47 = (bf16[2048,2048]{1,0:T(8,128)(2,1)}, f32[2048,2048]{1,0:T(8,128)}) fusion(bf16[2048,2048]{1,0:T(8,128)(2,1)} %collective-permute-done.24, bf16[2048,1024]{1,0:T(8,128)(2,1)S(1)} %bitcast.127, bf16[4096,1024]{1,0:T(8,128)(2,1)} %get-tuple-element.23), kind=kOutput, calls=%fused_computation.147 | convolution fusion | flops 8602517504 | bytes 41943040 | tf_op jit(solution)/shard_map/dot_general | solution.py:40
  626.9 16.0 %collective-permute-done.27 = bf16[256,2048]{1,0:T(8,128)(2,1)S(1)} collective-permute-done((bf16[256,2048]{1,0:T(8,128)(2,1)S(1)}, bf16[256,2048]{1,0:T(8,128)(2,1)S(1)}, u32[]{:S(2)}, u32[]{:S(2)}) %collective-permute-start.27) | collective-permute-done | bytes 1048608 | tf_op jit(solution)/shard_map/ppermute | solution.py:24
  652.0 36.3 %collective-permute-done.33 = bf16[512,2048]{1,0:T(8,128)(2,1)S(1)} collective-permute-done((bf16[512,2048]{1,0:T(8,128)(2,1)S(1)}, bf16[512,2048]{1,0:T(8,128)(2,1)S(1)}, u32[]{:S(2)}, u32[]{:S(2)}) %collective-permute-start.33) | collective-permute-done | bytes 2097184 | tf_op jit(solution)/shard_map/ppermute | solution.py:24
  690.3 42.3 %collective-permute-done.28 = bf16[512,2048]{1,0:T(8,128)(2,1)} collective-permute-done((bf16[512,2048]{1,0:T(8,128)(2,1)}, bf16[512,2048]{1,0:T(8,128)(2,1)}, u32[]{:S(2)}, u32[]{:S(2)}) %collective-permute-start.28) | collective-permute-done | bytes 2097184 | tf_op jit(solution)/shard_map/ppermute | solution.py:24
  750.8 30.0 %all_to_all.41.grad_ref = bf16[8,2,256,256]{3,2,1,0:T(8,128)(2,1)} all-to-all(bf16[8,2,256,256]{3,2,1,0:T(8,128)(2,1)S(1)} %bitcast.111), channel_id=1, replica_groups=mesh['seq'=8,'rows'=4] {'seq'}, dimensions={0} | all-to-all | bytes 4194304 | tf_op jit(solution)/shard_map/all_to_all | solution.py:481
  780.8 66.2 %attend_back.1 = (f32[2,2048,256]{2,1,0:T(8,128)}, f32[2,2048,128]{2,1,0:T(8,128)}) custom-call(s32[2]{0:T(128)} %lengths.3, bf16[2,2048,256]{2,1,0:T(8,128)(2,1)} %get-tuple-element.20.q_ref, bf16[2,2048,128]{2,1,0:T(8,128)(2,1)} %get-tuple-element.21.kv_ref, f32[2,2048,256]{2,1,0:T(8,128)} %get-tuple-element.26.out_ref, ...), custom_call_target="tpu_custom_call" | custom-call | tf_op jit(solution)/shard_map/attend_back/pallas_call | solution.py:350
  846.9 15.3 %prepare_back.1 = (bf16[4096,384]{1,0:T(8,128)(2,1)}, f32[1,384]{1,0:T(1,128)}) custom-call(s32[1]{0:T(128)} %bitcast.1.me, f32[2,2048,384]{2,1,0:T(8,128)} %get-tuple-element.25.raw_ref, f32[2,2048,256]{2,1,0:T(8,128)} %get-tuple-element.28.dq_ref, f32[2,2048,128]{2,1,0:T(8,128)} %get-tuple-element.29.dkv_ref, f32[2048,128]{1,0:T(8,128)} %get-tuple-element.63.cos_ref, ...), custom_call_target="tpu_custom_call" | custom-call | tf_op jit(solution)/shard_map/prepare_back/pallas_call | solution.py:414
  876.5 43.5 %convolution_convert_fusion.3 = bf16[2048,2048]{1,0:T(8,128)(2,1)} fusion(bf16[4096,2048]{1,0:T(8,128)(2,1)} %constant_dynamic-update-slice_fusion.9.hidden_ref, bf16[4096,2048]{1,0:T(8,128)(2,1)} %get-tuple-element.24), kind=kOutput, calls=%fused_computation.10 | convolution fusion | flops 34363932672 | bytes 41943040 | tf_op jit(solution)/shard_map/dot_general | solution.py:46
  963.8 19.2 %collective-permute-done.37 = bf16[256,2048]{1,0:T(8,128)(2,1)} collective-permute-done((bf16[256,2048]{1,0:T(8,128)(2,1)}, bf16[256,2048]{1,0:T(8,128)(2,1)}, u32[]{:S(2)}, u32[]{:S(2)}) %collective-permute-start.37) | collective-permute-done | bytes 1048608 | tf_op jit(solution)/shard_map/ppermute | solution.py:24
  990.1 104.4 %reduce-scatter.8.cloned.1.call-done = bf16[8,64,2048]{2,1,0:T(8,128)(2,1)} async-done(((bf16[8,256,2048]{2,1,0:T(8,128)(2,1)}), bf16[8,64,2048]{2,1,0:T(8,128)(2,1)}) %reduce-scatter.8.cloned.1.call-update) | async-done | bytes 2097168 | tf_op jit(solution)/shard_map/reduce_scatter | solution.py:491
  1103.6 132.8 %psum.7 = f32[2,64]{1,0:T(2,128)} all-reduce(f32[2,64]{1,0:T(2,128)S(1)} %pad_maximum_fusion.11), channel_id=1, replica_groups=mesh['seq'=8,'rows'=4] {'seq','rows'}, use_global_device_ids=true, to_apply=%region_9.10 | all-reduce | flops 128 | bytes 1024 | tf_op jit(solution)/shard_map/psum | solution.py:593
  (318 shorter events, 333.3 us)
Async XLA Ops:
  7.2 183.3 %all-gather.5.cloned.1.call-start = ((), (), s32[]{:S(2)}) async-start(), calls=%async_computation.13 | async-start | bytes 1966080 | tf_op jit(solution)/shard_map/all_gather | solution.py:485
  25.2 261.0 %all-gather.7.cloned.1.call-start = ((), (), s32[]{:S(2)}) async-start(), calls=%async_computation.14 | async-start | bytes 8650752 | tf_op jit(solution)/shard_map/all_gather | solution.py:529
  30.6 407.7 %all-gather.11.cloned.1.call-start = ((), (), s32[]{:S(2)}) async-start(), calls=%async_computation.16 | async-start | bytes 5242880 | tf_op jit(solution)/shard_map/all_gather | solution.py:485
  60.2 108.5 %all-to-all-start.2 = ((bf16[8,64,2048]{2,1,0:T(8,128)(2,1)}), bf16[8,64,2048]{2,1,0:T(8,128)(2,1)}, u32[]{:S(2)}, u32[]{:S(2)}) async-start(bf16[8,64,2048]{2,1,0:T(8,128)(2,1)} %reshape.174), calls=%async_computation.2 | async-start | bytes 4194304 | tf_op jit(solution)/shard_map/all_to_all | solution.py:481
  64.6 373.8 %all-gather.9.cloned.1.call-start = ((), (), s32[]{:S(2)}) async-start(), calls=%async_computation.15 | async-start | bytes 10485760 | tf_op jit(solution)/shard_map/all_gather | solution.py:485
  110.4 66.9 %collective-permute-start.4 = (bf16[512,2048]{1,0:T(8,128)(2,1)}, bf16[512,2048]{1,0:T(8,128)(2,1)}, u32[]{:S(2)}, u32[]{:S(2)}) collective-permute-start(bf16[512,2048]{1,0:T(8,128)(2,1)} %get-tuple-element.71), channel_id=1, source_target_pairs={{0,4},{4,0},{8,12},{12,8},{16,20},{20,16},{24,28},{28,24},{1,5},{5... | collective-permute-start | bytes 6291464 | tf_op jit(solution)/shard_map/ppermute | solution.py:24
  110.4 70.4 %collective-permute-start.5 = (bf16[512,2048]{1,0:T(8,128)(2,1)}, bf16[512,2048]{1,0:T(8,128)(2,1)}, u32[]{:S(2)}, u32[]{:S(2)}) collective-permute-start(bf16[512,2048]{1,0:T(8,128)(2,1)} %collective-permute-done), channel_id=1, source_target_pairs={{0,4},{4,0},{8,12},{12,8},{16,20},{20,16},{24,28},{28,24},{1,5},{5... | collective-permute-start | bytes 6291464 | tf_op jit(solution)/shard_map/ppermute | solution.py:24
  116.5 67.6 %collective-permute-start.6 = (bf16[512,2048]{1,0:T(8,128)(2,1)}, bf16[512,2048]{1,0:T(8,128)(2,1)}, u32[]{:S(2)}, u32[]{:S(2)}) collective-permute-start(bf16[512,2048]{1,0:T(8,128)(2,1)} %collective-permute-done.1), channel_id=1, source_target_pairs={{0,4},{4,0},{8,12},{12,8},{16,20},{20,16},{24,28},{28,24},{1,5},{5... | collective-permute-start | bytes 6291464 | tf_op jit(solution)/shard_map/ppermute | solution.py:24
  254.2 683.0 %reduce-scatter.14.cloned.1.call-start = ((), (), s32[]{:S(2)}) async-start(), calls=%async_computation.21 | async-start | bytes 5242880 | tf_op jit(solution)/shard_map/reduce_scatter | solution.py:491
  254.8 70.5 %collective-permute-start.17 = (bf16[512,2048]{1,0:T(8,128)(2,1)}, bf16[512,2048]{1,0:T(8,128)(2,1)}, u32[]{:S(2)}, u32[]{:S(2)}) collective-permute-start(bf16[512,2048]{1,0:T(8,128)(2,1)} %bitcast.116), channel_id=1, source_target_pairs={{0,16},{4,20},{8,24},{12,28},{16,0},{20,4},{24,8},{28,12},{1,17},{... | collective-permute-start | bytes 6291464 | tf_op jit(solution)/shard_map/ppermute | solution.py:24
  256.7 71.0 %collective-permute-start.16 = (bf16[512,2048]{1,0:T(8,128)(2,1)}, bf16[512,2048]{1,0:T(8,128)(2,1)}, u32[]{:S(2)}, u32[]{:S(2)}) collective-permute-start(bf16[512,2048]{1,0:T(8,128)(2,1)} %bitcast.117), channel_id=1, source_target_pairs={{0,8},{4,12},{8,0},{12,4},{16,24},{20,28},{24,16},{28,20},{1,9},{5... | collective-permute-start | bytes 6291464 | tf_op jit(solution)/shard_map/ppermute | solution.py:24
  296.7 96.0 %collective-permute-start.9 = (bf16[512,2048]{1,0:T(8,128)(2,1)S(1)}, bf16[512,2048]{1,0:T(8,128)(2,1)S(1)}, u32[]{:S(2)}, u32[]{:S(2)}) collective-permute-start(bf16[512,2048]{1,0:T(8,128)(2,1)S(1)} %get-tuple-element.33), channel_id=1, source_target_pairs={{0,16},{4,20},{8,24},{12,28},{16,0},{20,4},{24,8},{28,12},{1,17},{... | collective-permute-start | bytes 6291464 | tf_op jit(solution)/shard_map/ppermute | solution.py:24
  329.5 67.6 %collective-permute-start.8 = (bf16[512,2048]{1,0:T(8,128)(2,1)S(1)}, bf16[512,2048]{1,0:T(8,128)(2,1)S(1)}, u32[]{:S(2)}, u32[]{:S(2)}) collective-permute-start(bf16[512,2048]{1,0:T(8,128)(2,1)S(1)} %get-tuple-element.33), channel_id=1, source_target_pairs={{0,8},{4,12},{8,0},{12,4},{16,24},{20,28},{24,16},{28,20},{1,9},{5... | collective-permute-start | bytes 6291464 | tf_op jit(solution)/shard_map/ppermute | solution.py:24
  330.3 68.5 %collective-permute-start.20 = (bf16[512,2048]{1,0:T(8,128)(2,1)S(1)}, bf16[512,2048]{1,0:T(8,128)(2,1)S(1)}, u32[]{:S(2)}, u32[]{:S(2)}) collective-permute-start(bf16[512,2048]{1,0:T(8,128)(2,1)S(1)} %bitcast.118), channel_id=1, source_target_pairs={{0,4},{4,0},{8,12},{12,8},{16,20},{20,16},{24,28},{28,24},{1,5},{5... | collective-permute-start | bytes 6291464 | tf_op jit(solution)/shard_map/ppermute | solution.py:24
  563.2 396.8 %reduce-scatter.6.cloned.1.call-start = ((), (), s32[]{:S(2)}) async-start(), calls=%async_computation.17 | async-start | bytes 1966080 | tf_op jit(solution)/shard_map/reduce_scatter | solution.py:491
  648.2 84.4 %collective-permute-start.28 = (bf16[512,2048]{1,0:T(8,128)(2,1)}, bf16[512,2048]{1,0:T(8,128)(2,1)}, u32[]{:S(2)}, u32[]{:S(2)}) collective-permute-start(bf16[512,2048]{1,0:T(8,128)(2,1)} %pad_maximum_fusion.4), channel_id=1, source_target_pairs={{0,16},{4,20},{8,24},{12,28},{16,0},{20,4},{24,8},{28,12},{1,17},{... | collective-permute-start | bytes 6291464 | tf_op jit(solution)/shard_map/ppermute | solution.py:24
  651.4 81.2 %collective-permute-start.26 = (bf16[512,2048]{1,0:T(8,128)(2,1)}, bf16[512,2048]{1,0:T(8,128)(2,1)}, u32[]{:S(2)}, u32[]{:S(2)}) collective-permute-start(bf16[512,2048]{1,0:T(8,128)(2,1)} %pad_maximum_fusion.3), channel_id=1, source_target_pairs={{0,8},{4,12},{8,0},{12,4},{16,24},{20,28},{24,16},{28,20},{1,9},{5... | collective-permute-start | bytes 6291464 | tf_op jit(solution)/shard_map/ppermute | solution.py:24
  876.5 218.0 %reduce-scatter.8.cloned.1.call-start = ((), (), s32[]{:S(2)}) async-start(), calls=%async_computation.18 | async-start | bytes 10485760 | tf_op jit(solution)/shard_map/reduce_scatter | solution.py:491
  920.1 335.8 %reduce-scatter.10.cloned.1.call-start = ((), (), s32[]{:S(2)}) async-start(), calls=%async_computation.19 | async-start | bytes 9437184 | tf_op jit(solution)/shard_map/reduce_scatter | solution.py:577
  960.0 134.5 %all-to-all-start.5 = ((bf16[8,64,384]{2,1,0:T(8,128)(2,1)}), bf16[8,64,384]{2,1,0:T(8,128)(2,1)S(1)}, u32[]{:S(2)}, u32[]{:S(2)}) async-start(bf16[8,64,384]{2,1,0:T(8,128)(2,1)} %reduce-scatter.6.cloned.1.call-done), calls=%async_computation.6 | async-start | bytes 786432 | tf_op jit(solution)/shard_map/all_to_all | solution.py:481
  989.8 271.7 %collective-permute-start.38 = (bf16[512,2048]{1,0:T(8,128)(2,1)}, bf16[512,2048]{1,0:T(8,128)(2,1)}, u32[]{:S(2)}, u32[]{:S(2)}) collective-permute-start(bf16[512,2048]{1,0:T(8,128)(2,1)} %pad_maximum_fusion.8), channel_id=1, source_target_pairs={{0,16},{4,20},{8,24},{12,28},{16,0},{20,4},{24,8},{28,12},{1,17},{... | collective-permute-start | bytes 6291464 | tf_op jit(solution)/shard_map/ppermute | solution.py:24
  1094.5 147.2 %all-to-all-start.6 = ((bf16[8,64,2048]{2,1,0:T(8,128)(2,1)}), bf16[8,64,2048]{2,1,0:T(8,128)(2,1)S(1)}, u32[]{:S(2)}, u32[]{:S(2)}) async-start(bf16[8,64,2048]{2,1,0:T(8,128)(2,1)} %reduce-scatter.8.cloned.1.call-done), calls=%async_computation.8 | async-start | bytes 4194304 | tf_op jit(solution)/shard_map/all_to_all | solution.py:481
  1098.2 184.4 %reduce-scatter.12.cloned.1.call-start = ((), (), s32[]{:S(2)}) async-start(), calls=%async_computation.20 | async-start | bytes 1310720 | tf_op jit(solution)/shard_map/reduce_scatter | solution.py:580
  1101.0 160.6 %collective-permute-start.36 = (bf16[512,2048]{1,0:T(8,128)(2,1)}, bf16[512,2048]{1,0:T(8,128)(2,1)}, u32[]{:S(2)}, u32[]{:S(2)}) collective-permute-start(bf16[512,2048]{1,0:T(8,128)(2,1)} %pad_maximum_fusion.7), channel_id=1, source_target_pairs={{0,8},{4,12},{8,0},{12,4},{16,24},{20,28},{24,16},{28,20},{1,9},{5... | collective-permute-start | bytes 6291464 | tf_op jit(solution)/shard_map/ppermute | solution.py:24
  (75 other events, 2374.9 us)
Sparse Core Ops, SparseCore 0:
  25.3 36.4 all-gather.4
  64.7 107.9 all-gather.6
  174.3 77.9 all-gather.10
  253.7 148.1 all-gather.8
  563.3 86.2 reduce-scatter.13
  876.6 64.7 reduce-scatter.5
  943.9 150.5 reduce-scatter.7
  1098.3 105.5 reduce-scatter.9
  1256.0 26.5 reduce-scatter.11

commit v2 on v1

--- a/solution.py
+++ b/solution.py
@@ -46,41 +46,80 @@
     return lax.dot_general(a, b, (((0,), (0,)), ((), ())), preferred_element_type=F32)
 
 
+def corner(result):
+    flat = result.reshape(-1, result.shape[-1])
+    return flat[:16, :128]
+
+
+def after(value, *results):
+    zero = sum(result.reshape(-1)[0].astype(F32) for result in results) * 0.0
+    return value + zero.astype(value.dtype)
+
+
+def gather_pieces(chunk, earlier):
+    half = chunk.shape[0] // 2
+    along_x, along_y = swap(chunk, 2), swap(chunk, 4)
+    through_x, through_y = after(along_y[:half], earlier), after(along_x[half:], earlier)
+    return [chunk, along_x, along_y, swap(through_x, 2), swap(through_y, 4)]
+
+
 def gather_plane(chunk):
-    half = chunk.shape[0] // 2
-    masks = masks_between_chips()
     own = [chunk]
-    if len(masks) == 2:
-        along_x = swap(chunk, 2)
-        along_y = swap(chunk, 4)
-        diagonal = jnp.concatenate([swap(along_y[:half], 2), swap(along_x[half:], 4)], axis=0)
-        own = [chunk, along_x, along_y, diagonal]
-    else:
-        for mask in masks:
-            own = own + [swap(part, mask) for part in own]
+    for mask in masks_between_chips():
+        own = own + [swap(part, mask) for part in own]
     return jnp.concatenate(own + [swap(part, 1) for part in own], axis=0)
 
 
-def scatter_plane(odd, even):
-    masks = masks_between_chips()
-    size = even.shape[0] >> len(masks)
-    half = size // 2
-    both = even + swap(odd, 1).astype(F32)
-    parts = [both[i * size : (i + 1) * size] for i in range(1 << len(masks))]
-    if len(masks) == 2:
+def gather_natural(block):
+    seq, me, size = lax.axis_size("seq"), lax.axis_index("seq"), block.shape[0]
+    parts = {mask: swap(block, mask) if mask > 0 else block for mask in range(0, seq, 2)}
+    parts.update({mask + 1: swap(part, 1) for mask, part in list(parts.items())})
+    whole = jnp.zeros((seq * size,) + block.shape[1:], block.dtype)
+    for m, part in parts.items():
+        whole = lax.dynamic_update_slice_in_dim(whole, part, (me ^ m) * size, 0)
+    return whole
+
+
+def scatter_chips(parts):
+    if len(parts) == 4:
         mine, to_x, to_y, diagonal = parts
+        half = mine.shape[0] // 2
         diagonal = diagonal.astype(BF16)
         from_x = swap(diagonal[:half], 2).astype(F32)
         from_y = swap(diagonal[half:], 4).astype(F32)
         to_x = jnp.concatenate([to_x[:half], to_x[half:] + from_y], axis=0).astype(BF16)
         to_y = jnp.concatenate([to_y[:half] + from_x, to_y[half:]], axis=0).astype(BF16)
         return mine + swap(to_x, 2).astype(F32) + swap(to_y, 4).astype(F32)
-    for mask in reversed(masks):
+    for mask in reversed(masks_between_chips()):
         kept = len(parts) // 2
         parts = [
             parts[i] + swap(parts[kept + i].astype(BF16), mask).astype(F32) for i in range(kept)
         ]
     return parts[0]
+
+
+def scatter_direct(parts, earlier):
+    total = after(parts[0].astype(F32), earlier)
+    for i in range(1, len(parts)):
+        total = total + swap(parts[i].astype(BF16), 2 * i).astype(F32)
+    return total
+
+
+def scatter_plane(odd, even, scatter=scatter_chips):
+    count = 1 << len(masks_between_chips())
+    size = even.shape[0] // count
+    both = even + swap(odd, 1).astype(F32)
+    return scatter([both[i * size : (i + 1) * size] for i in range(count)])
+
+
+def sum_everywhere(value):
+    for axis in ("seq", "rows"):
+        size = lax.axis_size(axis)
+        mask = 1
+        while mask < size:
+            value = value + lax.ppermute(value, axis, [(i, i ^ mask) for i in range(size)])
+            mask *= 2
+    return value
 
 
 def lane_of(shape):
@@ -110,9 +149,7 @@
         last = part.shape[1] // 128 - 1
         for s in range(last + 1):
             v = part[:, s * 128 : (s + 1) * 128]
-            factor = lax.rsqrt(head_mean(v * v) + EPSILON)
-            n = v * factor * gain_ref[:, s * 128 : (s + 1) * 128]
-            out = n * cos + swap_halves(n) * sin
+            out = normed_rotated(v, cos, sin, gain_ref[:, s * 128 : (s + 1) * 128])
             if s < last:
                 q_ref[r, :, s * 128 : (s + 1) * 128] = out.astype(BF16)
             else:
@@ -240,6 +277,9 @@
             jax.ShapeDtypeStruct((rows, 8, total), F32),
         ],
         compiler_params=pltpu.CompilerParams(vmem_limit_bytes=VMEM),
+        cost_estimate=pl.CostEstimate(
+            flops=rows * total * total * width * 16, bytes_accessed=rows * total * width * 8, transcendentals=0
+        ),
         name="attend",
     )(lengths, q, kv)
 
@@ -375,6 +415,9 @@
             jax.ShapeDtypeStruct((rows, total, 128), F32),
         ],
         compiler_params=pltpu.CompilerParams(vmem_limit_bytes=VMEM),
+        cost_estimate=pl.CostEstimate(
+            flops=rows * total * total * width * 28, bytes_accessed=rows * total * width * 14, transcendentals=0
+        ),
         name="attend_back",
     )(lengths, q, kv, attended, grads, logs)
 
@@ -438,17 +481,970 @@
     )(me, raw, dq, dkv, cos, sin, gains)
 
 
+def neighbours(me):
+    return {
+        "core": me + 1 - 2 * lax.rem(me, 2),
+        "x": me + 2 - 4 * lax.rem(lax.div(me, 2), 2),
+        "y": me + 4 - 8 * lax.div(me, 4),
+    }
+
+
+def remote(source, target, device, send, recv):
+    return pltpu.make_async_remote_copy(
+        src_ref=source,
+        dst_ref=target,
+        send_sem=send,
+        recv_sem=recv,
+        device_id=device,
+        device_id_type=pl.DeviceIdType.MESH,
+    )
+
+
+def greet(devices):
+    barrier = pltpu.get_barrier_semaphore()
+    for device in devices:
+        pl.semaphore_signal(barrier, inc=1, device_id=device, device_id_type=pl.DeviceIdType.MESH)
+    pl.semaphore_wait(barrier, len(devices))
+
+
+def greet_neighbours(to, rows):
+    greet([(to[device], rows) for device in ("core", "x", "y")])
+
+
+def flipped(index, mask, size):
+    result, bit = index, 1
+    while bit < size:
+        if mask & bit:
+            result = result + bit - 2 * bit * lax.rem(lax.div(index, bit), 2)
+        bit *= 2
+    return result
+
+
+class PlaneExchange:
+    def __init__(self, block, target, send, recv, local):
+        self.seq, self.rows = lax.axis_index("seq"), lax.axis_index("rows")
+        self.size = lax.axis_size("seq")
+        self.block, self.target, self.send, self.recv, self.local = block, target, send, recv, local
+
+    @staticmethod
+    def scratch():
+        others = lax.axis_size("seq") - 1
+        return [
+            pltpu.SemaphoreType.DMA((others,)),
+            pltpu.SemaphoreType.DMA((others,)),
+            pltpu.SemaphoreType.DMA,
+        ]
+
+    def peers(self):
+        return [(flipped(self.seq, mask, self.size), self.rows) for mask in range(1, self.size)]
+
+    def copies(self):
+        remotes = [
+            remote(self.block(peer[0]), self.target.at[self.seq], peer, self.send.at[i], self.recv.at[i])
+            for i, peer in enumerate(self.peers())
+        ]
+        own = pltpu.make_async_copy(self.block(self.seq), self.target.at[self.seq], self.local)
+        return remotes, own
+
+    def start(self):
+        remotes, own = self.copies()
+        for copy in remotes:
+            copy.start()
+        own.start()
+
+    def finish(self):
+        remotes, own = self.copies()
+        for copy in remotes:
+            copy.wait()
+        own.wait()
+
+
+class PlaneGather:
+    COPIES = 14
+
+    def __init__(self, own, whole, send, recv):
+        self.seq, self.rows = lax.axis_index("seq"), lax.axis_index("rows")
+        self.half = own.shape[0] // 2
+        self.own, self.whole, self.send, self.recv = own, whole, send, recv
+        self.to = neighbours(self.seq)
+
+    def place(self, at, half):
+        return pl.ds((2 * at + half) * self.half, self.half)
+
+    def copy(self, i):
+        half, own, whole = self.half, self.own, self.whole
+        first, second = own.at[pl.ds(0, half)], own.at[pl.ds(half, half)]
+
+        def moved(at, h, to):
+            return whole.at[self.place(at, h)], whole.at[self.place(to, h)]
+
+        source, target, device = (
+            (second, whole.at[self.place(1, 1)], "x"),
+            (first, whole.at[self.place(2, 0)], "y"),
+            (first, whole.at[self.place(1, 0)], "x"),
+            (second, whole.at[self.place(2, 1)], "y"),
+            (first, whole.at[self.place(4, 0)], "core"),
+            (second, whole.at[self.place(4, 1)], "core"),
+            moved(1, 1, 3) + ("y",),
+            moved(2, 0, 3) + ("x",),
+            moved(1, 1, 5) + ("core",),
+            moved(2, 0, 6) + ("core",),
+            moved(1, 0, 5) + ("core",),
+            moved(2, 1, 6) + ("core",),
+            moved(3, 0, 7) + ("core",),
+            moved(3, 1, 7) + ("core",),
+        )[i]
+        return remote(
+            source, target, (self.to[device], self.rows), self.send.at[i], self.recv.at[i]
+        )
+
+    def fetch(self, unit, target, sem):
+        begin = pl.multiple_of(unit_place(unit) * self.half, self.half)
+        return pltpu.make_async_copy(self.whole.at[pl.ds(begin, self.half)], target, sem)
+
+    def start_fetch(self, unit, target, sem):
+        @pl.when(unit < 2)
+        def _():
+            begin = pl.multiple_of(lax.rem(unit, 2) * self.half, self.half)
+            pltpu.make_async_copy(self.own.at[pl.ds(begin, self.half)], target, sem).start()
+
+        @pl.when(unit >= 2)
+        def _():
+            self.fetch(unit, target, sem).start()
+
+    def keep(self, unit, source, sem):
+        begin = pl.multiple_of(lax.rem(unit, 2) * self.half, self.half)
+        return pltpu.make_async_copy(source, self.whole.at[pl.ds(begin, self.half)], sem)
+
+    def start(self):
+        for i in (0, 1, 2, 3, 4, 5):
+            self.copy(i).start()
+
+    def open_group(self, group):
+        if group == 1:
+            self.copy(0).wait_recv()
+            self.copy(6).start()
+            self.copy(8).start()
+            self.copy(1).wait_recv()
+            self.copy(7).start()
+            self.copy(9).start()
+        if group == 2:
+            self.copy(2).wait_recv()
+            self.copy(10).start()
+            self.copy(3).wait_recv()
+            self.copy(11).start()
+        if group == 3:
+            self.copy(7).wait_recv()
+            self.copy(12).start()
+            self.copy(6).wait_recv()
+            self.copy(13).start()
+
+    def open_second(self, group):
+        for i in ((4, 5), (8, 9), (10, 11), (12, 13))[group]:
+            self.copy(i).wait_recv()
+
+    def finish(self):
+        for i in range(self.COPIES):
+            self.copy(i).wait_send()
+
+
+def unit_place(unit):
+    group, k = lax.div(unit, 4), lax.rem(unit, 4)
+    odd, late = lax.rem(group, 2), lax.div(group, 2)
+    base = 3 * odd + 2 * late + odd * late
+    stride = 1 + 2 * late * (1 - odd)
+    return 8 * lax.div(k, 2) + base + stride * lax.rem(k, 2)
+
+
+def at_unit(unit, value, action):
+    @pl.when(unit == value)
+    def _():
+        action()
+
+
+def normed_rotated(raw, cos, sin, gain):
+    factor = lax.rsqrt(head_mean(raw * raw) + EPSILON)
+    n = raw * factor * gain
+    return n * cos + swap_halves(n) * sin
+
+
+def gather_qkv_kernel(
+    x_ref, w_ref, cos_ref, sin_ref, gain_ref, whole, raw_ref, q_ref, kv_ref,
+    xbuf, rawbuf, qbuf, kvbuf, load, store, keep, send, recv,
+):
+    gather = PlaneGather(x_ref, whole, send, recv)
+    half = gather.half
+    me = gather.seq
+    last = w_ref.shape[1] // 128 - 1
+    greet_neighbours(gather.to, gather.rows)
+    gather.start()
+
+    def stores(unit, slot):
+        place = unit_place(unit)
+        at, row = lax.rem(lax.div(place, 2), 4), lax.rem(place, 2)
+        core = lax.rem(lax.rem(me, 2) + lax.div(place, 8), 2)
+        x = lax.rem(lax.div(me, 2) + at, 2)
+        y = lax.rem(lax.div(me, 4) + lax.div(at, 2), 2)
+        block = core + 2 * x + 4 * y
+        begin = pl.ds(pl.multiple_of(block * half, half), half)
+        return [
+            pltpu.make_async_copy(rawbuf.at[slot], raw_ref.at[row, begin], store.at[0, slot]),
+            pltpu.make_async_copy(qbuf.at[slot], q_ref.at[row, begin], store.at[1, slot]),
+            pltpu.make_async_copy(kvbuf.at[slot], kv_ref.at[row, begin], store.at[2, slot]),
+        ], block
+
+    def body(unit, carry):
+        slot = lax.rem(unit, 2)
+        for group in range(4):
+            at_unit(unit, 4 * group, partial(gather.open_group, group))
+            at_unit(unit, 4 * group + 1, partial(gather.open_second, group))
+
+        @pl.when(lax.rem(unit, 4) == 0)
+        def _():
+            gather.start_fetch(unit, xbuf.at[slot], load.at[slot])
+
+        gather.fetch(unit, xbuf.at[slot], load.at[slot]).wait()
+
+        @pl.when(unit < 2)
+        def _():
+            gather.keep(unit, xbuf.at[slot], keep.at[slot]).start()
+
+        @pl.when((unit == 1) | (unit == 2))
+        def _():
+            gather.keep(unit - 1, xbuf.at[1 - slot], keep.at[1 - slot]).wait()
+
+        @pl.when(lax.rem(unit, 4) != 3)
+        def _():
+            gather.start_fetch(unit + 1, xbuf.at[1 - slot], load.at[1 - slot])
+
+        copies, block = stores(unit, slot)
+
+        @pl.when(unit >= 2)
+        def _():
+            for copy in stores(unit - 2, slot)[0]:
+                copy.wait()
+
+        raw = dot_nn(xbuf[slot], w_ref[...])
+        rawbuf[slot] = raw
+        turn = pl.ds(pl.multiple_of(block * half, half), half)
+        cos, sin = cos_ref[turn, :], sin_ref[turn, :]
+        for s in range(last + 1):
+            lanes = slice(s * 128, (s + 1) * 128)
+            v = raw[:, lanes]
+            out = normed_rotated(v, cos, sin, gain_ref[:, lanes])
+            if s < last:
+                qbuf[slot, :, lanes] = out.astype(BF16)
+            else:
+                kvbuf[slot] = jnp.where(lane_of(v.shape) < HEAD, out, v).astype(BF16)
+        for copy in copies:
+            copy.start()
+        return carry
+
+    lax.fori_loop(0, 16, body, 0)
+    for slot in range(2):
+        for copy in stores(14 + slot, slot)[0]:
+            copy.wait()
+    gather.finish()
+
+
+def gather_qkv_call(x, w, cos, sin, gains, rows, slots):
+    count, width = x.shape
+    seq = lax.axis_size("seq")
+    total = seq * slots
+    cols = w.shape[1]
+    here, there = pl.BlockSpec(memory_space=pltpu.VMEM), pl.BlockSpec(memory_space=pl.ANY)
+    return pl.pallas_call(
+        gather_qkv_kernel,
+        in_specs=[there, here, here, here, here],
+        out_specs=[there] * 4,
+        out_shape=[
+            jax.ShapeDtypeStruct((seq * count, width), BF16),
+            jax.ShapeDtypeStruct((rows, total, cols), F32),
+            jax.ShapeDtypeStruct((rows, total, cols - 128), BF16),
+            jax.ShapeDtypeStruct((rows, total, 128), BF16),
+        ],
+        scratch_shapes=[
+            pltpu.VMEM((2, slots, width), BF16),
+            pltpu.VMEM((2, slots, cols), F32),
+            pltpu.VMEM((2, slots, cols - 128), BF16),
+            pltpu.VMEM((2, slots, 128), BF16),
+            pltpu.SemaphoreType.DMA((2,)),
+            pltpu.SemaphoreType.DMA((3, 2)),
+            pltpu.SemaphoreType.DMA((2,)),
+            pltpu.SemaphoreType.DMA((PlaneGather.COPIES,)),
+            pltpu.SemaphoreType.DMA((PlaneGather.COPIES,)),
+        ],
+        compiler_params=pltpu.CompilerParams(
+            collective_id=1, has_side_effects=True, vmem_limit_bytes=VMEM
+        ),
+        cost_estimate=pl.CostEstimate(
+            flops=2 * seq * count * width * cols * 8, bytes_accessed=seq * count * width * 4, transcendentals=0
+        ),
+        name="gather_qkv",
+    )(x, w, cos, sin, gains)
+
+
+class PlaneScatter:
+    def __init__(self, own, from_x, from_y, odd, even, held, other, diagonal, sems):
+        self.seq, self.rows = lax.axis_index("seq"), lax.axis_index("rows")
+        self.to = neighbours(self.seq)
+        self.half = odd.shape[1]
+        self.own, self.from_x, self.from_y = own, from_x, from_y
+        self.odd, self.even, self.held, self.other, self.diagonal = odd, even, held, other, diagonal
+        self.odd_send, self.odd_recv, self.send, self.recv, self.store = sems
+
+    @staticmethod
+    def scratch(half, width):
+        return [
+            pltpu.VMEM((2, half, width), BF16),
+            pltpu.VMEM((6, half, width), BF16),
+            pltpu.VMEM((2, half, width), F32),
+            pltpu.VMEM((8, half, width), BF16),
+            pltpu.VMEM((2, half, width), BF16),
+            pltpu.SemaphoreType.DMA((2,)),
+            pltpu.SemaphoreType.DMA((8,)),
+            pltpu.SemaphoreType.DMA((6,)),
+            pltpu.SemaphoreType.DMA((6,)),
+            pltpu.SemaphoreType.DMA((2,)),
+        ]
+
+    @staticmethod
+    def place(pair):
+        two, b = lax.div(pair, 2), lax.rem(pair, 2)
+        odd, late = lax.rem(two, 2), lax.div(two, 2)
+        base = 6 * (1 - odd) * (1 - late) + 2 * odd * (1 - late) + 3 * (1 - odd) * late
+        return base + b * (1 + 2 * odd * (1 - late))
+
+    def hand_over(self, pair):
+        slot = lax.rem(pair, 2)
+        return remote(
+            self.odd.at[slot],
+            self.other.at[pair],
+            (self.to["core"], self.rows),
+            self.odd_send.at[slot],
+            self.odd_recv.at[pair],
+        )
+
+    def copy(self, i):
+        first, second = pl.ds(0, self.half), pl.ds(self.half, self.half)
+        target, device = (
+            (self.diagonal.at[0], "x"),
+            (self.diagonal.at[1], "y"),
+            (self.from_x.at[first], "x"),
+            (self.from_y.at[second], "y"),
+            (self.from_x.at[second], "x"),
+            (self.from_y.at[first], "y"),
+        )[i]
+        return remote(
+            self.even.at[i], target, (self.to[device], self.rows), self.send.at[i], self.recv.at[i]
+        )
+
+    def keep(self, i):
+        return pltpu.make_async_copy(
+            self.held.at[i], self.own.at[pl.ds(i * self.half, self.half)], self.store.at[i]
+        )
+
+    def give_odd(self, pair, value):
+        @pl.when(pair >= 2)
+        def _():
+            self.hand_over(pair - 2).wait_send()
+
+        self.odd[lax.rem(pair, 2)] = value.astype(BF16)
+        self.hand_over(pair).start()
+
+    def give_even(self, pair, value_ref):
+        self.hand_over(pair).wait_recv()
+        for at, i in ((0, 0), (1, 1), (2, 2), (3, 3), (4, 4), (5, 5)):
+
+            @pl.when(pair == at)
+            def _(at=at, i=i):
+                total = value_ref[...] + self.other[at].astype(F32)
+                if i >= 4:
+                    self.copy(5 - i).wait_recv()
+                    total = total + self.diagonal[5 - i].astype(F32)
+                self.even[i] = total.astype(BF16)
+                self.copy(i).start()
+
+        for at, i in ((6, 0), (7, 1)):
+
+            @pl.when(pair == at)
+            def _(at=at, i=i):
+                self.held[i] = value_ref[...] + self.other[at].astype(F32)
+                self.keep(i).start()
+
+    def finish(self):
+        for pair in (6, 7):
+            self.hand_over(pair).wait_send()
+        for i in range(6):
+            self.copy(i).wait_send()
+        for i in (2, 3, 4, 5):
+            self.copy(i).wait_recv()
+        for i in range(2):
+            self.keep(i).wait()
+
+
+def gate_and_up(hidden, gu_ref):
+    part = gu_ref.shape[1] // 2
+    gate = dot_nn(hidden, gu_ref[:, :part])
+    up = dot_nn(hidden, gu_ref[:, part:])
+    return gate, up, (gate / (1.0 + jnp.exp(-gate)) * up).astype(BF16)
+
+
+def gate_and_up_back(gate, up, d_act):
+    sigmoid = 1.0 / (1.0 + jnp.exp(-gate))
+    silu = gate * sigmoid
+    d_gate = d_act * up * (sigmoid + silu * (1.0 - sigmoid))
+    return d_gate.astype(BF16), (d_act * silu).astype(BF16)
+
+
+def gather_ffn_kernel(
+    x_ref, c0_ref, cx_ref, cy_ref, cd0_ref, cd1_ref, gu_hbm,
+    whole, near_ref, far_ref, gate_up_ref, act_ref,
+    gu, hbuf, cbuf, gbuf, abuf, weight_sem, load, store, keep, send, recv, piece_send, piece_recv,
+):
+    gather = PlaneGather(x_ref, whole, send, recv)
+    half = gather.half
+    part = gu.shape[1] // 2
+    weights = pltpu.make_async_copy(gu_hbm, gu, weight_sem)
+    weights.start()
+    greet_neighbours(gather.to, gather.rows)
+    gather.start()
+
+    def stores(unit, slot):
+        begin = pl.ds(pl.multiple_of(unit_place(unit) * half, half), half)
+        return [
+            pltpu.make_async_copy(abuf.at[slot], act_ref.at[begin], store.at[0, slot]),
+            pltpu.make_async_copy(gbuf.at[slot], gate_up_ref.at[begin], store.at[1, slot]),
+        ]
+
+    piece_refs = (c0_ref, cx_ref, cy_ref, cd0_ref, cd1_ref)
+    piece_at = ((0, 2), (2, 2), (4, 2), (6, 1), (7, 1))
+
+    def piece(i):
+        begin, size = piece_at[i]
+        target = far_ref.at[pl.ds(begin * half, size * half)]
+        return remote(
+            piece_refs[i],
+            target,
+            (gather.to["core"], gather.rows),
+            piece_send.at[i],
+            piece_recv.at[i],
+        )
+
+    for i in range(5):
+        piece(i).start()
+
+    def passing(at):
+        i = (0, 0, 1, 1, 2, 2, 3, 4)[at]
+        source = piece_refs[i].at[pl.ds((at - piece_at[i][0]) * half, half)]
+        return (
+            pltpu.make_async_copy(source, cbuf.at[at % 2], keep.at[1, 0]),
+            pltpu.make_async_copy(
+                cbuf.at[at % 2], near_ref.at[pl.ds(at * half, half)], keep.at[1, 1]
+            ),
+        )
+
+    def read_piece(at):
+        passing(at)[0].start()
+
+    def write_piece(at):
+        passing(at)[0].wait()
+        passing(at)[1].start()
+
+    def end_piece(at):
+        passing(at)[1].wait()
+
+    def body(unit, carry):
+        slot = lax.rem(unit, 2)
+        for at in range(8):
+            at_unit(unit, 2 * at, partial(read_piece, at))
+            at_unit(unit, 2 * at + 1, partial(write_piece, at))
+            if at < 7:
+                at_unit(unit, 2 * at + 2, partial(end_piece, at))
+        for group in range(4):
+            at_unit(unit, 4 * group, partial(gather.open_group, group))
+            at_unit(unit, 4 * group + 1, partial(gather.open_second, group))
+
+        @pl.when(lax.rem(unit, 4) == 0)
+        def _():
+            gather.start_fetch(unit, hbuf.at[slot], load.at[slot])
+
+        at_unit(unit, 0, weights.wait)
+        gather.fetch(unit, hbuf.at[slot], load.at[slot]).wait()
+
+        @pl.when(unit < 2)
+        def _():
+            gather.keep(unit, hbuf.at[slot], keep.at[0, slot]).start()
+
+        @pl.when((unit == 1) | (unit == 2))
+        def _():
+            gather.keep(unit - 1, hbuf.at[1 - slot], keep.at[0, 1 - slot]).wait()
+
+        @pl.when(lax.rem(unit, 4) != 3)
+        def _():
+            gather.start_fetch(unit + 1, hbuf.at[1 - slot], load.at[1 - slot])
+
+        @pl.when(unit >= 2)
+        def _():
+            for copy in stores(unit - 2, slot):
+                copy.wait()
+
+        gate, up, act = gate_and_up(hbuf[slot], gu)
+        abuf[slot] = act
+        gbuf[slot, :, :part] = gate.astype(BF16)
+        gbuf[slot, :, part:] = up.astype(BF16)
+        for copy in stores(unit, slot):
+            copy.start()
+        return carry
+
+    lax.fori_loop(0, 16, body, 0)
+    for slot in range(2):
+        for copy in stores(14 + slot, slot):
+            copy.wait()
+    end_piece(7)
+    for i in range(5):
+        piece(i).wait_recv()
+        piece(i).wait_send()
+    gather.finish()
+
+
+def gather_ffn_call(x, pieces, gu):
+    count, width = x.shape
+    seq = lax.axis_size("seq")
+    cols = gu.shape[1]
+    half = count // 2
+    there = pl.BlockSpec(memory_space=pl.ANY)
+    return pl.pallas_call(
+        gather_ffn_kernel,
+        in_specs=[there] * 7,
+        out_specs=[there] * 5,
+        out_shape=[
+            jax.ShapeDtypeStruct((seq * count, width), BF16),
+            jax.ShapeDtypeStruct((seq * half, width), BF16),
+            jax.ShapeDtypeStruct((seq * half, width), BF16),
+            jax.ShapeDtypeStruct((seq * count, cols), BF16),
+            jax.ShapeDtypeStruct((seq * count, cols // 2), BF16),
+        ],
+        scratch_shapes=[
+            pltpu.VMEM(gu.shape, BF16),
+            pltpu.VMEM((2, half, width), BF16),
+            pltpu.VMEM((2, half, width), BF16),
+            pltpu.VMEM((2, half, cols), BF16),
+            pltpu.VMEM((2, half, cols // 2), BF16),
+            pltpu.SemaphoreType.DMA,
+            pltpu.SemaphoreType.DMA((2,)),
+            pltpu.SemaphoreType.DMA((2, 2)),
+            pltpu.SemaphoreType.DMA((2, 2)),
+            pltpu.SemaphoreType.DMA((PlaneGather.COPIES,)),
+            pltpu.SemaphoreType.DMA((PlaneGather.COPIES,)),
+            pltpu.SemaphoreType.DMA((5,)),
+            pltpu.SemaphoreType.DMA((5,)),
+        ],
+        compiler_params=pltpu.CompilerParams(
+            collective_id=2, has_side_effects=True, vmem_limit_bytes=VMEM
+        ),
+        cost_estimate=pl.CostEstimate(
+            flops=4 * seq * count * width * cols, bytes_accessed=seq * count * width * 8, transcendentals=0
+        ),
+        name="gather_ffn",
+    )(x, *pieces, gu)
+
+
+def ffn_back_kernel(
+    near_ref, far_ref, gate_up_ref, gu_hbm, down_hbm, _, own, from_x, from_y, dgu_ref,
+    gu, down, cbuf, gbuf, dbuf, total, odd, even, held, other, diagonal,
+    odd_send, odd_recv, send, recv, keep, weight_sem, load, store,
+):
+    scatter = PlaneScatter(
+        own, from_x, from_y, odd, even, held, other, diagonal, (odd_send, odd_recv, send, recv, keep)
+    )
+    half = scatter.half
+    part = down.shape[1]
+    weights = [
+        pltpu.make_async_copy(down_hbm, down, weight_sem.at[0]),
+        pltpu.make_async_copy(gu_hbm, gu, weight_sem.at[1]),
+    ]
+    for copy in weights:
+        copy.start()
+
+    def row_of(unit, whole):
+        side = 8 * (1 - lax.rem(unit, 2)) if whole else 0
+        place = PlaneScatter.place(lax.div(unit, 2)) + side
+        return pl.ds(pl.multiple_of(place * half, half), half)
+
+    def fetch(unit, slot):
+        return [
+            pltpu.make_async_copy(near_ref.at[row_of(unit, False)], cbuf.at[slot], load.at[0, slot]),
+            pltpu.make_async_copy(
+                gate_up_ref.at[row_of(unit, True)], gbuf.at[slot], load.at[1, slot]
+            ),
+        ]
+
+    def start_fetch(unit, slot):
+        near, gates = fetch(unit, slot)
+        gates.start()
+
+        @pl.when(lax.rem(unit, 2) == 0)
+        def _():
+            pltpu.make_async_copy(
+                far_ref.at[row_of(unit, False)], cbuf.at[slot], load.at[0, slot]
+            ).start()
+
+        @pl.when(lax.rem(unit, 2) == 1)
+        def _():
+            near.start()
+
+    def stores(unit, slot):
+        return pltpu.make_async_copy(dbuf.at[slot], dgu_ref.at[row_of(unit, True)], store.at[slot])
+
+    start_fetch(0, 0)
+    greet_neighbours(scatter.to, scatter.rows)
+
+    def body(unit, carry):
+        slot = lax.rem(unit, 2)
+        pair = lax.div(unit, 2)
+        at_unit(unit, 0, weights[0].wait)
+        for copy in fetch(unit, slot):
+            copy.wait()
+
+        @pl.when(unit < 15)
+        def _():
+            start_fetch(unit + 1, 1 - slot)
+
+        @pl.when(unit >= 2)
+        def _():
+            stores(unit - 2, slot).wait()
+
+        d_act = dot_nn(cbuf[slot], down[...])
+        gate, up = gbuf[slot, :, :part].astype(F32), gbuf[slot, :, part:].astype(F32)
+        d_gate, d_up = gate_and_up_back(gate, up, d_act)
+        dbuf[slot, :, :part] = d_gate
+        dbuf[slot, :, part:] = d_up
+        stores(unit, slot).start()
+        at_unit(unit, 0, weights[1].wait)
+        total[...] = dot_nt(dbuf[slot], gu[...])
+
+        @pl.when(slot == 0)
+        def _():
+            scatter.give_odd(pair, total[...])
+
+        @pl.when(slot == 1)
+        def _():
+            scatter.give_even(pair, total)
+
+        return carry
+
+    lax.fori_loop(0, 16, body, 0)
+    for slot in range(2):
+        stores(14 + slot, slot).wait()
+    scatter.finish()
+
+
+def weight_grad_kernel(*refs):
+    lefts, right_ref, out_ref = refs[:-3], refs[-3], refs[-1]
+    depth = out_ref.shape[1]
+    size = right_ref.shape[0] // len(lefts)
+    grad = None
+    for i, left in enumerate(lefts):
+        term = dot_tn(left[...], right_ref[i * size : (i + 1) * size, :])
+        grad = term if grad is None else grad + term
+    for z in range(out_ref.shape[0]):
+        out_ref[z] = grad[z * depth : (z + 1) * depth].astype(BF16)
+
+
+def weight_grad_call(lefts, right, earlier, depth, name):
+    seq, parts = lax.axis_size("seq"), lax.axis_size("rows")
+    width = lefts[0].shape[1]
+    block = width // seq
+    tokens, cols = right.shape
+    return pl.pallas_call(
+        weight_grad_kernel,
+        grid=(seq,),
+        in_specs=[pl.BlockSpec((left.shape[0], block), lambda i: (0, i)) for left in lefts]
+        + [
+            pl.BlockSpec(right.shape, lambda i: (0, 0), pipeline_mode=pl.Buffered(1)),
+            pl.BlockSpec(memory_space=pl.ANY),
+        ],
+        out_specs=pl.BlockSpec((parts, depth, cols), lambda i: (0, i, 0)),
+        out_shape=jax.ShapeDtypeStruct((parts, seq * depth, cols), BF16),
+        compiler_params=pltpu.CompilerParams(vmem_limit_bytes=VMEM),
+        cost_estimate=pl.CostEstimate(
+            flops=2 * tokens * width * cols,
+            bytes_accessed=2 * tokens * (width + cols),
+            transcendentals=0,
+        ),
+        name=name,
+    )(*lefts, right, earlier)
+
+
+def grad_exchange_kernel(
+    left_ref, right_ref, spread_ref, blocks_ref, _, out_ref, spread_out, blocks_out, *sems
+):
+    width = spread_out.shape[2]
+
+    def columns(i):
+        return spread_ref.at[:, pl.ds(pl.multiple_of(i * width, width), width)]
+
+    spread = PlaneExchange(columns, spread_out, *sems[:3])
+    blocks = PlaneExchange(lambda i: blocks_ref.at[i], blocks_out, *sems[3:])
+
+    @pl.when(pl.program_id(0) == 0)
+    def _():
+        greet(spread.peers())
+        spread.start()
+        blocks.start()
+
+    depth = out_ref.shape[1]
+    grad = dot_tn(left_ref[...], right_ref[...])
+    for z in range(out_ref.shape[0]):
+        out_ref[z] = grad[z * depth : (z + 1) * depth].astype(BF16)
+
+    @pl.when(pl.program_id(0) == pl.num_programs(0) - 1)
+    def _():
+        spread.finish()
+        blocks.finish()
+
+
+def grad_exchange_call(left, right, spread, blocks, earlier, depth):
+    seq, parts = lax.axis_size("seq"), lax.axis_size("rows")
+    tokens, cols = right.shape
+    width = left.shape[1]
+    block = width // seq
+    there = pl.BlockSpec(memory_space=pl.ANY)
+    return pl.pallas_call(
+        grad_exchange_kernel,
+        grid=(seq,),
+        in_specs=[
+            pl.BlockSpec((tokens, block), lambda i: (0, i)),
+            pl.BlockSpec(right.shape, lambda i: (0, 0), pipeline_mode=pl.Buffered(1)),
+            there,
+            there,
+            there,
+        ],
+        out_specs=[pl.BlockSpec((parts, depth, cols), lambda i: (0, i, 0)), there, there],
+        out_shape=[
+            jax.ShapeDtypeStruct((parts, seq * depth, cols), BF16),
+            jax.ShapeDtypeStruct((seq, spread.shape[0], spread.shape[1] // seq), BF16),
+            jax.ShapeDtypeStruct(blocks.shape, BF16),
+        ],
+        scratch_shapes=PlaneExchange.scratch() + PlaneExchange.scratch(),
+        compiler_params=pltpu.CompilerParams(
+            collective_id=5, has_side_effects=True, vmem_limit_bytes=VMEM
+        ),
+        cost_estimate=pl.CostEstimate(
+            flops=2 * tokens * width * cols,
+            bytes_accessed=2 * tokens * (width + cols),
+            transcendentals=0,
+        ),
+        name="gate_up_grad",
+    )(left, right, spread, blocks, earlier)
+
+
+def branch_kernel(near_ref, far_ref, w_ref, _, near_out, far_out):
+    near_out[...] = dot_nt(near_ref[...], w_ref[...]).astype(BF16)
+    far_out[...] = dot_nt(far_ref[...], w_ref[...]).astype(BF16)
+
+
+def branch_call(act, w, earlier):
+    tokens, part = act.shape
+    width = w.shape[0]
+    block = 256
+    steps = tokens // 2 // block
+    shape = jax.ShapeDtypeStruct((tokens // 2, width), BF16)
+    return pl.pallas_call(
+        branch_kernel,
+        grid=(steps,),
+        in_specs=[
+            pl.BlockSpec((block, part), lambda i: (i, 0)),
+            pl.BlockSpec((block, part), lambda i: (i + steps, 0)),
+            pl.BlockSpec(w.shape, lambda i: (0, 0), pipeline_mode=pl.Buffered(1)),
+            pl.BlockSpec(memory_space=pl.ANY),
+        ],
+        out_specs=[pl.BlockSpec((block, width), lambda i: (i, 0))] * 2,
+        out_shape=[shape, shape],
+        compiler_params=pltpu.CompilerParams(vmem_limit_bytes=VMEM),
+        cost_estimate=pl.CostEstimate(
+            flops=2 * tokens * width * part, bytes_accessed=2 * tokens * width, transcendentals=0
+        ),
+        name="branch",
+    )(act, act, w, earlier)
+
+
+def out_grad_kernel(me, near_ref, far_ref, right_ref, _, near_out, far_out):
+    near_out[...] = dot_tn(near_ref[...], right_ref[...]).astype(BF16)
+    far_out[...] = dot_tn(far_ref[...], right_ref[...]).astype(BF16)
+
+
+def out_grad_call(me, left, right, earlier):
+    seq = lax.axis_size("seq")
+    tokens, width = left.shape
+    block, cols = width // seq, right.shape[1]
+    shape = jax.ShapeDtypeStruct((width // 2, cols), BF16)
+    return pl.pallas_call(
+        out_grad_kernel,
+        grid_spec=pltpu.PrefetchScalarGridSpec(
+            num_scalar_prefetch=1,
+            grid=(seq // 2,),
+            in_specs=[
+                pl.BlockSpec((tokens, block), lambda i, me: (0, natural(i, me, seq))),
+                pl.BlockSpec((tokens, block), lambda i, me: (0, natural(i + seq // 2, me, seq))),
+                pl.BlockSpec(right.shape, lambda i, me: (0, 0)),
+                pl.BlockSpec(memory_space=pl.ANY),
+            ],
+            out_specs=[pl.BlockSpec((block, cols), lambda i, me: (i, 0))] * 2,
+        ),
+        out_shape=[shape, shape],
+        compiler_params=pltpu.CompilerParams(vmem_limit_bytes=VMEM),
+        cost_estimate=pl.CostEstimate(
+            flops=2 * tokens * width * cols, bytes_accessed=2 * width * cols, transcendentals=0
+        ),
+        name="out_grad",
+    )(me, left, left, right, earlier)
+
+
+def scatter_shapes(count, width):
+    return [
+        jax.ShapeDtypeStruct((count, width), F32),
+        jax.ShapeDtypeStruct((count, width), BF16),
+        jax.ShapeDtypeStruct((count, width), BF16),
+    ]
+
+
+def ffn_back_call(near, far, gate_up, gu, down, count, earlier):
+    width, part = down.shape
+    half = count // 2
+    there = pl.BlockSpec(memory_space=pl.ANY)
+    own, from_x, from_y, d_gu = pl.pallas_call(
+        ffn_back_kernel,
+        in_specs=[there] * 6,
+        out_specs=[there] * 4,
+        out_shape=scatter_shapes(count, width) + [jax.ShapeDtypeStruct(gate_up.shape, BF16)],
+        scratch_shapes=[
+            pltpu.VMEM(gu.shape, BF16),
+            pltpu.VMEM(down.shape, BF16),
+            pltpu.VMEM((2, half, width), BF16),
+            pltpu.VMEM((2, half, 2 * part), BF16),
+            pltpu.VMEM((2, half, 2 * part), BF16),
+            pltpu.VMEM((half, width), F32),
+        ]
+        + PlaneScatter.scratch(half, width)
+        + [
+            pltpu.SemaphoreType.DMA((2,)),
+            pltpu.SemaphoreType.DMA((2, 2)),
+            pltpu.SemaphoreType.DMA((2,)),
+        ],
+        compiler_params=pltpu.CompilerParams(
+            collective_id=3, has_side_effects=True, vmem_limit_bytes=VMEM
+        ),
+        cost_estimate=pl.CostEstimate(
+            flops=8 * gate_up.shape[0] * width * part, bytes_accessed=gate_up.shape[0] * width * 8, transcendentals=0
+        ),
+        name="ffn_back",
+    )(near, far, gate_up, gu, down, earlier)
+    return own + from_x.astype(F32) + from_y.astype(F32), d_gu
+
+
+def project_back_kernel(
+    d_ref, w_ref, gain_ref, blocks_ref, own, from_x, from_y, gain_out, blocks_out,
+    gain_sum, gain_from, gain_send, gain_recv, block_send, block_recv, block_local,
+    total, odd, even, held, other, diagonal, odd_send, odd_recv, send, recv, keep,
+):
+    scatter = PlaneScatter(
+        own, from_x, from_y, odd, even, held, other, diagonal, (odd_send, odd_recv, send, recv, keep)
+    )
+    half = scatter.half
+    blocks = PlaneExchange(
+        lambda i: blocks_ref.at[i], blocks_out, block_send, block_recv, block_local
+    )
+    partners = [(scatter.to[device], scatter.rows) for device in ("core", "x", "y")]
+    size = lax.axis_size("rows")
+    mask = 1
+    others = []
+    while mask < size:
+        others.append((scatter.seq, flipped(scatter.rows, mask, size)))
+        mask *= 2
+    partners = partners + others
+    greet(blocks.peers() + others)
+    gain_sum[0] = gain_ref[...]
+
+    def exchange(i):
+        return remote(
+            gain_sum.at[i], gain_from.at[i], partners[i], gain_send.at[i], gain_recv.at[i]
+        )
+
+    def add_gains(i):
+        exchange(i).wait_recv()
+        gain_sum[i + 1] = gain_sum[i] + gain_from[i]
+
+    def body(unit, carry):
+        for i in range(len(partners)):
+            at_unit(unit, 2 * i + 1, exchange(i).start)
+            at_unit(unit, 2 * i + 2, partial(add_gains, i))
+        at_unit(unit, 8, blocks.start)
+        pair, side = lax.div(unit, 2), 1 - lax.rem(unit, 2)
+        begin = pl.multiple_of((PlaneScatter.place(pair) + 8 * side) * half, half)
+        total[...] = dot_nt(d_ref[pl.ds(begin, half), :], w_ref[...])
+
+        @pl.when(side == 1)
+        def _():
+            scatter.give_odd(pair, total[...])
+
+        @pl.when(side == 0)
+        def _():
+            scatter.give_even(pair, total)
+
+        return carry
+
+    lax.fori_loop(0, 16, body, 0)
+    gain_out[...] = gain_sum[len(partners)]
+    blocks.finish()
+    for i in range(len(partners)):
+        exchange(i).wait_send()
+    scatter.finish()
+
+
+def project_back_call(d, w, gains, blocks, count):
+    width = w.shape[0]
+    half = count // 2
+    here, there = pl.BlockSpec(memory_space=pltpu.VMEM), pl.BlockSpec(memory_space=pl.ANY)
+    rounds = 3 + (lax.axis_size("rows") - 1).bit_length()
+    own, from_x, from_y, gains, blocks = pl.pallas_call(
+        project_back_kernel,
+        in_specs=[here] * 3 + [there],
+        out_specs=[there] * 3 + [here, there],
+        out_shape=scatter_shapes(count, width) + [
+            jax.ShapeDtypeStruct(gains.shape, F32),
+            jax.ShapeDtypeStruct(blocks.shape, BF16),
+        ],
+        scratch_shapes=[
+            pltpu.VMEM((rounds + 1,) + gains.shape, F32),
+            pltpu.VMEM((rounds,) + gains.shape, F32),
+            pltpu.SemaphoreType.DMA((rounds,)),
+            pltpu.SemaphoreType.DMA((rounds,)),
+        ]
+        + PlaneExchange.scratch()
+        + [
+            pltpu.VMEM((half, width), F32),
+        ]
+        + PlaneScatter.scratch(half, width),
+        compiler_params=pltpu.CompilerParams(
+            collective_id=4, has_side_effects=True, vmem_limit_bytes=VMEM
+        ),
+        cost_estimate=pl.CostEstimate(
+            flops=16 * d.shape[0] * width * w.shape[1], bytes_accessed=d.shape[0] * width * 8, transcendentals=0
+        ),
+        name="project_back",
+    )(d, w, gains, blocks)
+    return own + from_x.astype(F32) + from_y.astype(F32), gains, blocks
+
+
 def ffn_kernel(hidden_ref, grad_ref, gu_ref, down_ref, act_ref, dgu_ref):
     part = down_ref.shape[1]
-    hidden = hidden_ref[...]
-    gate = dot_nn(hidden, gu_ref[:, :part])
-    up = dot_nn(hidden, gu_ref[:, part:])
-    d_act = dot_nn(grad_ref[...], down_ref[...])
-    sigmoid = 1.0 / (1.0 + jnp.exp(-gate))
-    silu = gate * sigmoid
-    act_ref[...] = (silu * up).astype(BF16)
-    dgu_ref[:, :part] = (d_act * up * (sigmoid + silu * (1.0 - sigmoid))).astype(BF16)
-    dgu_ref[:, part:] = (d_act * silu).astype(BF16)
+    gate, up, act = gate_and_up(hidden_ref[...], gu_ref)
+    d_gate, d_up = gate_and_up_back(gate, up, dot_nn(grad_ref[...], down_ref[...]))
+    act_ref[...] = act
+    dgu_ref[:, :part] = d_gate
+    dgu_ref[:, part:] = d_up
 
 
 def ffn_call(hidden, grad, gu, down):
@@ -487,8 +1483,11 @@
 
 
 def scatter_z(grad):
-    grad = grad.reshape(lax.axis_size("seq"), -1, grad.shape[-1])
-    return lax.psum_scatter(grad, "rows", scatter_dimension=1, tiled=True)
+    parts, lines, cols = grad.shape
+    grad = lax.psum_scatter(
+        grad.reshape(parts * lines, cols), "rows", scatter_dimension=0, tiled=True
+    )
+    return grad.reshape(lax.axis_size("seq"), -1, cols)
 
 
 def shards(
@@ -526,12 +1525,11 @@
         axis=2,
     ).transpose(1, 0, 2)
     qkv_mine = gather_z(all_to_all(qkv_blocks))
-    out_full = lax.all_gather(out_weight, ("seq", "rows"), axis=0, tiled=True)
+    out_block = lax.all_gather(out_weight, "rows", axis=0, tiled=True)
     gu_scaled = (gate_up_weight.astype(F32) * gains[1][:, None]).astype(BF16)
     gu_blocks = gu_scaled.reshape(depth, 2, seq, part).transpose(2, 0, 1, 3)
     gu_mine = gather_z(all_to_all(gu_blocks.reshape(seq, depth, 2 * part)))
     down_blocks = down_weight.reshape(depth, seq, part).transpose(1, 0, 2)
-    down_mine = gather_z(all_to_all(down_blocks))
 
     lane = jnp.arange(128) % HEAD
     frequency = jnp.exp(
@@ -545,25 +1543,37 @@
 
     inputs = tokens.reshape(count, width).astype(F32)
     r0 = lax.rsqrt(jnp.mean(inputs * inputs, axis=-1, keepdims=True) + EPSILON)
-    unit0 = gather_plane((inputs * r0).astype(BF16))
-    raw, q, kv = qkv_call(me, unit0, qkv_mine, cos, sin, head_gains, rows, slots)
+    unit0 = (inputs * r0).astype(BF16)
+    if seq == 8:
+        unit0, raw, q, kv = gather_qkv_call(unit0, qkv_mine, cos, sin, head_gains, rows, slots)
+    else:
+        unit0 = gather_plane(unit0)
+        raw, q, kv = qkv_call(me, unit0, qkv_mine, cos, sin, head_gains, rows, slots)
+    out_full = gather_natural(after(out_block, q))
+    down_mine = gather_z(after(all_to_all(down_blocks), q))
     attended_mine, attended_low, logs = attend_call(lengths, q, kv, slots)
     attended = all_to_all(attended_low).transpose(1, 2, 0, 3).reshape(count, kv_at)
     middle = inputs + dot_nt(attended, out_full)
     r1 = lax.rsqrt(jnp.mean(middle * middle, axis=-1, keepdims=True) + EPSILON)
 
     grad_low = cotangent.reshape(count, width)
-    grad_all = gather_plane(grad_low)
-    unit1 = gather_plane((middle * r1).astype(BF16))
-    act, d_gu = ffn_call(unit1, grad_all, gu_mine, down_mine)
+    unit1 = (middle * r1).astype(BF16)
     half = seq * count // 2
-    u_odd = dot_nt(d_gu[half:], gu_mine).astype(BF16)
-    u = scatter_plane(u_odd, dot_nt(d_gu[:half], gu_mine))
-    down_sum = scatter_z(dot_tn(grad_all, act).astype(BF16))
-    gu_sum = scatter_z(dot_tn(unit1, d_gu).astype(BF16))
-    branch_odd = dot_nt(act[half:], down_mine).astype(BF16)
-    branch = scatter_plane(branch_odd, dot_nt(act[:half], down_mine))
-    output = (middle + branch).astype(BF16).reshape(rows, slots, width)
+    if seq == 8:
+        unit1, near, far, gate_up, act = gather_ffn_call(
+            unit1, gather_pieces(grad_low, q), gu_mine
+        )
+        down_grad = weight_grad_call([near, far], act, corner(act), depth, "down_grad")
+        u, d_gu = ffn_back_call(near, far, gate_up, gu_mine, down_mine, count, corner(down_grad))
+    else:
+        grad_all = gather_plane(grad_low)
+        unit1 = gather_plane(unit1)
+        act, d_gu = ffn_call(unit1, grad_all, gu_mine, down_mine)
+        u_odd = dot_nt(d_gu[half:], gu_mine).astype(BF16)
+        u = scatter_plane(u_odd, dot_nt(d_gu[:half], gu_mine))
+        near, far = grad_all[:half], grad_all[half:]
+        down_grad = weight_grad_call([near, far], act, corner(act), depth, "down_grad")
+    down_sum = scatter_z(down_grad)
 
     d_middle = (
         grad_low.astype(F32)
@@ -572,17 +1582,48 @@
     )
     d_branch = d_middle.astype(BF16)
     d_attended = dot_nn(d_branch, out_full).astype(BF16)
-    d_attended = d_attended.reshape(rows, slots, seq, query_width).transpose(2, 0, 1, 3)
-    d_attended = all_to_all(d_attended)
-    out_sum = lax.psum_scatter(
-        dot_tn(d_branch, attended).astype(BF16), "seq", scatter_dimension=0, tiled=True
-    )
-    out_sum = lax.psum_scatter(out_sum, "rows", scatter_dimension=0, tiled=True)
-    dq, dkv = attend_back_call(lengths, q, kv, attended_mine, d_attended, logs)
+    branch_near, branch_far = branch_call(act, down_mine, corner(d_attended))
+    if seq == 8:
+        gu_grad, d_attended, down_sum = grad_exchange_call(
+            unit1, d_gu, d_attended, down_sum, corner(branch_near), depth
+        )
+        d_attended = d_attended.reshape(seq, rows, slots, query_width)
+    else:
+        gu_grad = weight_grad_call([unit1], d_gu, corner(branch_near), depth, "gate_up_grad")
+        d_attended = d_attended.reshape(rows, slots, seq, query_width).transpose(2, 0, 1, 3)
+        d_attended = all_to_all(d_attended)
+        down_sum = all_to_all(down_sum)
+    gu_sum = scatter_z(gu_grad)
+    features = width // seq
+    out_near, out_far = out_grad_call(me, d_branch, attended, corner(gu_grad))
+    chips = seq // 2
+    branch_all = (branch_near.astype(F32) + swap(branch_far, 1).astype(F32)).astype(BF16)
+    out_all = (out_near.astype(F32) + swap(out_far, 1).astype(F32)).astype(BF16)
+    branch_parts = [branch_all[i * count : (i + 1) * count] for i in range(chips)]
+    out_parts = [out_all[i * features : (i + 1) * features] for i in range(chips)]
+    ready = after(lengths, gu_grad, *branch_parts, *out_parts)
+    dq, dkv = attend_back_call(ready, q, kv, attended_mine, d_attended, logs)
     d_qkv, head_gain_grad = prepare_back_call(me, raw, dq, dkv, cos, sin, head_gains, slots)
-    u0_odd = dot_nt(d_qkv[half:], qkv_mine).astype(BF16)
-    u0 = scatter_plane(u0_odd, dot_nt(d_qkv[:half], qkv_mine))
-    qkv_sum = scatter_z(dot_tn(unit0, d_qkv).astype(BF16))
+    qkv_grad = weight_grad_call([unit0], d_qkv, corner(d_qkv), depth, "qkv_grad")
+    branch = scatter_direct(branch_parts, d_qkv)
+    output = (middle + branch).astype(BF16).reshape(rows, slots, width)
+    out_sum = scatter_direct(out_parts, d_qkv)
+    if seq == 8:
+        gain_rows = after(head_gain_grad, qkv_grad, output, out_sum)
+        gain_rows = jnp.broadcast_to(gain_rows, (8, gain_rows.shape[1]))
+        u0, head_gain_grad, gu_owned = project_back_call(
+            d_qkv, qkv_mine, gain_rows, gu_sum, count
+        )
+    else:
+        u0_odd = dot_nt(d_qkv[half:], qkv_mine).astype(BF16)
+        u0 = scatter_plane(u0_odd, dot_nt(d_qkv[:half], qkv_mine))
+        head_gain_grad = sum_everywhere(head_gain_grad)
+        gu_owned = all_to_all(gu_sum)
+    parts = lax.axis_size("rows")
+    out_blocks = after(out_sum, gu_sum).astype(BF16).reshape(parts, depth * seq, kv_at // seq)
+    attn_sum = scatter_z(jnp.concatenate([qkv_grad, out_blocks], axis=2))
+    qkv_sum = attn_sum[:, :, : query_width + 2 * HEAD]
+    out_sum = attn_sum[:, :, query_width + 2 * HEAD :].reshape(depth, kv_at)
     input_grad = (
         d_middle + r0 * u0 - inputs * (r0 * r0 * r0) * jnp.mean(u0 * inputs, axis=-1, keepdims=True)
     )
@@ -590,11 +1631,10 @@
     qk_grad = jnp.stack(
         [head_gain_grad[0, :query_width].reshape(group, HEAD).sum(0), head_gain_grad[0, query_width : query_width + HEAD]]
     )
-    qk_grad = lax.psum(qk_grad, ("seq", "rows"))
-
-    gu_sum = all_to_all(gu_sum).reshape(seq, depth, 2, part).transpose(1, 2, 0, 3)
+
+    gu_sum = gu_owned.reshape(seq, depth, 2, part).transpose(1, 2, 0, 3)
     gu_sum = gu_sum.reshape(depth, 2 * seq * part).astype(F32)
-    down_sum = all_to_all(down_sum).transpose(1, 0, 2).reshape(depth, seq * part).astype(F32)
+    down_sum = down_sum.transpose(1, 0, 2).reshape(depth, seq * part).astype(F32)
     qkv_sum = all_to_all(qkv_sum).transpose(1, 0, 2).astype(F32)
     kv_sum = qkv_sum[:, :, query_width:].reshape(depth, KEY_VALUE_HEADS, sharing, 2 * HEAD).sum(2)
     qkv_sum = jnp.concatenate(

time: 1300 us -> 984 us (0.76)
  Pallas kernels: 204 us -> 654 us
  waiting for transfers between devices: 477 us -> 49.3 us
  matrix products: 207 us -> 16 us
  blocking collectives: 176 us -> 13.4 us
  local copies, waits for them, and re-layouts: 98.3 us -> 118 us
  starting transfers between devices: 49.8 us -> 33.8 us
    pallas_call x2 -> x9, Pallas kernels: 83.3 us -> 532 us  [the longest x1 122 us: project_back_call(): pl.pallas_call(project_back_kernel, in_specs=[here] * 3 + [there], out_sp...]
    ppermute x39 -> x19, waiting for transfers between devices: 323 us -> 7.22 us  [swap(): lax.ppermute(block, 'seq', [(i, i ^ mask) for i in range(lax.axis_size('s...]
    psum x1 -> x0, blocking collectives: 133 us -> none  [shards(): qk_grad = lax.psum(qk_grad, ('seq', 'rows'))]
    reduce_scatter x5 -> x3, waiting for transfers between devices: 115 us -> 0.02 us  [scatter_z(): lax.psum_scatter(grad.reshape(parts * lines, cols), 'rows', scatter_dimen...]
    dot_general x7 -> x1, matrix products: 109 us -> 7.16 us  [dot_nt(): lax.dot_general(a, b, (((1,), (1,)), ((), ())), preferred_element_type=F3...]
    dot_general x4 -> x0, matrix products: 88.4 us -> none  [dot_tn(): lax.dot_general(a, b, (((0,), (0,)), ((), ())), preferred_element_type=F32)]
    all_to_all x2 -> x1, blocking collectives: 43.4 us -> 13.4 us  [all_to_all(): return lax.all_to_all(block, 'seq', 0, 0, tiled=True)]
    convert_element_type x0 -> x7, other arithmetic: none -> 26.8 us  [the longest x1 7.57 us: shards(): (branch_near.astype(F32) + swap(branch_far, 1).astype(F32)).astype(BF16)]
  transfers between devices with their start and end apart: 54 -> 30, of which waited for: 21 -> 4; matrix products, arithmetic and copies ran while one was open for 26% -> 18% of each run, Pallas kernels for 11% -> 67%
where the time goes in v2:
time: 984 us; the launch traced here: 973 us
  Pallas kernels  654 us (66%)
  local copies, waits for them, and re-layouts  118 us (12%)
  other arithmetic  64.7 us (7%)
  waiting for transfers between devices  49.3 us (5%)
  starting transfers between devices  33.8 us (3%)
  between operations  24.8 us (3%)
  matrix products  16 us (2%)
  blocking collectives  13.4 us (1%)
    pallas_call x1, Pallas kernels, project_back_call(): pl.pallas_call(project_back_kernel, in_specs=[here] * 3 + [there], out_sp...  122 us
    pallas_call x1, Pallas kernels, gather_qkv_call(): pl.pallas_call(gather_qkv_kernel, in_specs=[there, here, here, here, here...  119 us
    pallas_call x1, Pallas kernels, ffn_back_call(): pl.pallas_call(ffn_back_kernel, in_specs=[there] * 6, out_specs=[there] *...  92.4 us
    pallas_call x1, Pallas kernels, gather_ffn_call(): pl.pallas_call(gather_ffn_kernel, in_specs=[there] * 7, out_specs=[there]...  82.6 us
    pallas_call x1, Pallas kernels, attend_back_call(): pl.pallas_call(attend_back_kernel, grid_spec=pltpu.PrefetchScalarGridSpec...  67.8 us
    pallas_call x1, Pallas kernels, grad_exchange_call(): pl.pallas_call(grad_exchange_kernel, grid=(seq,), in_specs=[pl.BlockSpec(...  46.2 us
    unnamed x105, local copies, waits for them, and re-layouts  41.9 us
    all_to_all x4, waiting for transfers between devices, all_to_all(): return lax.all_to_all(block, 'seq', 0, 0, tiled=True)  41.2 us
  transfers between devices with their start and end apart: 30, of which 4 were waited for; matrix products, arithmetic and copies ran while one was open for 18% of the time, Pallas kernels for 67%

profile of v2, /device:TPU:0, one launch (start us, length us, event | category | flops | bytes accessed | tf_op | source)
XLA Modules:
  0.0 973.3 jit_solution(13444063393130028248)
XLA Ops:
  9.6 13.4 %all_to_all.25 = bf16[8,64,384]{2,1,0:T(8,128)(2,1)} all-to-all(bf16[8,64,384]{2,1,0:T(8,128)(2,1)S(1)} %maximum_bitcast_fusion), channel_id=1, replica_groups=mesh['seq'=8,'rows'=4] {'seq'}, dimensions={0} | all-to-all | bytes 786432 | tf_op jit(solution)/shard_map/all_to_all | solution.py:1477
  35.0 25.8 %all-to-all-done.2 = bf16[8,64,2048]{2,1,0:T(8,128)(2,1)} async-done(((bf16[8,64,2048]{2,1,0:T(8,128)(2,1)}), bf16[8,64,2048]{2,1,0:T(8,128)(2,1)}, u32[]{:S(2)}, u32[]{:S(2)}) %all-to-all-start.2) | async-done | bytes 2097184 | tf_op jit(solution)/shard_map/all_to_all | solution.py:1477
  75.7 118.6 %gather_qkv.1 = (bf16[4096,2048]{1,0:T(8,128)(2,1)}, f32[2,2048,384]{2,1,0:T(8,128)}, bf16[2,2048,256]{2,1,0:T(8,128)(2,1)}, bf16[2,2048,128]{2,1,0:T(8,128)(2,1)}) custom-call(bf16[512,2048]{1,0:T(8,128)(2,1)} %fusion.3.x_ref, bf16[2048,384]{1,0:T(8,128)(2,1)} %bitcast.182, f32[2048,128]{1,0:T(8,128)} %get-tuple-element.101.cos_ref, ...), custom_call_target="tpu_custom_call" | custom-call | flops 51539607552 | bytes 33554432 | tf_op jit(solution)/shard_map/gather_qkv/pallas_call | solution.py:756
  208.9 38.9 %attend.1 = (f32[2,2048,256]{2,1,0:T(8,128)}, bf16[8,2,256,256]{3,2,1,0:T(8,128)(2,1)}, f32[2,8,2048]{2,1,0:T(8,128)}) custom-call(s32[2]{0:T(128)} %lengths.1, bf16[2,2048,256]{2,1,0:T(8,128)(2,1)} %get-tuple-element.40.q_ref, bf16[2,2048,128]{2,1,0:T(8,128)(2,1)} %get-tuple-element.41.kv_ref), custom_call_target="tpu_custom_call" | custom-call | flops 34359738368 | bytes 8388608 | tf_op jit(solution)/shard_map/attend/pallas_call | solution.py:254
  270.1 9.6 all-to-all-done.1
  290.9 7.2 multiply_reduce_fusion.1
  301.7 82.6 %gather_ffn.1 = (bf16[4096,2048]{1,0:T(8,128)(2,1)}, bf16[2048,2048]{1,0:T(8,128)(2,1)}, bf16[2048,2048]{1,0:T(8,128)(2,1)}, bf16[4096,2048]{1,0:T(8,128)(2,1)}, bf16[4096,1024]{1,0:T(8,128)(2,1)}) custom-call(bf16[512,2048]{1,0:T(8,128)(2,1)} %multiply_convert_fusion.x_ref, bf16[512,2048]{1,0:T(8,128)(2,1)} %bitcast.146, ...), custom_call_target="tpu_custom_call" | custom-call | flops 68719476736 | bytes 67108864 | tf_op jit(solution)/shard_map/gather_ffn/pallas_call | solution.py:1017
  385.6 23.9 %down_grad.1 = bf16[4,512,1024]{2,1,0:T(8,128)(2,1)} custom-call(bf16[2048,2048]{1,0:T(8,128)(2,1)} %get-tuple-element.44.refs_0_.near_ref, bf16[2048,2048]{1,0:T(8,128)(2,1)} %get-tuple-element.45.refs_1_.far_ref, bf16[4096,1024]{1,0:T(8,128)(2,1)} %get-tuple-element.43.refs_2_.near_ref.far_ref, bf16[16,128]{1,0:T(8,128)(2,1)} %slice.158.refs_3_), custom_call_target="tpu_custom_call" | custom-call | flops 17179869184 | bytes 25165824 | tf_op jit(solution)/shard_map/down_grad/pallas_call | solution.py:1160
  411.2 92.4 %ffn_back.1 = (f32[512,2048]{1,0:T(8,128)}, bf16[512,2048]{1,0:T(8,128)(2,1)}, bf16[512,2048]{1,0:T(8,128)(2,1)}, bf16[4096,2048]{1,0:T(8,128)(2,1)}) custom-call(bf16[2048,2048]{1,0:T(8,128)(2,1)} %get-tuple-element.44.refs_0_.near_ref, bf16[2048,2048]{1,0:T(8,128)(2,1)} %get-tuple-element.45.refs_1_.far_ref, ...), custom_call_target="tpu_custom_call" | custom-call | flops 68719476736 | bytes 67108864 | tf_op jit(solution)/shard_map/ffn_back/pallas_call | solution.py:1317
  513.5 8.8 convolution_convert_fusion.spread_ref
  524.2 22.7 %branch.1 = (bf16[2048,2048]{1,0:T(8,128)(2,1)}, bf16[2048,2048]{1,0:T(8,128)(2,1)}) custom-call(bf16[4096,1024]{1,0:T(8,128)(2,1)} %get-tuple-element.43.refs_2_.near_ref.far_ref, bf16[4096,1024]{1,0:T(8,128)(2,1)} %get-tuple-element.43.refs_2_.near_ref.far_ref, bf16[2048,1024]{1,0:T(8,128)(2,1)} %bitcast.181, bf16[16,128]{1,0:T(8,128)(2,1)} %slice.201._), custom_call_target="tpu_custom_call" | custom-call | flops 17179869184 | bytes 16777216 | tf_op jit(solution)/shard_map/branch/pallas_call | solution.py:1254
  548.3 46.2 %gate_up_grad.1 = (bf16[4,512,2048]{2,1,0:T(8,128)(2,1)}, bf16[8,512,256]{2,1,0:T(8,128)(2,1)}, bf16[8,64,1024]{2,1,0:T(8,128)(2,1)}) custom-call(bf16[4096,2048]{1,0:T(8,128)(2,1)} %get-tuple-element.53.left_ref, bf16[4096,2048]{1,0:T(8,128)(2,1)} %get-tuple-element.54.right_ref, bf16[512,2048]{1,0:T(8,128)(2,1)} %copy-done.39, ...), custom_call_target="tpu_custom_call" | custom-call | flops 34359738368 | bytes 33554432 | tf_op jit(solution)/shard_map/gate_up_grad/pallas_call | solution.py:1214
  595.9 8.3 out_grad.1
  606.5 9.9 %copy.48 = bf16[256,16,8,128]{3,1,2,0:T(8,128)(2,1)} copy(bf16[256,16,8,128]{3,2,1,0:T(8,128)(2,1)} %bitcast.130) | data formatting | bytes 16777216
  617.6 7.6 add_convert_fusion
  655.1 67.8 %attend_back.1 = (f32[2,2048,256]{2,1,0:T(8,128)}, f32[2,2048,128]{2,1,0:T(8,128)}) custom-call(s32[2]{0:T(128)} %broadcast_add_fusion.2.lengths, bf16[2,2048,256]{2,1,0:T(8,128)(2,1)} %get-tuple-element.40.q_ref, bf16[2,2048,128]{2,1,0:T(8,128)(2,1)} %get-tuple-element.41.kv_ref, f32[2,2048,256]{2,1,0:T(8,128)} %get-tuple-element.58.out_ref, ...), custom_call_target="tpu_custom_call" | custom-call | flops 60129542144 | bytes 14680064 | tf_op jit(solution)/shard_map/attend_back/pallas_call | solution.py:390
  722.9 15.3 %prepare_back.1 = (bf16[4096,384]{1,0:T(8,128)(2,1)}, f32[1,384]{1,0:T(1,128)}) custom-call(s32[1]{0:T(128)} %bitcast.17.me, f32[2,2048,384]{2,1,0:T(8,128)} %get-tuple-element.52.raw_ref, f32[2,2048,256]{2,1,0:T(8,128)} %get-tuple-element.61.dq_ref, f32[2,2048,128]{2,1,0:T(8,128)} %get-tuple-element.62.dkv_ref, f32[2048,128]{1,0:T(8,128)} %get-tuple-element.101.cos_ref, ...), custom_call_target="tpu_custom_call" | custom-call | tf_op jit(solution)/shard_map/prepare_back/pallas_call | solution.py:457
  740.8 14.9 %qkv_grad.1 = bf16[4,512,384]{2,1,0:T(8,128)(2,1)} custom-call(bf16[4096,2048]{1,0:T(8,128)(2,1)} %get-tuple-element.65.refs_0_, bf16[4096,384]{1,0:T(8,128)(2,1)} %get-tuple-element.63.refs_1_.d_ref, bf16[16,128]{1,0:T(8,128)(2,1)} %slice.181.refs_2_), custom_call_target="tpu_custom_call" | custom-call | flops 6442450944 | bytes 19922944 | tf_op jit(solution)/shard_map/qkv_grad/pallas_call | solution.py:1160
  755.8 6.4 reshape.284
  765.3 6.7 add_convert_fusion.2
  779.1 7.2 collective-permute-done.17
  797.2 122.0 %project_back.1 = (f32[512,2048]{1,0:T(8,128)}, bf16[512,2048]{1,0:T(8,128)(2,1)}, bf16[512,2048]{1,0:T(8,128)(2,1)}, f32[8,384]{1,0:T(8,128)}, bf16[8,64,2048]{2,1,0:T(8,128)(2,1)}) custom-call(bf16[4096,384]{1,0:T(8,128)(2,1)} %get-tuple-element.63.refs_1_.d_ref, bf16[2048,384]{1,0:T(8,128)(2,1)} %bitcast.183, f32[8,384]{1,0:T(8,128)} %broadcast_in_dim.41.gain_ref, ...), custom_call_target="tpu_custom_call" | custom-call | flops 51539607552 | bytes 67108864 | tf_op jit(solution)/shard_map/project_back/pallas_call | solution.py:1411
  920.7 6.7 reshape.305
  957.8 5.8 all-to-all-done.4
  (268 shorter events, 179.9 us)
Async XLA Ops:
  7.2 68.5 %all-gather.5.cloned.1.call-start = ((), (), s32[]{:S(2)}) async-start(), calls=%async_computation.8 | async-start | bytes 1966080 | tf_op jit(solution)/shard_map/all_gather | solution.py:1481
  34.2 165.1 %all-gather.7.cloned.1.call-start = ((), (), s32[]{:S(2)}) async-start(), calls=%async_computation.9 | async-start | bytes 1310720 | tf_op jit(solution)/shard_map/all_gather | solution.py:1528
  35.0 266.7 %all-gather.9.cloned.1.call-start = ((), (), s32[]{:S(2)}) async-start(), calls=%async_computation.10 | async-start | bytes 10485760 | tf_op jit(solution)/shard_map/all_gather | solution.py:1481
  60.9 195.0 %collective-permute-start.8 = (bf16[512,2048]{1,0:T(8,128)(2,1)}, bf16[512,2048]{1,0:T(8,128)(2,1)}, u32[]{:S(2)}, u32[]{:S(2)}) collective-permute-start(bf16[512,2048]{1,0:T(8,128)(2,1)} %bitcast.144), channel_id=1, source_target_pairs={{0,16},{4,20},{8,24},{12,28},{16,0},{20,4},{24,8},{28,12},{1,17},{... | collective-permute-start | bytes 6291464 | tf_op jit(solution)/shard_map/ppermute | solution.py:24
  61.5 192.3 %collective-permute-start.7 = (bf16[512,2048]{1,0:T(8,128)(2,1)}, bf16[512,2048]{1,0:T(8,128)(2,1)}, u32[]{:S(2)}, u32[]{:S(2)}) collective-permute-start(bf16[512,2048]{1,0:T(8,128)(2,1)} %bitcast.145), channel_id=1, source_target_pairs={{0,8},{4,12},{8,0},{12,4},{16,24},{20,28},{24,16},{28,20},{1,9},{5... | collective-permute-start | bytes 6291464 | tf_op jit(solution)/shard_map/ppermute | solution.py:24
  63.2 184.7 %all-to-all-start.3 = ((bf16[8,64,1024]{2,1,0:T(8,128)(2,1)}), bf16[8,64,1024]{2,1,0:T(8,128)(2,1)S(1)}, u32[]{:S(2)}, u32[]{:S(2)}) async-start(bf16[8,64,1024]{2,1,0:T(8,128)(2,1)} %bitcast.143), calls=%async_computation.3 | async-start | bytes 2097152 | tf_op jit(solution)/shard_map/all_to_all | solution.py:1477
  205.3 54.5 %collective-permute-start.2 = (bf16[256,2048]{1,0:T(8,128)(2,1)}, bf16[256,2048]{1,0:T(8,128)(2,1)}, u32[]{:S(2)}, u32[]{:S(2)}) collective-permute-start(bf16[256,2048]{1,0:T(8,128)(2,1)} %get-tuple-element.75), channel_id=1, source_target_pairs={{0,24},{4,28},{8,16},{12,20},{16,8},{20,12},{24,0},{28,4},{1,25},{... | collective-permute-start | bytes 3145736 | tf_op jit(solution)/shard_map/ppermute | solution.py:24
  208.4 51.9 %collective-permute-start.1 = (bf16[256,2048]{1,0:T(8,128)(2,1)}, bf16[256,2048]{1,0:T(8,128)(2,1)}, u32[]{:S(2)}, u32[]{:S(2)}) collective-permute-start(bf16[256,2048]{1,0:T(8,128)(2,1)} %get-tuple-element.75), channel_id=1, source_target_pairs={{0,16},{4,20},{8,24},{12,28},{16,0},{20,4},{24,8},{28,12},{1,17},{... | collective-permute-start | bytes 3145736 | tf_op jit(solution)/shard_map/ppermute | solution.py:24
  208.5 49.0 %collective-permute-start = (bf16[256,2048]{1,0:T(8,128)(2,1)}, bf16[256,2048]{1,0:T(8,128)(2,1)}, u32[]{:S(2)}, u32[]{:S(2)}) collective-permute-start(bf16[256,2048]{1,0:T(8,128)(2,1)} %get-tuple-element.75), channel_id=1, source_target_pairs={{0,8},{4,12},{8,0},{12,4},{16,24},{20,28},{24,16},{28,20},{1,9},{5... | collective-permute-start | bytes 3145736 | tf_op jit(solution)/shard_map/ppermute | solution.py:24
  247.8 31.8 %all-to-all-start.1 = ((bf16[8,2,256,256]{3,2,1,0:T(8,128)(2,1)}), bf16[8,2,256,256]{3,2,1,0:T(8,128)(2,1)}, u32[]{:S(2)}, u32[]{:S(2)}) async-start(bf16[8,2,256,256]{3,2,1,0:T(8,128)(2,1)} %get-tuple-element.42), calls=%async_computation.1 | async-start | bytes 4194304 | tf_op jit(solution)/shard_map/all_to_all | solution.py:1477
  252.3 158.9 %all-gather.11.cloned.1.call-start = ((), (), s32[]{:S(2)}) async-start(), calls=%async_computation.11 | async-start | bytes 5242880 | tf_op jit(solution)/shard_map/all_gather | solution.py:1481
  253.5 294.8 %reduce-scatter.4.cloned.1.call-start = ((), (), s32[]{:S(2)}) async-start(), calls=%async_computation.12 | async-start | bytes 5242880 | tf_op jit(solution)/shard_map/reduce_scatter | solution.py:1487
  255.9 45.7 %collective-permute-start.10 = (bf16[256,2048]{1,0:T(8,128)(2,1)S(1)}, bf16[256,2048]{1,0:T(8,128)(2,1)}, u32[]{:S(2)}, u32[]{:S(2)}) collective-permute-start(bf16[256,2048]{1,0:T(8,128)(2,1)S(1)} %slice_add_fusion), channel_id=1, source_target_pairs={{0,16},{4,20},{8,24},{12,28},{16,0},{20,4},{24,8},{28,12},{1,17},{... | collective-permute-start | bytes 3145736 | tf_op jit(solution)/shard_map/ppermute | solution.py:24
  267.4 34.3 %collective-permute-start.9 = (bf16[256,2048]{1,0:T(8,128)(2,1)}, bf16[256,2048]{1,0:T(8,128)(2,1)}, u32[]{:S(2)}, u32[]{:S(2)}) collective-permute-start(bf16[256,2048]{1,0:T(8,128)(2,1)} %slice_add_fusion.1), channel_id=1, source_target_pairs={{0,8},{4,12},{8,0},{12,4},{16,24},{20,28},{24,16},{28,20},{1,9},{5... | collective-permute-start | bytes 3145736 | tf_op jit(solution)/shard_map/ppermute | solution.py:24
  410.7 365.0 %reduce-scatter.6.cloned.1.call-start = ((), (), s32[]{:S(2)}) async-start(), calls=%async_computation.13 | async-start | bytes 10485760 | tf_op jit(solution)/shard_map/reduce_scatter | solution.py:1487
  548.2 69.4 %collective-permute-start.11 = (bf16[2048,2048]{1,0:T(8,128)(2,1)}, bf16[2048,2048]{1,0:T(8,128)(2,1)}, u32[]{:S(2)}, u32[]{:S(2)}) collective-permute-start(bf16[2048,2048]{1,0:T(8,128)(2,1)} %get-tuple-element.51), channel_id=1, source_target_pairs={{0,4},{4,0},{8,12},{12,8},{16,20},{20,16},{24,28},{28,24},{1,5},{5... | collective-permute-start | bytes 25165832 | tf_op jit(solution)/shard_map/ppermute | solution.py:24
  594.6 355.6 %reduce-scatter.8.cloned.1.call-start = ((), (), s32[]{:S(2)}) async-start(), calls=%async_computation.14 | async-start | bytes 3276800 | tf_op jit(solution)/shard_map/reduce_scatter | solution.py:1487
  604.1 37.5 %collective-permute-start.12 = (bf16[1024,2048]{1,0:T(8,128)(2,1)}, bf16[1024,2048]{1,0:T(8,128)(2,1)S(1)}, u32[]{:S(2)}, u32[]{:S(2)}) collective-permute-start(bf16[1024,2048]{1,0:T(8,128)(2,1)} %get-tuple-element.57), channel_id=1, source_target_pairs={{0,4},{4,0},{8,12},{12,8},{16,20},{20,16},{24,28},{28,24},{1,5},{5... | collective-permute-start | bytes 12582920 | tf_op jit(solution)/shard_map/ppermute | solution.py:24
  635.1 104.4 %collective-permute-start.15 = (bf16[512,2048]{1,0:T(8,128)(2,1)}, bf16[512,2048]{1,0:T(8,128)(2,1)S(1)}, u32[]{:S(2)}, u32[]{:S(2)}) collective-permute-start(bf16[512,2048]{1,0:T(8,128)(2,1)} %get-tuple-element.80), channel_id=1, source_target_pairs={{0,24},{4,28},{8,16},{12,20},{16,8},{20,12},{24,0},{28,4},{1,25},{... | collective-permute-start | bytes 6291464 | tf_op jit(solution)/shard_map/ppermute | solution.py:24
  636.9 128.3 %collective-permute-start.14 = (bf16[512,2048]{1,0:T(8,128)(2,1)}, bf16[512,2048]{1,0:T(8,128)(2,1)}, u32[]{:S(2)}, u32[]{:S(2)}) collective-permute-start(bf16[512,2048]{1,0:T(8,128)(2,1)} %get-tuple-element.81), channel_id=1, source_target_pairs={{0,16},{4,20},{8,24},{12,28},{16,0},{20,4},{24,8},{28,12},{1,17},{... | collective-permute-start | bytes 6291464 | tf_op jit(solution)/shard_map/ppermute | solution.py:24
  637.6 127.7 %collective-permute-start.13 = (bf16[512,2048]{1,0:T(8,128)(2,1)}, bf16[512,2048]{1,0:T(8,128)(2,1)}, u32[]{:S(2)}, u32[]{:S(2)}) collective-permute-start(bf16[512,2048]{1,0:T(8,128)(2,1)} %get-tuple-element.82), channel_id=1, source_target_pairs={{0,8},{4,12},{8,0},{12,4},{16,24},{20,28},{24,16},{28,20},{1,9},{5... | collective-permute-start | bytes 6291464 | tf_op jit(solution)/shard_map/ppermute | solution.py:24
  649.6 129.5 %collective-permute-start.16 = (bf16[256,2048]{1,0:T(8,128)(2,1)}, bf16[256,2048]{1,0:T(8,128)(2,1)}, u32[]{:S(2)}, u32[]{:S(2)}) collective-permute-start(bf16[256,2048]{1,0:T(8,128)(2,1)} %get-tuple-element.87), channel_id=1, source_target_pairs={{0,8},{4,12},{8,0},{12,4},{16,24},{20,28},{24,16},{28,20},{1,9},{5... | collective-permute-start | bytes 3145736 | tf_op jit(solution)/shard_map/ppermute | solution.py:24
  650.7 128.5 %collective-permute-start.18 = (bf16[256,2048]{1,0:T(8,128)(2,1)}, bf16[256,2048]{1,0:T(8,128)(2,1)}, u32[]{:S(2)}, u32[]{:S(2)}) collective-permute-start(bf16[256,2048]{1,0:T(8,128)(2,1)} %get-tuple-element.91), channel_id=1, source_target_pairs={{0,24},{4,28},{8,16},{12,20},{16,8},{20,12},{24,0},{28,4},{1,25},{... | collective-permute-start | bytes 3145736 | tf_op jit(solution)/shard_map/ppermute | solution.py:24
  739.5 46.8 %collective-permute-start.17 = (bf16[256,2048]{1,0:T(8,128)(2,1)}, bf16[256,2048]{1,0:T(8,128)(2,1)}, u32[]{:S(2)}, u32[]{:S(2)}) collective-permute-start(bf16[256,2048]{1,0:T(8,128)(2,1)} %get-tuple-element.92), channel_id=1, source_target_pairs={{0,16},{4,20},{8,24},{12,28},{16,0},{20,4},{24,8},{28,12},{1,17},{... | collective-permute-start | bytes 3145736 | tf_op jit(solution)/shard_map/ppermute | solution.py:24
  (48 other events, 681.1 us)
Sparse Core Ops, SparseCore 0:
  23.2 36.4 all-gather.4
  61.3 26.7 all-gather.6
  89.7 149.1 all-gather.8
  254.4 87.2 all-gather.10
  410.9 82.0 reduce-scatter.3
  594.7 149.2 reduce-scatter.5
  795.2 63.7 reduce-scatter.7

commit v3 on v2

--- a/solution.py
+++ b/solution.py
@@ -46,13 +46,8 @@
     return lax.dot_general(a, b, (((0,), (0,)), ((), ())), preferred_element_type=F32)
 
 
-def corner(result):
-    flat = result.reshape(-1, result.shape[-1])
-    return flat[:16, :128]
-
-
 def after(value, *results):
-    zero = sum(result.reshape(-1)[0].astype(F32) for result in results) * 0.0
+    zero = sum(result[(0,) * result.ndim].astype(F32) for result in results) * 0.0
     return value + zero.astype(value.dtype)
 
 
@@ -96,13 +91,6 @@
             parts[i] + swap(parts[kept + i].astype(BF16), mask).astype(F32) for i in range(kept)
         ]
     return parts[0]
-
-
-def scatter_direct(parts, earlier):
-    total = after(parts[0].astype(F32), earlier)
-    for i in range(1, len(parts)):
-        total = total + swap(parts[i].astype(BF16), 2 * i).astype(F32)
-    return total
 
 
 def scatter_plane(odd, even, scatter=scatter_chips):
@@ -285,8 +273,9 @@
 
 
 def attend_back_kernel(
-    lengths, q_ref, kv_ref, out_ref, grad_ref, log_ref, dq_ref, dkv_ref, delta, dqt, kacc, vacc
+    lengths, q_ref, kv_ref, out_ref, grad_ref, log_ref, *refs
 ):
+    dq_ref, dkv_ref, delta, dqt, kacc, vacc = refs[-6:]
     row, step = pl.program_id(0), pl.program_id(1)
     block = kv_ref.shape[1]
     count = q_ref.shape[1] // block
@@ -384,7 +373,7 @@
                 )
 
 
-def attend_back_call(lengths, q, kv, attended, grads, logs):
+def attend_back_call(lengths, q, kv, attended, grads, logs, earlier):
     rows, total, width = q.shape
     seq, block = grads.shape[0], grads.shape[2]
     return pl.pallas_call(
@@ -398,7 +387,8 @@
                 pl.BlockSpec((1, total, width), lambda r, i, n: (r, 0, 0)),
                 pl.BlockSpec((seq, 1, block, width), lambda r, i, n: (0, r, 0, 0)),
                 pl.BlockSpec((1, 8, total), lambda r, i, n: (r, 0, 0)),
-            ],
+            ]
+            + [pl.BlockSpec(memory_space=pl.ANY)] * len(earlier),
             out_specs=[
                 pl.BlockSpec((1, total, width), lambda r, i, n: (r, 0, 0)),
                 pl.BlockSpec((1, block, 128), lambda r, i, n: (r, i, 0)),
@@ -419,11 +409,11 @@
             flops=rows * total * total * width * 28, bytes_accessed=rows * total * width * 14, transcendentals=0
         ),
         name="attend_back",
-    )(lengths, q, kv, attended, grads, logs)
+    )(lengths, q, kv, attended, grads, logs, *earlier)
 
 
 def prepare_back_kernel(
-    me, raw_ref, dq_ref, dkv_ref, cos_ref, sin_ref, gain_ref, out_ref, gain_grad_ref
+    me, raw_ref, dq_ref, dkv_ref, cos_ref, sin_ref, gain_ref, _, out_ref, gain_grad_ref
 ):
     rows, slots = dq_ref.shape[0], dq_ref.shape[1]
     cos, sin = cos_ref[...], sin_ref[...]
@@ -451,7 +441,7 @@
             out_ref[r * slots : (r + 1) * slots, lanes] = result.astype(BF16)
 
 
-def prepare_back_call(me, raw, dq, dkv, cos, sin, gains, slots):
+def prepare_back_call(me, raw, dq, dkv, cos, sin, gains, slots, earlier):
     rows, total, width = raw.shape
     seq = total // slots
     return pl.pallas_call(
@@ -466,6 +456,7 @@
                 pl.BlockSpec((slots, 128), lambda i, me: (natural(i, me, seq), 0)),
                 pl.BlockSpec((slots, 128), lambda i, me: (natural(i, me, seq), 0)),
                 pl.BlockSpec((1, width), lambda i, me: (0, 0)),
+                pl.BlockSpec(memory_space=pl.ANY),
             ],
             out_specs=[
                 pl.BlockSpec((rows * slots, width), lambda i, me: (i, 0)),
@@ -478,7 +469,7 @@
         ],
         compiler_params=pltpu.CompilerParams(vmem_limit_bytes=VMEM),
         name="prepare_back",
-    )(me, raw, dq, dkv, cos, sin, gains)
+    )(me, raw, dq, dkv, cos, sin, gains, earlier)
 
 
 def neighbours(me):
@@ -1177,22 +1168,22 @@
     )(*lefts, right, earlier)
 
 
-def grad_exchange_kernel(
-    left_ref, right_ref, spread_ref, blocks_ref, _, out_ref, spread_out, blocks_out, *sems
+def grad_send_kernel(
+    left_ref, right_ref, to_x, to_y, out_ref, from_x, from_y, send, recv
 ):
-    width = spread_out.shape[2]
-
-    def columns(i):
-        return spread_ref.at[:, pl.ds(pl.multiple_of(i * width, width), width)]
-
-    spread = PlaneExchange(columns, spread_out, *sems[:3])
-    blocks = PlaneExchange(lambda i: blocks_ref.at[i], blocks_out, *sems[3:])
+    seq, rows = lax.axis_index("seq"), lax.axis_index("rows")
+    to = neighbours(seq)
+    lines = pl.ds(0, from_x.shape[0])
+    copies = [
+        remote(source.at[lines], target, (to[device], rows), send.at[i], recv.at[i])
+        for i, (source, target, device) in enumerate(((to_x, from_x, "x"), (to_y, from_y, "y")))
+    ]
 
     @pl.when(pl.program_id(0) == 0)
     def _():
-        greet(spread.peers())
-        spread.start()
-        blocks.start()
+        greet([(to["x"], rows), (to["y"], rows)])
+        for copy in copies:
+            copy.start()
 
     depth = out_ref.shape[1]
     grad = dot_tn(left_ref[...], right_ref[...])
@@ -1201,33 +1192,28 @@
 
     @pl.when(pl.program_id(0) == pl.num_programs(0) - 1)
     def _():
-        spread.finish()
-        blocks.finish()
-
-
-def grad_exchange_call(left, right, spread, blocks, earlier, depth):
+        for copy in copies:
+            copy.wait()
+
+
+def grad_send_call(left, right, to_x, to_y, count, depth):
     seq, parts = lax.axis_size("seq"), lax.axis_size("rows")
     tokens, cols = right.shape
     width = left.shape[1]
-    block = width // seq
     there = pl.BlockSpec(memory_space=pl.ANY)
+    lines = jax.ShapeDtypeStruct((count, to_x.shape[1]), BF16)
     return pl.pallas_call(
-        grad_exchange_kernel,
+        grad_send_kernel,
         grid=(seq,),
         in_specs=[
-            pl.BlockSpec((tokens, block), lambda i: (0, i)),
+            pl.BlockSpec((tokens, width // seq), lambda i: (0, i)),
             pl.BlockSpec(right.shape, lambda i: (0, 0), pipeline_mode=pl.Buffered(1)),
             there,
             there,
-            there,
         ],
         out_specs=[pl.BlockSpec((parts, depth, cols), lambda i: (0, i, 0)), there, there],
-        out_shape=[
-            jax.ShapeDtypeStruct((parts, seq * depth, cols), BF16),
-            jax.ShapeDtypeStruct((seq, spread.shape[0], spread.shape[1] // seq), BF16),
-            jax.ShapeDtypeStruct(blocks.shape, BF16),
-        ],
-        scratch_shapes=PlaneExchange.scratch() + PlaneExchange.scratch(),
+        out_shape=[jax.ShapeDtypeStruct((parts, seq * depth, cols), BF16), lines, lines],
+        scratch_shapes=[pltpu.SemaphoreType.DMA((2,)), pltpu.SemaphoreType.DMA((2,))],
         compiler_params=pltpu.CompilerParams(
             collective_id=5, has_side_effects=True, vmem_limit_bytes=VMEM
         ),
@@ -1237,7 +1223,122 @@
             transcendentals=0,
         ),
         name="gate_up_grad",
-    )(left, right, spread, blocks, earlier)
+    )(left, right, to_x, to_y)
+
+
+def branch_sum_kernel(
+    act_ref, w_ref, left_ref, right_ref, spread_ref, blocks_ref,
+    mine, to_x, to_y, to_diagonal, spread_out, blocks_out,
+    odd, even, other, odd_send, odd_recv, store, *sems,
+):
+    width = spread_out.shape[2]
+    half = odd.shape[1]
+    outs = (mine, to_x, to_y, to_diagonal)
+
+    def columns(i):
+        return spread_ref.at[:, pl.ds(pl.multiple_of(i * width, width), width)]
+
+    spread = PlaneExchange(columns, spread_out, *sems[:3])
+    blocks = PlaneExchange(lambda i: blocks_ref.at[i], blocks_out, *sems[3:])
+    core = (neighbours(spread.seq)["core"], spread.rows)
+    greet(spread.peers())
+    spread.start()
+    blocks.start()
+
+    def hand_over(pair):
+        slot = lax.rem(pair, 2)
+        return remote(odd.at[slot], other.at[pair], core, odd_send.at[slot], odd_recv.at[pair])
+
+    def keep(pair):
+        at, place = (pair // 2, pair % 2) if pair < 8 else (pair - 8, 2)
+        target = outs[at].at[pl.ds(place * half, half)]
+        return pltpu.make_async_copy(even.at[pair % 2], target, store.at[pair % 2])
+
+    def body(unit, carry):
+        pair, side = lax.div(unit, 2), 1 - lax.rem(unit, 2)
+        begin = pl.multiple_of((pair + 8 * side) * half, half)
+        value = dot_nt(act_ref[pl.ds(begin, half), :], w_ref[...])
+
+        @pl.when(side == 1)
+        def _():
+            @pl.when(pair >= 2)
+            def _():
+                hand_over(pair - 2).wait_send()
+
+            odd[lax.rem(pair, 2)] = value.astype(BF16)
+            hand_over(pair).start()
+
+        @pl.when(side == 0)
+        def _():
+            hand_over(pair).wait_recv()
+            for p in range(8):
+
+                @pl.when(pair == p)
+                def _(p=p):
+                    if p >= 2:
+                        keep(p - 2).wait()
+                    even[p % 2] = (value + other[p].astype(F32)).astype(BF16)
+                    keep(p).start()
+
+        return carry
+
+    lax.fori_loop(0, 16, body, 0)
+
+    def columns_grad(mask):
+        at = pl.multiple_of(flipped(spread.seq, mask, spread.size) * half, half)
+        return dot_tn(left_ref[:, pl.ds(at, half)], right_ref[...])
+
+    for pair in range(8, 12):
+        mask = 2 * (pair - 8)
+        hand_over(pair - 2).wait_send()
+        odd[pair % 2] = columns_grad(mask + 1).astype(BF16)
+        hand_over(pair).start()
+        value = columns_grad(mask)
+        hand_over(pair).wait_recv()
+        keep(pair - 2).wait()
+        even[pair % 2] = (value + other[pair].astype(F32)).astype(BF16)
+        keep(pair).start()
+    for pair in (10, 11):
+        hand_over(pair).wait_send()
+        keep(pair).wait()
+    spread.finish()
+    blocks.finish()
+
+
+def branch_sum_call(act, w, left, right, spread, blocks):
+    tokens, part = act.shape
+    width = w.shape[0]
+    seq = lax.axis_size("seq")
+    count = tokens // seq
+    half = count // 2
+    here, there = pl.BlockSpec(memory_space=pltpu.VMEM), pl.BlockSpec(memory_space=pl.ANY)
+    return pl.pallas_call(
+        branch_sum_kernel,
+        in_specs=[here] * 4 + [there] * 2,
+        out_specs=[there] * 6,
+        out_shape=[jax.ShapeDtypeStruct((count + half, width), BF16)] * 4
+        + [
+            jax.ShapeDtypeStruct((seq, spread.shape[0], spread.shape[1] // seq), BF16),
+            jax.ShapeDtypeStruct(blocks.shape, BF16),
+        ],
+        scratch_shapes=[
+            pltpu.VMEM((2, half, width), BF16),
+            pltpu.VMEM((2, half, width), BF16),
+            pltpu.VMEM((12, half, width), BF16),
+            pltpu.SemaphoreType.DMA((2,)),
+            pltpu.SemaphoreType.DMA((12,)),
+            pltpu.SemaphoreType.DMA((2,)),
+        ]
+        + PlaneExchange.scratch()
+        + PlaneExchange.scratch(),
+        compiler_params=pltpu.CompilerParams(
+            collective_id=6, has_side_effects=True, vmem_limit_bytes=VMEM
+        ),
+        cost_estimate=pl.CostEstimate(
+            flops=2 * tokens * width * part, bytes_accessed=2 * tokens * width, transcendentals=0
+        ),
+        name="branch_sum",
+    )(act, w, left, right, spread, blocks)
 
 
 def branch_kernel(near_ref, far_ref, w_ref, _, near_out, far_out):
@@ -1300,6 +1401,45 @@
         ),
         name="out_grad",
     )(me, left, left, right, earlier)
+
+
+def finish_kernel(blocks_ref, weight_ref, gain_ref, out_ref, sum_ref):
+    @pl.when((pl.program_id(0) == 0) & (pl.program_id(1) == 0))
+    def _():
+        sum_ref[...] = jnp.zeros_like(sum_ref)
+
+    grad = blocks_ref[0].astype(F32)
+    products = weight_ref[...].astype(F32) * grad
+    sum_ref[...] += jnp.broadcast_to(jnp.sum(products, axis=1, keepdims=True), sum_ref.shape)
+    out_ref[...] = grad * gain_ref[...]
+
+
+def finish_call(blocks, weight, gain, groups):
+    seq, depth, cols = blocks.shape
+    part = cols // groups
+    grad, sums = pl.pallas_call(
+        finish_kernel,
+        grid=(seq, groups),
+        in_specs=[
+            pl.BlockSpec((1, depth, part), lambda i, g: (i, 0, g)),
+            pl.BlockSpec((depth, part), lambda i, g: (0, g * seq + i)),
+            pl.BlockSpec((depth, 1), lambda i, g: (0, 0)),
+        ],
+        out_specs=[
+            pl.BlockSpec((depth, part), lambda i, g: (0, g * seq + i)),
+            pl.BlockSpec((depth, 128), lambda i, g: (0, 0)),
+        ],
+        out_shape=[
+            jax.ShapeDtypeStruct((depth, seq * cols), F32),
+            jax.ShapeDtypeStruct((depth, 128), F32),
+        ],
+        compiler_params=pltpu.CompilerParams(vmem_limit_bytes=VMEM),
+        cost_estimate=pl.CostEstimate(
+            flops=4 * depth * seq * cols, bytes_accessed=8 * depth * seq * cols, transcendentals=0
+        ),
+        name="finish_grad",
+    )(blocks, weight, gain)
+    return grad, sums[:, 0]
 
 
 def scatter_shapes(count, width):
@@ -1345,7 +1485,7 @@
 
 
 def project_back_kernel(
-    d_ref, w_ref, gain_ref, blocks_ref, own, from_x, from_y, gain_out, blocks_out,
+    d_ref, w_ref, gain_ref, blocks_ref, _, own, from_x, from_y, gain_out, blocks_out,
     gain_sum, gain_from, gain_send, gain_recv, block_send, block_recv, block_local,
     total, odd, even, held, other, diagonal, odd_send, odd_recv, send, recv, keep,
 ):
@@ -1380,7 +1520,7 @@
         for i in range(len(partners)):
             at_unit(unit, 2 * i + 1, exchange(i).start)
             at_unit(unit, 2 * i + 2, partial(add_gains, i))
-        at_unit(unit, 8, blocks.start)
+        at_unit(unit, 13, blocks.start)
         pair, side = lax.div(unit, 2), 1 - lax.rem(unit, 2)
         begin = pl.multiple_of((PlaneScatter.place(pair) + 8 * side) * half, half)
         total[...] = dot_nt(d_ref[pl.ds(begin, half), :], w_ref[...])
@@ -1403,14 +1543,14 @@
     scatter.finish()
 
 
-def project_back_call(d, w, gains, blocks, count):
+def project_back_call(d, w, gains, blocks, count, earlier):
     width = w.shape[0]
     half = count // 2
     here, there = pl.BlockSpec(memory_space=pltpu.VMEM), pl.BlockSpec(memory_space=pl.ANY)
     rounds = 3 + (lax.axis_size("rows") - 1).bit_length()
     own, from_x, from_y, gains, blocks = pl.pallas_call(
         project_back_kernel,
-        in_specs=[here] * 3 + [there],
+        in_specs=[here] * 3 + [there] * 2,
         out_specs=[there] * 3 + [here, there],
         out_shape=scatter_shapes(count, width) + [
             jax.ShapeDtypeStruct(gains.shape, F32),
@@ -1434,7 +1574,7 @@
             flops=16 * d.shape[0] * width * w.shape[1], bytes_accessed=d.shape[0] * width * 8, transcendentals=0
         ),
         name="project_back",
-    )(d, w, gains, blocks)
+    )(d, w, gains, blocks, earlier)
     return own + from_x.astype(F32) + from_y.astype(F32), gains, blocks
 
 
@@ -1563,8 +1703,8 @@
         unit1, near, far, gate_up, act = gather_ffn_call(
             unit1, gather_pieces(grad_low, q), gu_mine
         )
-        down_grad = weight_grad_call([near, far], act, corner(act), depth, "down_grad")
-        u, d_gu = ffn_back_call(near, far, gate_up, gu_mine, down_mine, count, corner(down_grad))
+        down_grad = weight_grad_call([near, far], act, act, depth, "down_grad")
+        u, d_gu = ffn_back_call(near, far, gate_up, gu_mine, down_mine, count, down_grad)
     else:
         grad_all = gather_plane(grad_low)
         unit1 = gather_plane(unit1)
@@ -1572,7 +1712,7 @@
         u_odd = dot_nt(d_gu[half:], gu_mine).astype(BF16)
         u = scatter_plane(u_odd, dot_nt(d_gu[:half], gu_mine))
         near, far = grad_all[:half], grad_all[half:]
-        down_grad = weight_grad_call([near, far], act, corner(act), depth, "down_grad")
+        down_grad = weight_grad_call([near, far], act, act, depth, "down_grad")
     down_sum = scatter_z(down_grad)
 
     d_middle = (
@@ -1582,37 +1722,56 @@
     )
     d_branch = d_middle.astype(BF16)
     d_attended = dot_nn(d_branch, out_full).astype(BF16)
-    branch_near, branch_far = branch_call(act, down_mine, corner(d_attended))
     if seq == 8:
-        gu_grad, d_attended, down_sum = grad_exchange_call(
-            unit1, d_gu, d_attended, down_sum, corner(branch_near), depth
+        *sums, d_attended, down_owned = branch_sum_call(
+            act, down_mine, d_branch, attended, d_attended, down_sum
         )
         d_attended = d_attended.reshape(seq, rows, slots, query_width)
+        gu_grad, from_x, from_y = grad_send_call(unit1, d_gu, sums[1], sums[2], count, depth)
     else:
-        gu_grad = weight_grad_call([unit1], d_gu, corner(branch_near), depth, "gate_up_grad")
+        branch_near, branch_far = branch_call(act, down_mine, d_attended)
+        branch_far = swap(branch_far, 1).astype(F32)
+        branch_all = (branch_near.astype(F32) + branch_far).astype(BF16)
+        branch_parts = [branch_all[i * count : (i + 1) * count] for i in range(seq // 2)]
+        gu_grad = weight_grad_call([unit1], d_gu, branch_near, depth, "gate_up_grad")
         d_attended = d_attended.reshape(rows, slots, seq, query_width).transpose(2, 0, 1, 3)
         d_attended = all_to_all(d_attended)
-        down_sum = all_to_all(down_sum)
+        down_owned = all_to_all(down_sum)
     gu_sum = scatter_z(gu_grad)
     features = width // seq
-    out_near, out_far = out_grad_call(me, d_branch, attended, corner(gu_grad))
-    chips = seq // 2
-    branch_all = (branch_near.astype(F32) + swap(branch_far, 1).astype(F32)).astype(BF16)
-    out_all = (out_near.astype(F32) + swap(out_far, 1).astype(F32)).astype(BF16)
-    branch_parts = [branch_all[i * count : (i + 1) * count] for i in range(chips)]
-    out_parts = [out_all[i * features : (i + 1) * features] for i in range(chips)]
-    ready = after(lengths, gu_grad, *branch_parts, *out_parts)
-    dq, dkv = attend_back_call(ready, q, kv, attended_mine, d_attended, logs)
-    d_qkv, head_gain_grad = prepare_back_call(me, raw, dq, dkv, cos, sin, head_gains, slots)
-    qkv_grad = weight_grad_call([unit0], d_qkv, corner(d_qkv), depth, "qkv_grad")
-    branch = scatter_direct(branch_parts, d_qkv)
+    if seq != 8:
+        out_near, out_far = out_grad_call(me, d_branch, attended, gu_grad)
+        out_all = (out_near.astype(F32) + swap(out_far, 1).astype(F32)).astype(BF16)
+        sums = [
+            jnp.concatenate([branch_parts[i], out_all[i * features : (i + 1) * features]], axis=0)
+            for i in range(seq // 2)
+        ]
+    dq, dkv = attend_back_call(
+        lengths, q, kv, attended_mine, d_attended, logs, [gu_grad, *sums]
+    )
+    d_qkv, head_gain_grad = prepare_back_call(
+        me, raw, dq, dkv, cos, sin, head_gains, slots, dq
+    )
+    if seq == 8:
+        diagonal = swap(sums[3], 6)
+        arrived = [from_x, from_y, diagonal[:count]]
+        out_arrived = [swap(sums[i][count:], 2 * i) for i in (1, 2)] + [diagonal[count:]]
+    else:
+        arrived = [swap(sums[i], 2 * i) for i in range(1, seq // 2)]
+        out_arrived = [part[count:] for part in arrived]
+        arrived = [part[:count] for part in arrived]
+    branch = after(sums[0][:count].astype(F32), d_qkv)
+    for part_sum in arrived:
+        branch = branch + part_sum.astype(F32)
+    out_sum = after(sums[0][count:].astype(F32), d_qkv)
+    for part_sum in out_arrived:
+        out_sum = out_sum + part_sum.astype(F32)
     output = (middle + branch).astype(BF16).reshape(rows, slots, width)
-    out_sum = scatter_direct(out_parts, d_qkv)
+    qkv_grad = weight_grad_call([unit0], d_qkv, output, depth, "qkv_grad")
     if seq == 8:
-        gain_rows = after(head_gain_grad, qkv_grad, output, out_sum)
-        gain_rows = jnp.broadcast_to(gain_rows, (8, gain_rows.shape[1]))
+        gain_rows = jnp.broadcast_to(head_gain_grad, (8, head_gain_grad.shape[1]))
         u0, head_gain_grad, gu_owned = project_back_call(
-            d_qkv, qkv_mine, gain_rows, gu_sum, count
+            d_qkv, qkv_mine, gain_rows, gu_sum, count, qkv_grad
         )
     else:
         u0_odd = dot_nt(d_qkv[half:], qkv_mine).astype(BF16)
@@ -1620,8 +1779,9 @@
         head_gain_grad = sum_everywhere(head_gain_grad)
         gu_owned = all_to_all(gu_sum)
     parts = lax.axis_size("rows")
-    out_blocks = after(out_sum, gu_sum).astype(BF16).reshape(parts, depth * seq, kv_at // seq)
-    attn_sum = scatter_z(jnp.concatenate([qkv_grad, out_blocks], axis=2))
+    out_blocks = out_sum.astype(BF16).reshape(parts, depth * seq, kv_at // seq)
+    attn_grad = after(jnp.concatenate([qkv_grad, out_blocks], axis=2), gu_sum)
+    attn_sum = scatter_z(attn_grad)
     qkv_sum = attn_sum[:, :, : query_width + 2 * HEAD]
     out_sum = attn_sum[:, :, query_width + 2 * HEAD :].reshape(depth, kv_at)
     input_grad = (
@@ -1632,9 +1792,8 @@
         [head_gain_grad[0, :query_width].reshape(group, HEAD).sum(0), head_gain_grad[0, query_width : query_width + HEAD]]
     )
 
-    gu_sum = gu_owned.reshape(seq, depth, 2, part).transpose(1, 2, 0, 3)
-    gu_sum = gu_sum.reshape(depth, 2 * seq * part).astype(F32)
-    down_sum = down_sum.transpose(1, 0, 2).reshape(depth, seq * part).astype(F32)
+    gu_out, gu_rows = finish_call(gu_owned, gate_up_weight, gains[1][:, None], 2)
+    down_out, _ = finish_call(down_owned, down_weight, jnp.ones((depth, 1), F32), 1)
     qkv_sum = all_to_all(qkv_sum).transpose(1, 0, 2).astype(F32)
     kv_sum = qkv_sum[:, :, query_width:].reshape(depth, KEY_VALUE_HEADS, sharing, 2 * HEAD).sum(2)
     qkv_sum = jnp.concatenate(
@@ -1648,7 +1807,7 @@
     norm_gain_grad = jnp.stack(
         [
             jnp.sum(qkv_weight.astype(F32) * qkv_sum, axis=1),
-            jnp.sum(gate_up_weight.astype(F32) * gu_sum, axis=1),
+            gu_rows,
         ]
     )
     return (
@@ -1658,8 +1817,8 @@
         qk_grad,
         qkv_sum * gains[0][:, None],
         out_sum.astype(F32),
-        gu_sum * gains[1][:, None],
-        down_sum,
+        gu_out,
+        down_out,
     )
 
 

time: 984 us -> 960 us (0.976)
  local copies, waits for them, and re-layouts: 118 us -> 56.3 us
  Pallas kernels: 654 us -> 696 us
  waiting for transfers between devices: 49.3 us -> 67.2 us
  other arithmetic: 64.7 us -> 52.1 us
    pallas_call x4 -> x5, Pallas kernels: 199 us -> 242 us  [the longest x1 112 us: project_back_call(): pl.pallas_call(project_back_kernel, in_specs=[here] * 3 + [there] * 2, ou...]
    unnamed x105 -> x62, local copies, waits for them, and re-layouts: 41.9 us -> 9.47 us
    reduce_scatter x3, waiting for transfers between devices: 0.02 us -> 24.6 us  [scatter_z(): lax.psum_scatter(grad.reshape(parts * lines, cols), 'rows', scatter_dimen...]
    convert_element_type x3 -> x0, local copies, waits for them, and re-layouts: 12.8 us -> none  [the longest x2 11.3 us: shards(): gu_sum = gu_sum.reshape(depth, 2 * seq * part).astype(F32)]
    convert_element_type x3 -> x1, other arithmetic: 13.5 us -> 2.98 us  [shards(): out_blocks = out_sum.astype(BF16).reshape(parts, depth * seq, kv_at // seq)]
  transfers between devices with their start and end apart: 30 -> 25, of which waited for: 4 -> 4; matrix products, arithmetic and copies ran while one was open for 18% -> 11% of each run, Pallas kernels for 67% -> 62%
where the time goes in v3:
time: 960 us; the launch traced here: 949 us
  Pallas kernels  696 us (72%)
  waiting for transfers between devices  67.2 us (7%)
  local copies, waits for them, and re-layouts  56.3 us (6%)
  other arithmetic  52.1 us (5%)
  starting transfers between devices  29.2 us (3%)
  between operations  17.2 us (2%)
  matrix products  17 us (2%)
  blocking collectives  13.4 us (1%)
    pallas_call x1, Pallas kernels, gather_qkv_call(): pl.pallas_call(gather_qkv_kernel, in_specs=[there, here, here, here, here...  120 us
    pallas_call x1, Pallas kernels, project_back_call(): pl.pallas_call(project_back_kernel, in_specs=[here] * 3 + [there] * 2, ou...  112 us
    pallas_call x1, Pallas kernels, ffn_back_call(): pl.pallas_call(ffn_back_kernel, in_specs=[there] * 6, out_specs=[there] *...  92.4 us
    pallas_call x1, Pallas kernels, gather_ffn_call(): pl.pallas_call(gather_ffn_kernel, in_specs=[there] * 7, out_specs=[there]...  82.5 us
    pallas_call x1, Pallas kernels, attend_back_call(): pl.pallas_call(attend_back_kernel, grid_spec=pltpu.PrefetchScalarGridSpec...  66.3 us
    pallas_call x1, Pallas kernels, branch_sum_call(): pl.pallas_call(branch_sum_kernel, in_specs=[here] * 4 + [there] * 2, out_...  56.4 us
    pallas_call x1, Pallas kernels, grad_send_call(): pl.pallas_call(grad_send_kernel, grid=(seq,), in_specs=[pl.BlockSpec((tok...  55.5 us
    all_to_all x4, waiting for transfers between devices, all_to_all(): return lax.all_to_all(block, 'seq', 0, 0, tiled=True)  41.7 us
  transfers between devices with their start and end apart: 25, of which 4 were waited for; matrix products, arithmetic and copies ran while one was open for 11% of the time, Pallas kernels for 62%

profile of v3, /device:TPU:0, one launch (start us, length us, event | category | flops | bytes accessed | tf_op | source)
XLA Modules:
  0.0 948.6 jit_solution(16230209754792182909)
XLA Ops:
  10.1 13.4 %all_to_all.25 = bf16[8,64,384]{2,1,0:T(8,128)(2,1)} all-to-all(bf16[8,64,384]{2,1,0:T(8,128)(2,1)S(1)} %maximum_bitcast_fusion), channel_id=1, replica_groups=mesh['seq'=8,'rows'=4] {'seq'}, dimensions={0} | all-to-all | bytes 786432 | tf_op jit(solution)/shard_map/all_to_all | solution.py:1617
  35.5 25.8 %all-to-all-done.2 = bf16[8,64,2048]{2,1,0:T(8,128)(2,1)} async-done(((bf16[8,64,2048]{2,1,0:T(8,128)(2,1)}), bf16[8,64,2048]{2,1,0:T(8,128)(2,1)}, u32[]{:S(2)}, u32[]{:S(2)}) %all-to-all-start.2) | async-done | bytes 2097184 | tf_op jit(solution)/shard_map/all_to_all | solution.py:1617
  68.5 5.6 fusion.6
  75.9 120.2 %gather_qkv.1 = (bf16[4096,2048]{1,0:T(8,128)(2,1)}, f32[2,2048,384]{2,1,0:T(8,128)}, bf16[2,2048,256]{2,1,0:T(8,128)(2,1)}, bf16[2,2048,128]{2,1,0:T(8,128)(2,1)}) custom-call(bf16[512,2048]{1,0:T(8,128)(2,1)} %fusion.1.x_ref, bf16[2048,384]{1,0:T(8,128)(2,1)} %bitcast.118, f32[2048,128]{1,0:T(8,128)} %get-tuple-element.93.cos_ref, ...), custom_call_target="tpu_custom_call" | custom-call | flops 51539607552 | bytes 33554432 | tf_op jit(solution)/shard_map/gather_qkv/pallas_call | solution.py:747
  207.4 38.8 %attend.1 = (f32[2,2048,256]{2,1,0:T(8,128)}, bf16[8,2,256,256]{3,2,1,0:T(8,128)(2,1)}, f32[2,8,2048]{2,1,0:T(8,128)}) custom-call(s32[2]{0:T(128)} %lengths.3, bf16[2,2048,256]{2,1,0:T(8,128)(2,1)} %get-tuple-element.45.q_ref, bf16[2,2048,128]{2,1,0:T(8,128)(2,1)} %get-tuple-element.46.kv_ref), custom_call_target="tpu_custom_call" | custom-call | flops 34359738368 | bytes 8388608 | tf_op jit(solution)/shard_map/attend/pallas_call | solution.py:242
  246.3 4.6 all-to-all-start.1
  267.9 10.1 %all-to-all-done.1 = bf16[8,2,256,256]{3,2,1,0:T(8,128)(2,1)} async-done(((bf16[8,2,256,256]{3,2,1,0:T(8,128)(2,1)}), bf16[8,2,256,256]{3,2,1,0:T(8,128)(2,1)}, u32[]{:S(2)}, u32[]{:S(2)}) %all-to-all-start.1) | async-done | bytes 2097184 | tf_op jit(solution)/shard_map/all_to_all | solution.py:1617
  289.2 7.2 multiply_reduce_fusion.1
  300.0 82.5 %gather_ffn.1 = (bf16[4096,2048]{1,0:T(8,128)(2,1)}, bf16[2048,2048]{1,0:T(8,128)(2,1)}, bf16[2048,2048]{1,0:T(8,128)(2,1)}, bf16[4096,2048]{1,0:T(8,128)(2,1)}, bf16[4096,1024]{1,0:T(8,128)(2,1)}) custom-call(bf16[512,2048]{1,0:T(8,128)(2,1)} %multiply_convert_fusion.1.x_ref, bf16[512,2048]{1,0:T(8,128)(2,1)} %bitcast.94, ...), custom_call_target="tpu_custom_call" | custom-call | flops 68719476736 | bytes 67108864 | tf_op jit(solution)/shard_map/gather_ffn/pallas_call | solution.py:1008
  382.5 24.0 %down_grad.1._ = bf16[4,512,1024]{2,1,0:T(8,128)(2,1)} custom-call(bf16[2048,2048]{1,0:T(8,128)(2,1)} %get-tuple-element.49.refs_0_.near_ref, bf16[2048,2048]{1,0:T(8,128)(2,1)} %get-tuple-element.50.refs_1_.far_ref, bf16[4096,1024]{1,0:T(8,128)(2,1)} %get-tuple-element.48.refs_2_.refs_3_.act_ref, bf16[4096,1024]{1,0:T(8,128)(2,1)} %get-tuple-element.48.refs_2_.refs_3_.act_ref), custom_call_target="tpu_custom_call" | custom-call | flops 17179869184 | bytes 25165824 | tf_op jit(solution)/shard_map/down_grad/pallas_call | solution.py:1151
  407.0 92.4 %ffn_back.1 = (f32[512,2048]{1,0:T(8,128)}, bf16[512,2048]{1,0:T(8,128)(2,1)}, bf16[512,2048]{1,0:T(8,128)(2,1)}, bf16[4096,2048]{1,0:T(8,128)(2,1)}) custom-call(bf16[2048,2048]{1,0:T(8,128)(2,1)} %get-tuple-element.49.refs_0_.near_ref, bf16[2048,2048]{1,0:T(8,128)(2,1)} %get-tuple-element.50.refs_1_.far_ref, ...), custom_call_target="tpu_custom_call" | custom-call | flops 68719476736 | bytes 67108864 | tf_op jit(solution)/shard_map/ffn_back/pallas_call | solution.py:1457
  499.4 4.5 multiply_reduce_fusion
  509.2 9.8 %convolution_convert_fusion.spread_ref = bf16[512,2048]{1,0:T(8,128)(2,1)} fusion(bf16[512,2048]{1,0:T(8,128)(2,1)S(1)} %get-tuple-element.82.left_ref, bf16[2048,2048]{1,0:T(8,128)(2,1)} %constant_dynamic-update-slice_fusion.3), kind=kOutput, calls=%fused_computation.19 | convolution fusion | flops 4296015872 | bytes 12582912 | tf_op jit(solution)/shard_map/dot_general | solution.py:36
  518.9 56.4 %branch_sum.1 = (bf16[768,2048]{1,0:T(8,128)(2,1)}, bf16[768,2048]{1,0:T(8,128)(2,1)}, bf16[768,2048]{1,0:T(8,128)(2,1)}, bf16[768,2048]{1,0:T(8,128)(2,1)}, bf1...) custom-call(bf16[4096,1024]{1,0:T(8,128)(2,1)} %get-tuple-element.48.refs_2_.refs_3_.act_ref, ...), custom_call_target="tpu_custom_call" | custom-call | flops 17179869184 | bytes 16777216 | tf_op jit(solution)/shard_map/branch_sum/pallas_call | solution.py:1315
  575.4 55.5 %gate_up_grad.1 = (bf16[4,512,2048]{2,1,0:T(8,128)(2,1)}, bf16[512,2048]{1,0:T(8,128)(2,1)}, bf16[512,2048]{1,0:T(8,128)(2,1)}) custom-call(bf16[4096,2048]{1,0:T(8,128)(2,1)} %get-tuple-element.60.left_ref, bf16[4096,2048]{1,0:T(8,128)(2,1)} %get-tuple-element.61.right_ref, bf16[768,2048]{1,0:T(8,128)(2,1)} %get-tuple-element.62.to_x.refs_2_, ...), custom_call_target="tpu_custom_call" | custom-call | flops 34359738368 | bytes 33554432 | tf_op jit(solution)/shard_map/gate_up_grad/pallas_call | solution.py:1205
  640.3 66.3 %attend_back.1 = (f32[2,2048,256]{2,1,0:T(8,128)}, f32[2,2048,128]{2,1,0:T(8,128)}) custom-call(s32[2]{0:T(128)} %lengths.3, bf16[2,2048,256]{2,1,0:T(8,128)(2,1)} %get-tuple-element.45.q_ref, bf16[2,2048,128]{2,1,0:T(8,128)(2,1)} %get-tuple-element.46.kv_ref, f32[2,2048,256]{2,1,0:T(8,128)} %get-tuple-element.57.out_ref, ...), custom_call_target="tpu_custom_call" | custom-call | flops 60129542144 | bytes 14680064 | tf_op jit(solution)/shard_map/attend_back/pallas_call | solution.py:379
  706.7 15.3 %prepare_back.1 = (bf16[4096,384]{1,0:T(8,128)(2,1)}, f32[1,384]{1,0:T(1,128)}) custom-call(s32[1]{0:T(128)} %bitcast.18.me, f32[2,2048,384]{2,1,0:T(8,128)} %get-tuple-element.56.raw_ref, f32[2,2048,256]{2,1,0:T(8,128)} %get-tuple-element.66.dq_ref._, f32[2,2048,128]{2,1,0:T(8,128)} %get-tuple-element.67.dkv_ref, f32[2048,128]{1,0:T(8,128)} %get-tuple-element.93.cos_ref, ...), custom_call_target="tpu_custom_call" | custom-call | tf_op jit(solution)/shard_map/prepare_back/pallas_call | solution.py:447
  725.2 6.2 finish_grad.3
  736.6 8.1 add_convert_fusion
  744.7 15.2 %qkv_grad.1._ = bf16[4,512,384]{2,1,0:T(8,128)(2,1)} custom-call(bf16[4096,2048]{1,0:T(8,128)(2,1)} %get-tuple-element.72.refs_0_, bf16[4096,384]{1,0:T(8,128)(2,1)} %get-tuple-element.68.refs_1_.d_ref, bf16[2,256,2048]{2,1,0:T(8,128)(2,1)} %bitcast.99), custom_call_target="tpu_custom_call" | custom-call | flops 6442450944 | bytes 19922944 | tf_op jit(solution)/shard_map/qkv_grad/pallas_call | solution.py:1151
  759.9 24.6 %reduce-scatter.6.cloned.1.call-done = bf16[512,2048]{1,0:T(8,128)(2,1)} async-done(((bf16[2048,2048]{1,0:T(8,128)(2,1)}), bf16[512,2048]{1,0:T(8,128)(2,1)}) %reduce-scatter.6.cloned.1.call-update) | async-done | bytes 2097168 | tf_op jit(solution)/shard_map/reduce_scatter | solution.py:1627
  790.4 112.2 %project_back.1 = (f32[512,2048]{1,0:T(8,128)}, bf16[512,2048]{1,0:T(8,128)(2,1)}, bf16[512,2048]{1,0:T(8,128)(2,1)}, f32[8,384]{1,0:T(8,128)}, bf16[8,64,2048]{2,1,0:T(8,128)(2,1)}) custom-call(bf16[4096,384]{1,0:T(8,128)(2,1)} %get-tuple-element.68.refs_1_.d_ref, bf16[2048,384]{1,0:T(8,128)(2,1)} %bitcast.119, f32[8,384]{1,0:T(8,128)} %broadcast_in_dim.44.gain_ref, ...), custom_call_target="tpu_custom_call" | custom-call | flops 51539607552 | bytes 67108864 | tf_op jit(solution)/shard_map/project_back/pallas_call | solution.py:1551
  904.2 11.3 %finish_grad.2 = (f32[64,16384]{1,0:T(8,128)}, f32[64,128]{1,0:T(8,128)}) custom-call(bf16[8,64,2048]{2,1,0:T(8,128)(2,1)} %get-tuple-element.76.blocks_ref, bf16[64,16384]{1,0:T(8,128)(2,1)} %weight_ref.2, f32[64,1]{1,0:T(8,128)} %copy.36.gain_ref), custom_call_target="tpu_custom_call" | custom-call | flops 4194304 | bytes 8388608 | tf_op jit(solution)/shard_map/finish_grad/pallas_call | solution.py:1420
  932.9 5.8 all-to-all-done.4
  (192 shorter events, 115.7 us)
Async XLA Ops:
  7.2 68.7 %all-gather.5.cloned.1.call-start = ((), (), s32[]{:S(2)}) async-start(), calls=%async_computation.8 | async-start | bytes 1966080 | tf_op jit(solution)/shard_map/all_gather | solution.py:1621
  30.2 31.1 %all-to-all-start.2 = ((bf16[8,64,2048]{2,1,0:T(8,128)(2,1)}), bf16[8,64,2048]{2,1,0:T(8,128)(2,1)}, u32[]{:S(2)}, u32[]{:S(2)}) async-start(bf16[8,64,2048]{2,1,0:T(8,128)(2,1)} %reshape.190), calls=%async_computation.2 | async-start | bytes 4194304 | tf_op jit(solution)/shard_map/all_to_all | solution.py:1617
  34.7 163.3 %all-gather.7.cloned.1.call-start = ((), (), s32[]{:S(2)}) async-start(), calls=%async_computation.9 | async-start | bytes 1310720 | tf_op jit(solution)/shard_map/all_gather | solution.py:1668
  35.4 264.6 %all-gather.9.cloned.1.call-start = ((), (), s32[]{:S(2)}) async-start(), calls=%async_computation.10 | async-start | bytes 10485760 | tf_op jit(solution)/shard_map/all_gather | solution.py:1621
  61.4 192.4 %collective-permute-start.7 = (bf16[512,2048]{1,0:T(8,128)(2,1)}, bf16[512,2048]{1,0:T(8,128)(2,1)}, u32[]{:S(2)}, u32[]{:S(2)}) collective-permute-start(bf16[512,2048]{1,0:T(8,128)(2,1)} %bitcast.92), channel_id=1, source_target_pairs={{0,8},{4,12},{8,0},{12,4},{16,24},{20,28},{24,16},{28,20},{1,9},{5... | collective-permute-start | bytes 6291464 | tf_op jit(solution)/shard_map/ppermute | solution.py:24
  61.9 190.1 %collective-permute-start.8 = (bf16[512,2048]{1,0:T(8,128)(2,1)}, bf16[512,2048]{1,0:T(8,128)(2,1)}, u32[]{:S(2)}, u32[]{:S(2)}) collective-permute-start(bf16[512,2048]{1,0:T(8,128)(2,1)} %bitcast.93), channel_id=1, source_target_pairs={{0,16},{4,20},{8,24},{12,28},{16,0},{20,4},{24,8},{28,12},{1,17},{... | collective-permute-start | bytes 6291464 | tf_op jit(solution)/shard_map/ppermute | solution.py:24
  63.6 182.6 %all-to-all-start.3 = ((bf16[8,64,1024]{2,1,0:T(8,128)(2,1)}), bf16[8,64,1024]{2,1,0:T(8,128)(2,1)S(1)}, u32[]{:S(2)}, u32[]{:S(2)}) async-start(bf16[8,64,1024]{2,1,0:T(8,128)(2,1)} %bitcast.91), calls=%async_computation.3 | async-start | bytes 2097152 | tf_op jit(solution)/shard_map/all_to_all | solution.py:1617
  203.9 51.6 %collective-permute-start = (bf16[256,2048]{1,0:T(8,128)(2,1)}, bf16[256,2048]{1,0:T(8,128)(2,1)}, u32[]{:S(2)}, u32[]{:S(2)}) collective-permute-start(bf16[256,2048]{1,0:T(8,128)(2,1)} %get-tuple-element.85), channel_id=1, source_target_pairs={{0,8},{4,12},{8,0},{12,4},{16,24},{20,28},{24,16},{28,20},{1,9},{5... | collective-permute-start | bytes 3145736 | tf_op jit(solution)/shard_map/ppermute | solution.py:24
  204.9 53.0 %collective-permute-start.1 = (bf16[256,2048]{1,0:T(8,128)(2,1)}, bf16[256,2048]{1,0:T(8,128)(2,1)}, u32[]{:S(2)}, u32[]{:S(2)}) collective-permute-start(bf16[256,2048]{1,0:T(8,128)(2,1)} %get-tuple-element.85), channel_id=1, source_target_pairs={{0,16},{4,20},{8,24},{12,28},{16,0},{20,4},{24,8},{28,12},{1,17},{... | collective-permute-start | bytes 3145736 | tf_op jit(solution)/shard_map/ppermute | solution.py:24
  204.9 53.4 %collective-permute-start.2 = (bf16[256,2048]{1,0:T(8,128)(2,1)}, bf16[256,2048]{1,0:T(8,128)(2,1)}, u32[]{:S(2)}, u32[]{:S(2)}) collective-permute-start(bf16[256,2048]{1,0:T(8,128)(2,1)} %get-tuple-element.85), channel_id=1, source_target_pairs={{0,24},{4,28},{8,16},{12,20},{16,8},{20,12},{24,0},{28,4},{1,25},{... | collective-permute-start | bytes 3145736 | tf_op jit(solution)/shard_map/ppermute | solution.py:24
  246.3 31.7 %all-to-all-start.1 = ((bf16[8,2,256,256]{3,2,1,0:T(8,128)(2,1)}), bf16[8,2,256,256]{3,2,1,0:T(8,128)(2,1)}, u32[]{:S(2)}, u32[]{:S(2)}) async-start(bf16[8,2,256,256]{3,2,1,0:T(8,128)(2,1)} %get-tuple-element.47), calls=%async_computation.1 | async-start | bytes 4194304 | tf_op jit(solution)/shard_map/all_to_all | solution.py:1617
  250.8 156.1 %all-gather.11.cloned.1.call-start = ((), (), s32[]{:S(2)}) async-start(), calls=%async_computation.11 | async-start | bytes 5242880 | tf_op jit(solution)/shard_map/all_gather | solution.py:1621
  252.0 266.9 %reduce-scatter.4.cloned.1.call-start = ((), (), s32[]{:S(2)}) async-start(), calls=%async_computation.12 | async-start | bytes 5242880 | tf_op jit(solution)/shard_map/reduce_scatter | solution.py:1627
  252.1 13.3 %collective-permute-start.3 = (bf16[256,2048]{1,0:T(8,128)(2,1)}, bf16[256,2048]{1,0:T(8,128)(2,1)S(1)}, u32[]{:S(2)}, u32[]{:S(2)}) collective-permute-start(bf16[256,2048]{1,0:T(8,128)(2,1)} %get-tuple-element.85), channel_id=1, source_target_pairs={{0,4},{4,0},{8,12},{12,8},{16,20},{20,16},{24,28},{28,24},{1,5},{5... | collective-permute-start | bytes 3145736 | tf_op jit(solution)/shard_map/ppermute | solution.py:24
  253.8 46.2 %collective-permute-start.9 = (bf16[256,2048]{1,0:T(8,128)(2,1)S(1)}, bf16[256,2048]{1,0:T(8,128)(2,1)}, u32[]{:S(2)}, u32[]{:S(2)}) collective-permute-start(bf16[256,2048]{1,0:T(8,128)(2,1)S(1)} %slice_add_fusion.1), channel_id=1, source_target_pairs={{0,8},{4,12},{8,0},{12,4},{16,24},{20,28},{24,16},{28,20},{1,9},{5... | collective-permute-start | bytes 3145736 | tf_op jit(solution)/shard_map/ppermute | solution.py:24
  255.5 26.0 %collective-permute-start.4 = (bf16[256,2048]{1,0:T(8,128)(2,1)}, bf16[256,2048]{1,0:T(8,128)(2,1)}, u32[]{:S(2)}, u32[]{:S(2)}) collective-permute-start(bf16[256,2048]{1,0:T(8,128)(2,1)} %collective-permute-done), channel_id=1, source_target_pairs={{0,4},{4,0},{8,12},{12,8},{16,20},{20,16},{24,28},{28,24},{1,5},{5... | collective-permute-start | bytes 3145736 | tf_op jit(solution)/shard_map/ppermute | solution.py:24
  257.8 26.7 %collective-permute-start.5 = (bf16[256,2048]{1,0:T(8,128)(2,1)}, bf16[256,2048]{1,0:T(8,128)(2,1)}, u32[]{:S(2)}, u32[]{:S(2)}) collective-permute-start(bf16[256,2048]{1,0:T(8,128)(2,1)} %collective-permute-done.1), channel_id=1, source_target_pairs={{0,4},{4,0},{8,12},{12,8},{16,20},{20,16},{24,28},{28,24},{1,5},{5... | collective-permute-start | bytes 3145736 | tf_op jit(solution)/shard_map/ppermute | solution.py:24
  258.3 28.6 %collective-permute-start.6 = (bf16[256,2048]{1,0:T(8,128)(2,1)}, bf16[256,2048]{1,0:T(8,128)(2,1)}, u32[]{:S(2)}, u32[]{:S(2)}) collective-permute-start(bf16[256,2048]{1,0:T(8,128)(2,1)} %collective-permute-done.2), channel_id=1, source_target_pairs={{0,4},{4,0},{8,12},{12,8},{16,20},{20,16},{24,28},{28,24},{1,5},{5... | collective-permute-start | bytes 3145736 | tf_op jit(solution)/shard_map/ppermute | solution.py:24
  265.4 34.6 %collective-permute-start.10 = (bf16[256,2048]{1,0:T(8,128)(2,1)}, bf16[256,2048]{1,0:T(8,128)(2,1)}, u32[]{:S(2)}, u32[]{:S(2)}) collective-permute-start(bf16[256,2048]{1,0:T(8,128)(2,1)} %slice_add_fusion), channel_id=1, source_target_pairs={{0,16},{4,20},{8,24},{12,28},{16,0},{20,4},{24,8},{28,12},{1,17},{... | collective-permute-start | bytes 3145736 | tf_op jit(solution)/shard_map/ppermute | solution.py:24
  406.5 378.0 %reduce-scatter.6.cloned.1.call-start = ((), (), s32[]{:S(2)}) async-start(), calls=%async_computation.13 | async-start | bytes 10485760 | tf_op jit(solution)/shard_map/reduce_scatter | solution.py:1627
  630.9 294.3 %reduce-scatter.8.cloned.1.call-start = ((), (), s32[]{:S(2)}) async-start(), calls=%async_computation.14 | async-start | bytes 3276800 | tf_op jit(solution)/shard_map/reduce_scatter | solution.py:1627
  636.8 94.6 %collective-permute-start.11 = (bf16[768,2048]{1,0:T(8,128)(2,1)}, bf16[768,2048]{1,0:T(8,128)(2,1)S(1)}, u32[]{:S(2)}, u32[]{:S(2)}) collective-permute-start(bf16[768,2048]{1,0:T(8,128)(2,1)} %get-tuple-element.65.refs_4_), channel_id=1, source_target_pairs={{0,24},{4,28},{8,16},{12,20},{16,8},{20,12},{24,0},{28,4},{1,25},{... | collective-permute-start | bytes 9437192 | tf_op jit(solution)/shard_map/ppermute | solution.py:24
  638.3 93.1 %collective-permute-start.13 = (bf16[256,2048]{1,0:T(8,128)(2,1)}, bf16[256,2048]{1,0:T(8,128)(2,1)}, u32[]{:S(2)}, u32[]{:S(2)}) collective-permute-start(bf16[256,2048]{1,0:T(8,128)(2,1)} %slice.106), channel_id=1, source_target_pairs={{0,16},{4,20},{8,24},{12,28},{16,0},{20,4},{24,8},{28,12},{1,17},{... | collective-permute-start | bytes 3145736 | tf_op jit(solution)/shard_map/ppermute | solution.py:24
  638.9 92.5 %collective-permute-start.12 = (bf16[256,2048]{1,0:T(8,128)(2,1)}, bf16[256,2048]{1,0:T(8,128)(2,1)}, u32[]{:S(2)}, u32[]{:S(2)}) collective-permute-start(bf16[256,2048]{1,0:T(8,128)(2,1)} %slice.105), channel_id=1, source_target_pairs={{0,8},{4,12},{8,0},{12,4},{16,24},{20,28},{24,16},{28,20},{1,9},{5... | collective-permute-start | bytes 3145736 | tf_op jit(solution)/shard_map/ppermute | solution.py:24
  (29 other events, 451.0 us)
Sparse Core Ops, SparseCore 0:
  23.7 36.4 all-gather.4
  61.8 26.7 all-gather.6
  90.2 149.1 all-gather.8
  252.9 91.1 all-gather.10
  406.6 86.1 reduce-scatter.3
  631.0 153.4 reduce-scatter.5
  789.9 53.2 reduce-scatter.7

commit v4 on v3

--- a/solution.py
+++ b/solution.py
@@ -1408,25 +1408,30 @@
     def _():
         sum_ref[...] = jnp.zeros_like(sum_ref)
 
-    grad = blocks_ref[0].astype(F32)
-    products = weight_ref[...].astype(F32) * grad
-    sum_ref[...] += jnp.broadcast_to(jnp.sum(products, axis=1, keepdims=True), sum_ref.shape)
-    out_ref[...] = grad * gain_ref[...]
+    part = blocks_ref.shape[2]
+    for i in range(blocks_ref.shape[0]):
+        lanes = slice(i * part, (i + 1) * part)
+        grad = blocks_ref[i].astype(F32)
+        products = weight_ref[:, lanes].astype(F32) * grad
+        sum_ref[...] += jnp.broadcast_to(jnp.sum(products, axis=1, keepdims=True), sum_ref.shape)
+        out_ref[:, lanes] = grad * gain_ref[...]
 
 
 def finish_call(blocks, weight, gain, groups):
     seq, depth, cols = blocks.shape
     part = cols // groups
+    many = 4
+    steps = seq // many
     grad, sums = pl.pallas_call(
         finish_kernel,
-        grid=(seq, groups),
+        grid=(steps, groups),
         in_specs=[
-            pl.BlockSpec((1, depth, part), lambda i, g: (i, 0, g)),
-            pl.BlockSpec((depth, part), lambda i, g: (0, g * seq + i)),
+            pl.BlockSpec((many, depth, part), lambda i, g: (i, 0, g)),
+            pl.BlockSpec((depth, many * part), lambda i, g: (0, g * steps + i)),
             pl.BlockSpec((depth, 1), lambda i, g: (0, 0)),
         ],
         out_specs=[
-            pl.BlockSpec((depth, part), lambda i, g: (0, g * seq + i)),
+            pl.BlockSpec((depth, many * part), lambda i, g: (0, g * steps + i)),
             pl.BlockSpec((depth, 128), lambda i, g: (0, 0)),
         ],
         out_shape=[

time: 960 us -> 959 us (level)
  transfers between devices with their start and end apart: 25 -> 25, of which waited for: 4 -> 5; matrix products, arithmetic and copies ran while one was open for 11% -> 11% of each run, Pallas kernels for 62% -> 61%
where the time goes in v4:
time: 959 us; the launch traced here: 952 us
  Pallas kernels  691 us (72%)
  waiting for transfers between devices  75.3 us (8%)
  local copies, waits for them, and re-layouts  56.3 us (6%)
  other arithmetic  52.1 us (5%)
  starting transfers between devices  29.2 us (3%)
  between operations  17.2 us (2%)
  matrix products  16.9 us (2%)
  blocking collectives  13.4 us (1%)
    pallas_call x1, Pallas kernels, gather_qkv_call(): pl.pallas_call(gather_qkv_kernel, in_specs=[there, here, here, here, here...  120 us
    pallas_call x1, Pallas kernels, project_back_call(): pl.pallas_call(project_back_kernel, in_specs=[here] * 3 + [there] * 2, ou...  117 us
    pallas_call x1, Pallas kernels, ffn_back_call(): pl.pallas_call(ffn_back_kernel, in_specs=[there] * 6, out_specs=[there] *...  92.2 us
    pallas_call x1, Pallas kernels, gather_ffn_call(): pl.pallas_call(gather_ffn_kernel, in_specs=[there] * 7, out_specs=[there]...  82.7 us
    pallas_call x1, Pallas kernels, attend_back_call(): pl.pallas_call(attend_back_kernel, grid_spec=pltpu.PrefetchScalarGridSpec...  66.3 us
    pallas_call x1, Pallas kernels, branch_sum_call(): pl.pallas_call(branch_sum_kernel, in_specs=[here] * 4 + [there] * 2, out_...  56.4 us
    pallas_call x1, Pallas kernels, grad_send_call(): pl.pallas_call(grad_send_kernel, grid=(seq,), in_specs=[pl.BlockSpec((tok...  55.5 us
    all_to_all x4, waiting for transfers between devices, all_to_all(): return lax.all_to_all(block, 'seq', 0, 0, tiled=True)  41.7 us
  transfers between devices with their start and end apart: 25, of which 5 were waited for; matrix products, arithmetic and copies ran while one was open for 11% of the time, Pallas kernels for 61%

profile of v4, /device:TPU:0, one launch (start us, length us, event | category | flops | bytes accessed | tf_op | source)
XLA Modules:
  0.0 951.8 jit_solution(14360017006635088144)
XLA Ops:
  10.1 13.4 %all_to_all.25 = bf16[8,64,384]{2,1,0:T(8,128)(2,1)} all-to-all(bf16[8,64,384]{2,1,0:T(8,128)(2,1)S(1)} %maximum_bitcast_fusion), channel_id=1, replica_groups=mesh['seq'=8,'rows'=4] {'seq'}, dimensions={0} | all-to-all | bytes 786432 | tf_op jit(solution)/shard_map/all_to_all | solution.py:1622
  30.2 4.5 all-to-all-start.2
  35.5 25.8 %all-to-all-done.2 = bf16[8,64,2048]{2,1,0:T(8,128)(2,1)} async-done(((bf16[8,64,2048]{2,1,0:T(8,128)(2,1)}), bf16[8,64,2048]{2,1,0:T(8,128)(2,1)}, u32[]{:S(2)}, u32[]{:S(2)}) %all-to-all-start.2) | async-done | bytes 2097184 | tf_op jit(solution)/shard_map/all_to_all | solution.py:1622
  68.5 5.6 fusion.6
  75.9 120.2 %gather_qkv.1 = (bf16[4096,2048]{1,0:T(8,128)(2,1)}, f32[2,2048,384]{2,1,0:T(8,128)}, bf16[2,2048,256]{2,1,0:T(8,128)(2,1)}, bf16[2,2048,128]{2,1,0:T(8,128)(2,1)}) custom-call(bf16[512,2048]{1,0:T(8,128)(2,1)} %fusion.1.x_ref, bf16[2048,384]{1,0:T(8,128)(2,1)} %bitcast.118, f32[2048,128]{1,0:T(8,128)} %get-tuple-element.93.cos_ref, ...), custom_call_target="tpu_custom_call" | custom-call | flops 51539607552 | bytes 33554432 | tf_op jit(solution)/shard_map/gather_qkv/pallas_call | solution.py:747
  207.4 38.8 %attend.1 = (f32[2,2048,256]{2,1,0:T(8,128)}, bf16[8,2,256,256]{3,2,1,0:T(8,128)(2,1)}, f32[2,8,2048]{2,1,0:T(8,128)}) custom-call(s32[2]{0:T(128)} %lengths.3, bf16[2,2048,256]{2,1,0:T(8,128)(2,1)} %get-tuple-element.45.q_ref, bf16[2,2048,128]{2,1,0:T(8,128)(2,1)} %get-tuple-element.46.kv_ref), custom_call_target="tpu_custom_call" | custom-call | flops 34359738368 | bytes 8388608 | tf_op jit(solution)/shard_map/attend/pallas_call | solution.py:242
  246.3 4.6 all-to-all-start.1
  267.9 10.1 %all-to-all-done.1 = bf16[8,2,256,256]{3,2,1,0:T(8,128)(2,1)} async-done(((bf16[8,2,256,256]{3,2,1,0:T(8,128)(2,1)}), bf16[8,2,256,256]{3,2,1,0:T(8,128)(2,1)}, u32[]{:S(2)}, u32[]{:S(2)}) %all-to-all-start.1) | async-done | bytes 2097184 | tf_op jit(solution)/shard_map/all_to_all | solution.py:1622
  289.2 7.1 multiply_reduce_fusion.1
  300.0 82.7 %gather_ffn.1 = (bf16[4096,2048]{1,0:T(8,128)(2,1)}, bf16[2048,2048]{1,0:T(8,128)(2,1)}, bf16[2048,2048]{1,0:T(8,128)(2,1)}, bf16[4096,2048]{1,0:T(8,128)(2,1)}, bf16[4096,1024]{1,0:T(8,128)(2,1)}) custom-call(bf16[512,2048]{1,0:T(8,128)(2,1)} %multiply_convert_fusion.1.x_ref, bf16[512,2048]{1,0:T(8,128)(2,1)} %bitcast.94, ...), custom_call_target="tpu_custom_call" | custom-call | flops 68719476736 | bytes 67108864 | tf_op jit(solution)/shard_map/gather_ffn/pallas_call | solution.py:1008
  382.6 23.9 %down_grad.1._ = bf16[4,512,1024]{2,1,0:T(8,128)(2,1)} custom-call(bf16[2048,2048]{1,0:T(8,128)(2,1)} %get-tuple-element.49.refs_0_.near_ref, bf16[2048,2048]{1,0:T(8,128)(2,1)} %get-tuple-element.50.refs_1_.far_ref, bf16[4096,1024]{1,0:T(8,128)(2,1)} %get-tuple-element.48.refs_2_.refs_3_.act_ref, bf16[4096,1024]{1,0:T(8,128)(2,1)} %get-tuple-element.48.refs_2_.refs_3_.act_ref), custom_call_target="tpu_custom_call" | custom-call | flops 17179869184 | bytes 25165824 | tf_op jit(solution)/shard_map/down_grad/pallas_call | solution.py:1151
  407.1 92.2 %ffn_back.1 = (f32[512,2048]{1,0:T(8,128)}, bf16[512,2048]{1,0:T(8,128)(2,1)}, bf16[512,2048]{1,0:T(8,128)(2,1)}, bf16[4096,2048]{1,0:T(8,128)(2,1)}) custom-call(bf16[2048,2048]{1,0:T(8,128)(2,1)} %get-tuple-element.49.refs_0_.near_ref, bf16[2048,2048]{1,0:T(8,128)(2,1)} %get-tuple-element.50.refs_1_.far_ref, ...), custom_call_target="tpu_custom_call" | custom-call | flops 68719476736 | bytes 67108864 | tf_op jit(solution)/shard_map/ffn_back/pallas_call | solution.py:1462
  499.4 4.5 multiply_reduce_fusion
  509.2 9.8 %convolution_convert_fusion.spread_ref = bf16[512,2048]{1,0:T(8,128)(2,1)} fusion(bf16[512,2048]{1,0:T(8,128)(2,1)S(1)} %get-tuple-element.82.left_ref, bf16[2048,2048]{1,0:T(8,128)(2,1)} %constant_dynamic-update-slice_fusion.3), kind=kOutput, calls=%fused_computation.19 | convolution fusion | flops 4296015872 | bytes 12582912 | tf_op jit(solution)/shard_map/dot_general | solution.py:36
  518.9 56.4 %branch_sum.1 = (bf16[768,2048]{1,0:T(8,128)(2,1)}, bf16[768,2048]{1,0:T(8,128)(2,1)}, bf16[768,2048]{1,0:T(8,128)(2,1)}, bf16[768,2048]{1,0:T(8,128)(2,1)}, bf1...) custom-call(bf16[4096,1024]{1,0:T(8,128)(2,1)} %get-tuple-element.48.refs_2_.refs_3_.act_ref, ...), custom_call_target="tpu_custom_call" | custom-call | flops 17179869184 | bytes 16777216 | tf_op jit(solution)/shard_map/branch_sum/pallas_call | solution.py:1315
  575.3 55.5 %gate_up_grad.1 = (bf16[4,512,2048]{2,1,0:T(8,128)(2,1)}, bf16[512,2048]{1,0:T(8,128)(2,1)}, bf16[512,2048]{1,0:T(8,128)(2,1)}) custom-call(bf16[4096,2048]{1,0:T(8,128)(2,1)} %get-tuple-element.60.left_ref, bf16[4096,2048]{1,0:T(8,128)(2,1)} %get-tuple-element.61.right_ref, bf16[768,2048]{1,0:T(8,128)(2,1)} %get-tuple-element.62.to_x.refs_2_, ...), custom_call_target="tpu_custom_call" | custom-call | flops 34359738368 | bytes 33554432 | tf_op jit(solution)/shard_map/gate_up_grad/pallas_call | solution.py:1205
  640.3 66.3 %attend_back.1 = (f32[2,2048,256]{2,1,0:T(8,128)}, f32[2,2048,128]{2,1,0:T(8,128)}) custom-call(s32[2]{0:T(128)} %lengths.3, bf16[2,2048,256]{2,1,0:T(8,128)(2,1)} %get-tuple-element.45.q_ref, bf16[2,2048,128]{2,1,0:T(8,128)(2,1)} %get-tuple-element.46.kv_ref, f32[2,2048,256]{2,1,0:T(8,128)} %get-tuple-element.57.out_ref, ...), custom_call_target="tpu_custom_call" | custom-call | flops 60129542144 | bytes 14680064 | tf_op jit(solution)/shard_map/attend_back/pallas_call | solution.py:379
  706.6 15.3 %prepare_back.1 = (bf16[4096,384]{1,0:T(8,128)(2,1)}, f32[1,384]{1,0:T(1,128)}) custom-call(s32[1]{0:T(128)} %bitcast.18.me, f32[2,2048,384]{2,1,0:T(8,128)} %get-tuple-element.56.raw_ref, f32[2,2048,256]{2,1,0:T(8,128)} %get-tuple-element.66.dq_ref._, f32[2,2048,128]{2,1,0:T(8,128)} %get-tuple-element.67.dkv_ref, f32[2048,128]{1,0:T(8,128)} %get-tuple-element.93.cos_ref, ...), custom_call_target="tpu_custom_call" | custom-call | tf_op jit(solution)/shard_map/prepare_back/pallas_call | solution.py:447
  734.9 8.2 add_convert_fusion
  743.1 15.2 %qkv_grad.1._ = bf16[4,512,384]{2,1,0:T(8,128)(2,1)} custom-call(bf16[4096,2048]{1,0:T(8,128)(2,1)} %get-tuple-element.72.refs_0_, bf16[4096,384]{1,0:T(8,128)(2,1)} %get-tuple-element.68.refs_1_.d_ref, bf16[2,256,2048]{2,1,0:T(8,128)(2,1)} %bitcast.99), custom_call_target="tpu_custom_call" | custom-call | flops 6442450944 | bytes 19922944 | tf_op jit(solution)/shard_map/qkv_grad/pallas_call | solution.py:1151
  758.3 30.9 %reduce-scatter.6.cloned.1.call-done = bf16[512,2048]{1,0:T(8,128)(2,1)} async-done(((bf16[2048,2048]{1,0:T(8,128)(2,1)}), bf16[512,2048]{1,0:T(8,128)(2,1)}) %reduce-scatter.6.cloned.1.call-update) | async-done | bytes 2097168 | tf_op jit(solution)/shard_map/reduce_scatter | solution.py:1632
  795.1 116.6 %project_back.1 = (f32[512,2048]{1,0:T(8,128)}, bf16[512,2048]{1,0:T(8,128)(2,1)}, bf16[512,2048]{1,0:T(8,128)(2,1)}, f32[8,384]{1,0:T(8,128)}, bf16[8,64,2048]{2,1,0:T(8,128)(2,1)}) custom-call(bf16[4096,384]{1,0:T(8,128)(2,1)} %get-tuple-element.68.refs_1_.d_ref, bf16[2048,384]{1,0:T(8,128)(2,1)} %bitcast.119, f32[8,384]{1,0:T(8,128)} %broadcast_in_dim.44.gain_ref, ...), custom_call_target="tpu_custom_call" | custom-call | flops 51539607552 | bytes 67108864 | tf_op jit(solution)/shard_map/project_back/pallas_call | solution.py:1556
  913.4 5.3 finish_grad.2
  936.1 5.8 all-to-all-done.4
  (192 shorter events, 115.8 us)
Async XLA Ops:
  7.2 68.7 %all-gather.5.cloned.1.call-start = ((), (), s32[]{:S(2)}) async-start(), calls=%async_computation.8 | async-start | bytes 1966080 | tf_op jit(solution)/shard_map/all_gather | solution.py:1626
  30.2 31.1 %all-to-all-start.2 = ((bf16[8,64,2048]{2,1,0:T(8,128)(2,1)}), bf16[8,64,2048]{2,1,0:T(8,128)(2,1)}, u32[]{:S(2)}, u32[]{:S(2)}) async-start(bf16[8,64,2048]{2,1,0:T(8,128)(2,1)} %reshape.190), calls=%async_computation.2 | async-start | bytes 4194304 | tf_op jit(solution)/shard_map/all_to_all | solution.py:1622
  34.7 163.3 %all-gather.7.cloned.1.call-start = ((), (), s32[]{:S(2)}) async-start(), calls=%async_computation.9 | async-start | bytes 1310720 | tf_op jit(solution)/shard_map/all_gather | solution.py:1673
  35.4 264.5 %all-gather.9.cloned.1.call-start = ((), (), s32[]{:S(2)}) async-start(), calls=%async_computation.10 | async-start | bytes 10485760 | tf_op jit(solution)/shard_map/all_gather | solution.py:1626
  61.4 192.4 %collective-permute-start.7 = (bf16[512,2048]{1,0:T(8,128)(2,1)}, bf16[512,2048]{1,0:T(8,128)(2,1)}, u32[]{:S(2)}, u32[]{:S(2)}) collective-permute-start(bf16[512,2048]{1,0:T(8,128)(2,1)} %bitcast.92), channel_id=1, source_target_pairs={{0,8},{4,12},{8,0},{12,4},{16,24},{20,28},{24,16},{28,20},{1,9},{5... | collective-permute-start | bytes 6291464 | tf_op jit(solution)/shard_map/ppermute | solution.py:24
  61.9 190.1 %collective-permute-start.8 = (bf16[512,2048]{1,0:T(8,128)(2,1)}, bf16[512,2048]{1,0:T(8,128)(2,1)}, u32[]{:S(2)}, u32[]{:S(2)}) collective-permute-start(bf16[512,2048]{1,0:T(8,128)(2,1)} %bitcast.93), channel_id=1, source_target_pairs={{0,16},{4,20},{8,24},{12,28},{16,0},{20,4},{24,8},{28,12},{1,17},{... | collective-permute-start | bytes 6291464 | tf_op jit(solution)/shard_map/ppermute | solution.py:24
  63.6 182.6 %all-to-all-start.3 = ((bf16[8,64,1024]{2,1,0:T(8,128)(2,1)}), bf16[8,64,1024]{2,1,0:T(8,128)(2,1)S(1)}, u32[]{:S(2)}, u32[]{:S(2)}) async-start(bf16[8,64,1024]{2,1,0:T(8,128)(2,1)} %bitcast.91), calls=%async_computation.3 | async-start | bytes 2097152 | tf_op jit(solution)/shard_map/all_to_all | solution.py:1622
  203.9 51.6 %collective-permute-start = (bf16[256,2048]{1,0:T(8,128)(2,1)}, bf16[256,2048]{1,0:T(8,128)(2,1)}, u32[]{:S(2)}, u32[]{:S(2)}) collective-permute-start(bf16[256,2048]{1,0:T(8,128)(2,1)} %get-tuple-element.85), channel_id=1, source_target_pairs={{0,8},{4,12},{8,0},{12,4},{16,24},{20,28},{24,16},{28,20},{1,9},{5... | collective-permute-start | bytes 3145736 | tf_op jit(solution)/shard_map/ppermute | solution.py:24
  204.9 53.0 %collective-permute-start.1 = (bf16[256,2048]{1,0:T(8,128)(2,1)}, bf16[256,2048]{1,0:T(8,128)(2,1)}, u32[]{:S(2)}, u32[]{:S(2)}) collective-permute-start(bf16[256,2048]{1,0:T(8,128)(2,1)} %get-tuple-element.85), channel_id=1, source_target_pairs={{0,16},{4,20},{8,24},{12,28},{16,0},{20,4},{24,8},{28,12},{1,17},{... | collective-permute-start | bytes 3145736 | tf_op jit(solution)/shard_map/ppermute | solution.py:24
  204.9 53.4 %collective-permute-start.2 = (bf16[256,2048]{1,0:T(8,128)(2,1)}, bf16[256,2048]{1,0:T(8,128)(2,1)}, u32[]{:S(2)}, u32[]{:S(2)}) collective-permute-start(bf16[256,2048]{1,0:T(8,128)(2,1)} %get-tuple-element.85), channel_id=1, source_target_pairs={{0,24},{4,28},{8,16},{12,20},{16,8},{20,12},{24,0},{28,4},{1,25},{... | collective-permute-start | bytes 3145736 | tf_op jit(solution)/shard_map/ppermute | solution.py:24
  246.3 31.7 %all-to-all-start.1 = ((bf16[8,2,256,256]{3,2,1,0:T(8,128)(2,1)}), bf16[8,2,256,256]{3,2,1,0:T(8,128)(2,1)}, u32[]{:S(2)}, u32[]{:S(2)}) async-start(bf16[8,2,256,256]{3,2,1,0:T(8,128)(2,1)} %get-tuple-element.47), calls=%async_computation.1 | async-start | bytes 4194304 | tf_op jit(solution)/shard_map/all_to_all | solution.py:1622
  250.8 156.2 %all-gather.11.cloned.1.call-start = ((), (), s32[]{:S(2)}) async-start(), calls=%async_computation.11 | async-start | bytes 5242880 | tf_op jit(solution)/shard_map/all_gather | solution.py:1626
  252.0 266.9 %reduce-scatter.4.cloned.1.call-start = ((), (), s32[]{:S(2)}) async-start(), calls=%async_computation.12 | async-start | bytes 5242880 | tf_op jit(solution)/shard_map/reduce_scatter | solution.py:1632
  252.1 13.3 %collective-permute-start.3 = (bf16[256,2048]{1,0:T(8,128)(2,1)}, bf16[256,2048]{1,0:T(8,128)(2,1)S(1)}, u32[]{:S(2)}, u32[]{:S(2)}) collective-permute-start(bf16[256,2048]{1,0:T(8,128)(2,1)} %get-tuple-element.85), channel_id=1, source_target_pairs={{0,4},{4,0},{8,12},{12,8},{16,20},{20,16},{24,28},{28,24},{1,5},{5... | collective-permute-start | bytes 3145736 | tf_op jit(solution)/shard_map/ppermute | solution.py:24
  253.8 46.2 %collective-permute-start.9 = (bf16[256,2048]{1,0:T(8,128)(2,1)S(1)}, bf16[256,2048]{1,0:T(8,128)(2,1)}, u32[]{:S(2)}, u32[]{:S(2)}) collective-permute-start(bf16[256,2048]{1,0:T(8,128)(2,1)S(1)} %slice_add_fusion.1), channel_id=1, source_target_pairs={{0,8},{4,12},{8,0},{12,4},{16,24},{20,28},{24,16},{28,20},{1,9},{5... | collective-permute-start | bytes 3145736 | tf_op jit(solution)/shard_map/ppermute | solution.py:24
  255.5 26.0 %collective-permute-start.4 = (bf16[256,2048]{1,0:T(8,128)(2,1)}, bf16[256,2048]{1,0:T(8,128)(2,1)}, u32[]{:S(2)}, u32[]{:S(2)}) collective-permute-start(bf16[256,2048]{1,0:T(8,128)(2,1)} %collective-permute-done), channel_id=1, source_target_pairs={{0,4},{4,0},{8,12},{12,8},{16,20},{20,16},{24,28},{28,24},{1,5},{5... | collective-permute-start | bytes 3145736 | tf_op jit(solution)/shard_map/ppermute | solution.py:24
  257.8 26.7 %collective-permute-start.5 = (bf16[256,2048]{1,0:T(8,128)(2,1)}, bf16[256,2048]{1,0:T(8,128)(2,1)}, u32[]{:S(2)}, u32[]{:S(2)}) collective-permute-start(bf16[256,2048]{1,0:T(8,128)(2,1)} %collective-permute-done.1), channel_id=1, source_target_pairs={{0,4},{4,0},{8,12},{12,8},{16,20},{20,16},{24,28},{28,24},{1,5},{5... | collective-permute-start | bytes 3145736 | tf_op jit(solution)/shard_map/ppermute | solution.py:24
  258.3 28.6 %collective-permute-start.6 = (bf16[256,2048]{1,0:T(8,128)(2,1)}, bf16[256,2048]{1,0:T(8,128)(2,1)}, u32[]{:S(2)}, u32[]{:S(2)}) collective-permute-start(bf16[256,2048]{1,0:T(8,128)(2,1)} %collective-permute-done.2), channel_id=1, source_target_pairs={{0,4},{4,0},{8,12},{12,8},{16,20},{20,16},{24,28},{28,24},{1,5},{5... | collective-permute-start | bytes 3145736 | tf_op jit(solution)/shard_map/ppermute | solution.py:24
  265.4 34.6 %collective-permute-start.10 = (bf16[256,2048]{1,0:T(8,128)(2,1)}, bf16[256,2048]{1,0:T(8,128)(2,1)}, u32[]{:S(2)}, u32[]{:S(2)}) collective-permute-start(bf16[256,2048]{1,0:T(8,128)(2,1)} %slice_add_fusion), channel_id=1, source_target_pairs={{0,16},{4,20},{8,24},{12,28},{16,0},{20,4},{24,8},{28,12},{1,17},{... | collective-permute-start | bytes 3145736 | tf_op jit(solution)/shard_map/ppermute | solution.py:24
  406.6 382.6 %reduce-scatter.6.cloned.1.call-start = ((), (), s32[]{:S(2)}) async-start(), calls=%async_computation.13 | async-start | bytes 10485760 | tf_op jit(solution)/shard_map/reduce_scatter | solution.py:1632
  630.8 297.5 %reduce-scatter.8.cloned.1.call-start = ((), (), s32[]{:S(2)}) async-start(), calls=%async_computation.14 | async-start | bytes 3276800 | tf_op jit(solution)/shard_map/reduce_scatter | solution.py:1632
  636.8 93.0 %collective-permute-start.11 = (bf16[768,2048]{1,0:T(8,128)(2,1)}, bf16[768,2048]{1,0:T(8,128)(2,1)S(1)}, u32[]{:S(2)}, u32[]{:S(2)}) collective-permute-start(bf16[768,2048]{1,0:T(8,128)(2,1)} %get-tuple-element.65.refs_4_), channel_id=1, source_target_pairs={{0,24},{4,28},{8,16},{12,20},{16,8},{20,12},{24,0},{28,4},{1,25},{... | collective-permute-start | bytes 9437192 | tf_op jit(solution)/shard_map/ppermute | solution.py:24
  638.2 91.5 %collective-permute-start.13 = (bf16[256,2048]{1,0:T(8,128)(2,1)}, bf16[256,2048]{1,0:T(8,128)(2,1)}, u32[]{:S(2)}, u32[]{:S(2)}) collective-permute-start(bf16[256,2048]{1,0:T(8,128)(2,1)} %slice.106), channel_id=1, source_target_pairs={{0,16},{4,20},{8,24},{12,28},{16,0},{20,4},{24,8},{28,12},{1,17},{... | collective-permute-start | bytes 3145736 | tf_op jit(solution)/shard_map/ppermute | solution.py:24
  639.0 90.7 %collective-permute-start.12 = (bf16[256,2048]{1,0:T(8,128)(2,1)}, bf16[256,2048]{1,0:T(8,128)(2,1)}, u32[]{:S(2)}, u32[]{:S(2)}) collective-permute-start(bf16[256,2048]{1,0:T(8,128)(2,1)} %slice.105), channel_id=1, source_target_pairs={{0,8},{4,12},{8,0},{12,4},{16,24},{20,28},{24,16},{28,20},{1,9},{5... | collective-permute-start | bytes 3145736 | tf_op jit(solution)/shard_map/ppermute | solution.py:24
  (29 other events, 438.8 us)
Sparse Core Ops, SparseCore 0:
  23.7 36.4 all-gather.4
  61.8 26.7 all-gather.6
  90.2 149.1 all-gather.8
  252.9 95.1 all-gather.10
  406.7 90.0 reduce-scatter.3
  631.0 158.2 reduce-scatter.5
  794.6 58.4 reduce-scatter.7
